TPU v7x, 32 devices: a whole 2x2x4 slice. The times are simulated.
32 devices in a mesh: dp: 8 (over z, x), mode: 4 (over y, core).
Axes of the slice: x: 2, y: 2, z: 4, core: 2. Of those that a mesh axis runs over, the one named last changes fastest.
Arguments:
- inputs: bfloat16 [512, 96, 512], P(('dp', 'mode')), may hold values from -6 to 6
- observed: int32 [512, 96], P(('dp', 'mode')), may hold values 0 or 1
- out_grad: bfloat16 [512, 96, 512], P(('dp', 'mode')), may hold values from -6 to 6
- mode_index: int32 [48], replicated, may hold values from 1 to 48, as said below
- owner_list: int32 [256], replicated, may hold values from 0 to 255, each once
- dense_master: float32 [5120, 512], P(('dp', 'mode')), may hold values from -0.25 to 0.25
- dense_first: float32 [5120, 512], P(('dp', 'mode')), may hold values from -64 to 64
- dense_second: float32 [5120, 512], P(('dp', 'mode')), may hold values from 638.976 to 2555.904
- mixer_master: float32 [48, 512, 128], P('mode', 'dp'), may hold values from -0.625 to 0.625
- mixer_first: float32 [48, 512, 128], P('mode', 'dp'), may hold values from -20 to 20
- mixer_second: float32 [48, 512, 128], P('mode', 'dp'), may hold values from 51.2 to 204.8
- small_master: float32 [1044], replicated, may hold values from -3 to 3
- small_first: float32 [1044], replicated, may hold values from -64 to 64
- small_second: float32 [1044], replicated, may hold values from 638.976 to 2555.904
Outputs:
- output: bfloat16 [512, 96, 512], P(('dp', 'mode'))
- input_grad: float32 [512, 96, 512], P(('dp', 'mode'))
- dense_first_new: float32 [5120, 512], P(('dp', 'mode'))
- dense_second_new: float32 [5120, 512], P(('dp', 'mode'))
- dense_new: float32 [5120, 512], P(('dp', 'mode'))
- mixer_first_new: float32 [48, 512, 128], P('mode', 'dp')
- mixer_second_new: float32 [48, 512, 128], P('mode', 'dp')
- mixer_new: float32 [48, 512, 128], P('mode', 'dp')
- small_first_new: float32 [1044], replicated
- small_second_new: float32 [1044], replicated
- small_new: float32 [1044], replicated
- bias_out_grad: float32 [512], replicated
Inputs may be any that keep to these rules, and one draw needn't show every extreme that they name: `mode_index`: distinct values. `owner_list`: a permutation of 0 to 255.
All inputs are finite; a program needn't handle non-finite values. No bound on the sum of `observed` on one device may be relied on, other than what follows from the above.
Results may differ from a plain program's by a relative error of at most 0.02.
Values may be sent and summed in bfloat16 or wider, within the bound.
A program may use at most 256 MiB of HBM per device.

v0:
```python
import jax
import jax.numpy as jnp
from jax import lax
from jax.sharding import PartitionSpec as P

HEADS = 8
FF = 2048
MODES = 48
BLOCKS = 256
STEP = 10


HIGH = lax.Precision.HIGHEST
KERNEL_SIZES = (7, 12, 14, 24, 48)
BETA_ONE = 0.9
BETA_TWO = 0.95
ADAM_EPS = 1e-08
DECAY_RATE = 0.1
RATE_DENSE = 0.03
RATE_MIXER = 0.03
RATE_SMALL = 0.5
CONTRACT_ROWS = (((0,), (0,)), ((), ()))
CONTRACT_COLS = (((1,), (1,)), ((), ()))


def average_tables(length):
    positions = jnp.arange(length, dtype=jnp.int32)
    tables = []
    for kernel in KERNEL_SIZES:
        offsets = jnp.arange(kernel, dtype=jnp.int32)
        clipped = jnp.clip(positions[:, None] - (kernel - 1) // 2 + offsets[None, :], 0, length - 1)
        counts = jnp.sum(
            (clipped[:, :, None] == positions[None, None, :]).astype(jnp.float32), axis=1
        )
        tables.append(counts / kernel)
    return jnp.stack(tables)


def fourier_tables(mode_index, length):
    positions = jnp.arange(length, dtype=jnp.int32)
    phases = mode_index[:, None] * positions[None, :] % length
    angles = phases.astype(jnp.float32) * (2.0 * jnp.pi / length)
    forward = jnp.stack([jnp.cos(angles), -jnp.sin(angles)])
    slot_ids = jnp.arange(mode_index.shape[0], dtype=jnp.int32)
    back_phase = slot_ids[:, None] * positions[None, :] % length
    back_angle = back_phase.astype(jnp.float32) * (2.0 * jnp.pi / length)
    coefs = jnp.where(slot_ids == 0, 1.0, 2.0).astype(jnp.float32) / length
    inverse = jnp.stack(
        [jnp.cos(back_angle) * coefs[:, None], -jnp.sin(back_angle) * coefs[:, None]]
    )
    return (forward, jnp.transpose(inverse, (2, 0, 1)))


def decompose(series, params, tables):
    averages = jnp.einsum("ktu,bud->kbtd", tables, series, precision=HIGH)
    logits = params[:5, None, None, None] * series[None] + params[5:, None, None, None]
    shares = jax.nn.softmax(logits, axis=0)
    return series - jnp.sum(shares * averages, axis=0)


def smooth(values):
    return jax.nn.gelu(values, approximate=False)


def adam_update(weight, gradient, moment, second, step_rate):
    moment_new = BETA_ONE * moment + (1.0 - BETA_ONE) * gradient
    second_new = BETA_TWO * second + (1.0 - BETA_TWO) * gradient * gradient
    scaled_m = moment_new / (1.0 - BETA_ONE**STEP)
    scaled_v = second_new / (1.0 - BETA_TWO**STEP)
    weight_new = weight - step_rate * (
        scaled_m / (jnp.sqrt(scaled_v) + ADAM_EPS) + DECAY_RATE * weight
    )
    return (moment_new, second_new, weight_new)


def shards(
    inputs,
    observed,
    out_grad,
    mode_index,
    owner_list,
    dense_master,
    dense_first,
    dense_second,
    mixer_master,
    mixer_first,
    mixer_second,
    small_master,
    small_first,
    small_second,
):
    mode_count = lax.axis_size("mode")
    per_device = MODES // mode_count
    windows_here = inputs.shape[0]
    length = inputs.shape[1]
    model_width = inputs.shape[2]
    head_size = mixer_master.shape[2] // 2
    gathered = lax.all_gather(dense_master.astype(jnp.bfloat16), ("dp", "mode"), axis=0, tiled=True)
    mixer_weights = lax.all_gather(mixer_master.astype(jnp.bfloat16), "dp", axis=1, tiled=True)
    restore = jnp.argsort(owner_list)
    weight_table = gathered.reshape(BLOCKS, -1, model_width)[restore].reshape(-1, model_width)
    w_query = weight_table[:model_width]
    w_out = weight_table[model_width : 2 * model_width]
    w_up = weight_table[2 * model_width : 2 * model_width + FF]
    w_down = weight_table[2 * model_width + FF :]
    forward, inverse = fourier_tables(mode_index, length)
    forward = forward.astype(jnp.bfloat16)
    inverse = inverse.astype(jnp.bfloat16)
    tables = average_tables(length)
    bias_query = small_master[:model_width]
    bias_out = small_master[model_width : 2 * model_width]
    first_mix = small_master[2 * model_width : 2 * model_width + 10]
    second_mix = small_master[2 * model_width + 10 : 2 * model_width + 20]

    def apply_decomp(series, params):
        return decompose(series, params, tables)

    mask_values = observed.astype(jnp.float32)[:, :, None]
    activations = inputs.astype(jnp.float32) * mask_values
    acts_low = activations.astype(jnp.bfloat16).reshape(-1, model_width)
    query_full = jnp.dot(acts_low, w_query, preferred_element_type=jnp.float32) + bias_query
    query_low = query_full.astype(jnp.bfloat16).reshape(windows_here, length, model_width)
    spectra = jnp.einsum(
        "cmt,btd->bcmd", forward, query_low, preferred_element_type=jnp.float32
    ).astype(jnp.bfloat16)
    spectra_all = lax.all_to_all(spectra, "mode", split_axis=2, concat_axis=0, tiled=True)
    group_rows = spectra_all.shape[0]
    split_modes = spectra_all.reshape(group_rows, 2, per_device, HEADS, head_size)
    kernel = mixer_weights.reshape(per_device, HEADS, head_size, 2 * head_size)
    products = jnp.einsum(
        "bcmhi,mhio->bcmho", split_modes, kernel, preferred_element_type=jnp.float32
    )
    real_part = products[:, 0, :, :, :head_size] - products[:, 1, :, :, head_size:]
    imag_part = products[:, 0, :, :, head_size:] + products[:, 1, :, :, :head_size]
    mixed_modes = (
        jnp.stack([real_part, imag_part], axis=1)
        .reshape(group_rows, 2, per_device, model_width)
        .astype(jnp.bfloat16)
    )
    mixed_here = lax.all_to_all(mixed_modes, "mode", split_axis=0, concat_axis=2, tiled=True)
    signal = jnp.einsum("tcm,bcmd->btd", inverse, mixed_here, preferred_element_type=jnp.float32)
    signal_low = signal.astype(jnp.bfloat16).reshape(-1, model_width)
    attended = jnp.dot(signal_low, w_out, preferred_element_type=jnp.float32) + bias_out
    summed = activations + attended.reshape(windows_here, length, model_width)
    first_out, first_back = jax.vjp(apply_decomp, summed, first_mix)
    first_low = first_out.astype(jnp.bfloat16).reshape(-1, model_width)
    hidden = lax.dot_general(first_low, w_up, CONTRACT_COLS, preferred_element_type=jnp.float32)
    active, gelu_back = jax.vjp(smooth, hidden)
    active_low = active.astype(jnp.bfloat16)
    branch = jnp.dot(active_low, w_down, preferred_element_type=jnp.float32)
    result, second_back = jax.vjp(
        apply_decomp, first_out + branch.reshape(windows_here, length, model_width), second_mix
    )
    output = result.astype(jnp.bfloat16)
    grad_second, grad_second_mix = second_back(out_grad.astype(jnp.float32))
    grad_branch = grad_second.astype(jnp.bfloat16).reshape(-1, model_width)
    g_down = lax.dot_general(
        active_low, grad_branch, CONTRACT_ROWS, preferred_element_type=jnp.float32
    )
    grad_active = lax.dot_general(
        grad_branch, w_down, CONTRACT_COLS, preferred_element_type=jnp.float32
    )
    grad_hidden = gelu_back(grad_active)[0].astype(jnp.bfloat16)
    g_up = lax.dot_general(
        grad_hidden, first_low, CONTRACT_ROWS, preferred_element_type=jnp.float32
    )
    grad_first = grad_second + jnp.dot(
        grad_hidden, w_up, preferred_element_type=jnp.float32
    ).reshape(windows_here, length, model_width)
    grad_summed, grad_first_mix = first_back(grad_first)
    grad_flat = grad_summed.reshape(-1, model_width)
    grad_low = grad_flat.astype(jnp.bfloat16)
    g_bias_out = jnp.sum(grad_flat, axis=0)
    g_out = lax.dot_general(signal_low, grad_low, CONTRACT_ROWS, preferred_element_type=jnp.float32)
    grad_signal = (
        lax.dot_general(grad_low, w_out, CONTRACT_COLS, preferred_element_type=jnp.float32)
        .astype(jnp.bfloat16)
        .reshape(windows_here, length, model_width)
    )
    grad_local = jnp.einsum(
        "tcm,btd->bcmd", inverse, grad_signal, preferred_element_type=jnp.float32
    ).astype(jnp.bfloat16)
    grad_mixed = lax.all_to_all(grad_local, "mode", split_axis=2, concat_axis=0, tiled=True)
    grad_split = grad_mixed.reshape(group_rows, 2, per_device, HEADS, head_size)
    real_grad = grad_split[:, 0]
    imag_grad = grad_split[:, 1]
    stacked = jnp.stack(
        [
            jnp.concatenate([real_grad, imag_grad], axis=-1),
            jnp.concatenate([imag_grad, -real_grad], axis=-1),
        ],
        axis=1,
    )
    grad_spectra = (
        jnp.einsum("bcmho,mhio->bcmhi", stacked, kernel, preferred_element_type=jnp.float32)
        .reshape(group_rows, 2, per_device, model_width)
        .astype(jnp.bfloat16)
    )
    g_mixer = jnp.einsum(
        "bcmhi,bcmho->mhio", split_modes, stacked, preferred_element_type=jnp.float32
    ).reshape(per_device, model_width, 2 * head_size)
    mixer_grad = lax.psum_scatter(
        g_mixer.astype(jnp.bfloat16), "dp", scatter_dimension=1, tiled=True
    ).astype(jnp.float32)
    spectra_grad = lax.all_to_all(grad_spectra, "mode", split_axis=0, concat_axis=2, tiled=True)
    grad_query = jnp.einsum(
        "cmt,bcmd->btd", forward, spectra_grad, preferred_element_type=jnp.float32
    ).reshape(-1, model_width)
    g_bias_query = jnp.sum(grad_query, axis=0)
    grad_query_low = grad_query.astype(jnp.bfloat16)
    g_query = lax.dot_general(
        acts_low, grad_query_low, CONTRACT_ROWS, preferred_element_type=jnp.float32
    )
    grad_acts = grad_flat + lax.dot_general(
        grad_query_low, w_query, CONTRACT_COLS, preferred_element_type=jnp.float32
    )
    input_grad = grad_acts.reshape(windows_here, length, model_width) * mask_values
    small_grad = jnp.concatenate([g_bias_query, g_bias_out, grad_first_mix, grad_second_mix])
    small_total = lax.psum(small_grad, ("dp", "mode"))
    dense_grad = (
        jnp.concatenate([g_query, g_out, g_up, g_down], axis=0)
        .reshape(BLOCKS, -1, model_width)[owner_list]
        .reshape(-1, model_width)
    )
    dense_mine = lax.psum_scatter(dense_grad, ("dp", "mode"), scatter_dimension=0, tiled=True)
    dense_first_new, dense_second_new, dense_new = adam_update(
        dense_master, dense_mine, dense_first, dense_second, RATE_DENSE
    )
    mixer_first_new, mixer_second_new, mixer_new = adam_update(
        mixer_master, mixer_grad, mixer_first, mixer_second, RATE_MIXER
    )
    small_first_new, small_second_new, small_new = adam_update(
        small_master, small_total, small_first, small_second, RATE_SMALL
    )
    bias_out_grad = small_total[model_width : 2 * model_width]
    return (
        output,
        input_grad,
        dense_first_new,
        dense_second_new,
        dense_new,
        mixer_first_new,
        mixer_second_new,
        mixer_new,
        small_first_new,
        small_second_new,
        small_new,
        bias_out_grad,
    )


def solution(mesh):
    placed = (
        P(("dp", "mode"), None, None),
        P(("dp", "mode"), None),
        P(("dp", "mode"), None, None),
        P(),
        P(),
        P(("dp", "mode"), None),
        P(("dp", "mode"), None),
        P(("dp", "mode"), None),
        P("mode", "dp", None),
        P("mode", "dp", None),
        P("mode", "dp", None),
        P(),
        P(),
        P(),
    )
    return jax.shard_map(
        shards,
        mesh=mesh,
        in_specs=placed,
        out_specs=(
            P(("dp", "mode"), None, None),
            P(("dp", "mode"), None, None),
            P(("dp", "mode"), None),
            P(("dp", "mode"), None),
            P(("dp", "mode"), None),
            P("mode", "dp", None),
            P("mode", "dp", None),
            P("mode", "dp", None),
            P(),
            P(),
            P(),
            P(),
        ),
        check_vma=False,
    )
```

profile of v0, /device:TPU:0, one launch (start us, length us, event | category | flops | bytes accessed | tf_op | source)
XLA Modules:
  0.0 687.3 jit_solution(14410468609735182902)
XLA Ops:
  12.2 3.8 sort.17
  19.3 60.2 %all-gather.3.cloned.1.call-done = bf16[5120,512]{1,0:T(8,128)(2,1)} async-done(((bf16[160,512]{1,0:T(8,128)(2,1)}), bf16[5120,512]{1,0:T(8,128)(2,1)}) %all-gather.3.cloned.1.call-update) | async-done | bytes 5242896 | tf_op jit(solution)/shard_map/all_gather | solution.py:98
  79.5 8.9 %reshape.507 = bf16[256,20,512]{2,1,0:T(8,128)(2,1)} reshape(bf16[5120,512]{1,0:T(8,128)(2,1)} %all-gather.3.cloned.1.call-done) | data formatting | bytes 10485760 | tf_op jit(solution)/shard_map/reshape | solution.py:101
  88.5 6.5 gather_fusion
  94.9 9.0 %reshape.508 = bf16[5120,512]{1,0:T(8,128)(2,1)} reshape(bf16[256,20,512]{2,1,0:T(8,128)(2,1)} %gather_fusion) | data formatting | bytes 10485760 | tf_op jit(solution)/shard_map/reshape | solution.py:101
  106.5 2.8 copy.96
  109.3 3.8 all-to-all-start
  115.7 17.4 %all-to-all-done = bf16[16,2,48,512]{3,1,0,2:T(2,128)(2,1)S(1)} async-done(((bf16[16,2,48,512]{3,1,0,2:T(2,128)(2,1)}), bf16[16,2,48,512]{3,1,0,2:T(2,128)(2,1)S(1)}, u32[]{:S(2)}, u32[]{:S(2)}) %all-to-all-start) | async-done | bytes 1572896 | tf_op jit(solution)/shard_map/all_to_all | solution.py:126
  134.7 3.9 reshape.510
  138.7 3.1 copy.119
  141.8 3.4 convolution_bitcast_fusion
  153.3 2.8 copy.102
  156.1 3.8 all-to-all-start.1
  160.2 19.8 %all-to-all-done.1 = bf16[64,2,12,512]{3,1,2,0:T(2,128)(2,1)S(1)} async-done(((bf16[64,2,12,512]{3,1,2,0:T(2,128)(2,1)}), bf16[64,2,12,512]{3,1,2,0:T(2,128)(2,1)S(1)}, u32[]{:S(2)}, u32[]{:S(2)}) %all-to-all-start.1) | async-done | bytes 1572896 | tf_op jit(solution)/shard_map/all_to_all | solution.py:140
  186.6 3.3 fusion.19
  193.0 23.8 %fusion.1 = (f32[16,96,512]{2,1,0:T(8,128)}, f32[16,512,5,96]{1,3,2,0:T(8,128)}) fusion(f32[16,96,512]{2,1,0:T(8,128)S(1)} %fusion.19, f32[16,96,512]{2,1,0:T(8,128)S(1)} %fusion.18, f32[5]{0:T(128)S(1)} %get-tuple-element.48, f32[16,96,512]{2,1,0:T(8,128)S(1)} %fusion.45, f32[5]{0:T(128)S(1)} %get-tuple-element.49, ...), kind=kOutput, calls=%fused_computation.8 | convolution fusion | flops 4552654848 | bytes 28495912 | tf_op jit(solution)/shard_map/jvp(ktu,bud->kbtd)/dot_general | solution.py:55
  216.8 2.7 fusion.116
  219.5 31.6 %multiply_convert_fusion = (bf16[1536,2048]{1,0:T(8,128)(2,1)S(1)}, f32[1536,2048]{1,0:T(8,128)}, f32[1536,2048]{1,0:T(8,128)}) fusion(bf16[1536,512]{1,0:T(8,128)(2,1)S(1)} %bitcast.252, bf16[5120,512]{1,0:T(8,128)(2,1)S(1)} %bitcast.231), kind=kOutput, calls=%fused_computation.41 | convolution fusion | flops 3425697792 | bytes 35127296 | tf_op jit(solution)/shard_map/dot_general | solution.py:147
  251.2 3.4 fusion.54
  257.1 3.2 fusion.17
  260.4 4.5 fusion.78
  264.9 30.1 %multiply_reduce_fusion.5 = (f32[16,96,512]{2,1,0:T(8,128)}, f32[16,96,512]{2,1,0:T(8,128)}, f32[16,512,5,96]{1,3,2,0:T(8,128)}) fusion(f32[16,96,512]{2,1,0:T(8,128)} %get-tuple-element.65, f32[16,96,512]{2,1,0:T(8,128)} %get-tuple-element.46, f32[16,96,512]{2,1,0:T(8,128)} %copy-done.10, f32[5]{0:T(128)S(1)} %get-tuple-element.50, ...), kind=kOutput, calls=%fused_computation.30 | convolution fusion | flops 4567597056 | bytes 37933096 | tf_op jit(solution)/shard_map/jvp(ktu,bud->kbtd)/dot_general | solution.py:55
  298.9 17.9 %fusion.109 = (f32[5]{0:T(128)}, f32[5]{0:T(128)}, f32[16,96,512]{2,1,0:T(8,128)S(1)}) fusion(f32[16,96,512]{2,1,0:T(8,128)S(1)} %add.298, f32[5]{0:T(128)S(1)} %get-tuple-element.47, f32[16,96,512]{2,1,0:T(8,128)S(1)} %copy-done.11, f32[5]{0:T(128)S(1)} %get-tuple-element.50, f32[16,96,512]{2,1,0:T(8,128)S(1)} %neg.52, f32[16,96,512]{2,1,0:T(8,128)S(1)} %copy-done.9, ...), kind=kLoop, calls=%fused_computation.210 | loop fusion | flops 46399480 | bytes 34603088 | tf_op jit(solution)/shard_map/transpose(jvp())/reduce_sum | solution.py:56
  316.8 16.1 %fusion.121 = (bf16[16,96,512]{2,1,0:T(8,128)(2,1)S(1)}, f32[16,96,512]{2,1,0:T(8,128)}) fusion(f32[5,96,96]{2,1,0:T(8,128)S(1)} %copy-done.54, f32[16,512,96]{1,2,0:T(8,128)S(1)} %copy-done.22, f32[16,512,96]{1,2,0:T(8,128)S(1)} %bitcast.225, f32[16,512,96]{1,2,0:T(8,128)S(1)} %bitcast.226, f32[5]{0:T(128)S(1)} %get-tuple-element.50, ...), kind=kOutput, calls=%fused_computation.217 | convolution fusion | flops 4552654848 | bytes 22204456 | tf_op jit(solution)/shard_map/transpose(jvp(ktu,bud->kbtd))/dot_general | solution.py:55
  334.2 13.5 %add_convert_fusion = bf16[1536,2048]{1,0:T(8,128)(2,1)} fusion(f32[1536,2048]{1,0:T(8,128)} %get-tuple-element.34, f32[1536,2048]{1,0:T(8,128)} %get-tuple-element.59, bf16[1536,512]{1,0:T(8,128)(2,1)S(1)} %bitcast.254, bf16[5120,512]{1,0:T(8,128)(2,1)S(1)} %bitcast.233), kind=kOutput, calls=%fused_computation.40 | convolution fusion | flops 3265265664 | bytes 35127296 | tf_op jit(solution)/shard_map/dot_general | solution.py:160
  347.7 5.8 fusion.56
  361.0 5.6 multiply_reduce_fusion.3
  369.6 17.3 %fusion.110 = (f32[5]{0:T(128)S(1)}, f32[5]{0:T(128)S(1)}, f32[16,96,512]{2,1,0:T(8,128)}) fusion(f32[16,96,512]{2,1,0:T(8,128)S(1)} %copy-done.1, f32[5]{0:T(128)S(1)} %copy-done.52, f32[16,96,512]{2,1,0:T(8,128)S(1)} %copy-done.5, f32[5]{0:T(128)S(1)} %copy-done.50, f32[16,96,512]{2,1,0:T(8,128)} %neg.55, f32[16,96,512]{2,1,0:T(8,128)S(1)} %copy-done.7, ...), kind=kLoop, calls=%fused_computation.211 | loop fusion | flops 46399480 | bytes 34603088 | tf_op jit(solution)/shard_map/transpose(jvp())/reduce_sum | solution.py:56
  387.0 16.9 %bitcast_add_fusion = f32[16,96,512]{2,1,0:T(8,128)S(1)} fusion(f32[16,96,512]{2,1,0:T(8,128)} %copy-done.17, f32[16,96,512]{2,1,0:T(8,128)} %get-tuple-element.21, f32[16,512,96]{1,2,0:T(8,128)} %get-tuple-element.31, f32[16,512,96]{1,2,0:T(8,128)S(1)} %bitcast.224, f32[16,512,96]{1,2,0:T(8,128)S(1)} %bitcast.223, f32[5]{0:T(128)S(1)} %copy-done.50, ...), kind=kOutput, calls=%fused_computation.79 | convolution fusion | flops 4551081984 | bytes 22204456 | tf_op jit(solution)/shard_map/transpose(jvp(ktu,bud->kbtd))/dot_general | solution.py:55
  407.5 2.8 copy.108
  410.3 3.6 all-to-all-start.2
  413.9 8.7 %fusion.123 = f32[2048,512]{1,0:T(8,128)} fusion(bf16[1536,2048]{1,0:T(8,128)(2,1)} %copy-done.61, bf16[1536,512]{1,0:T(8,128)(2,1)} %bitcast.255), kind=kOutput, calls=%fused_computation.219 | convolution fusion | flops 3221225472 | bytes 12058624 | tf_op jit(solution)/shard_map/dot_general | solution.py:157
  422.6 11.3 %all-to-all-done.2 = bf16[16,2,48,512]{3,1,0,2:T(2,128)(2,1)S(1)} async-done(((bf16[16,2,48,512]{3,1,0,2:T(2,128)(2,1)}), bf16[16,2,48,512]{3,1,0,2:T(2,128)(2,1)S(1)}, u32[]{:S(2)}, u32[]{:S(2)}) %all-to-all-start.2) | async-done | bytes 1572896 | tf_op jit(solution)/shard_map/all_to_all | solution.py:183
  435.5 4.2 reshape.520
  449.7 2.7 reshape.559
  452.4 3.6 all-to-all-start.3
  456.1 4.5 fusion.70
  460.6 8.4 %fusion.122 = f32[2048,512]{1,0:T(8,128)} fusion(bf16[1536,2048]{1,0:T(8,128)(2,1)} %add_convert_fusion, bf16[1536,512]{1,0:T(8,128)(2,1)S(1)} %bitcast.253), kind=kOutput, calls=%fused_computation.218 | convolution fusion | flops 3221225472 | bytes 12058624 | tf_op jit(solution)/shard_map/dot_general | solution.py:164
  469.0 7.0 %all-to-all-done.3 = bf16[64,2,12,512]{3,1,2,0:T(2,128)(2,1)S(1)} async-done(((bf16[64,2,12,512]{3,1,2,0:T(2,128)(2,1)}), bf16[64,2,12,512]{3,1,2,0:T(2,128)(2,1)S(1)}, u32[]{:S(2)}, u32[]{:S(2)}) %all-to-all-start.3) | async-done | bytes 1572896 | tf_op jit(solution)/shard_map/all_to_all | solution.py:205
  476.7 3.0 bitcast_convert_fusion.1
  481.9 8.7 %pad_maximum_fusion = f32[5120,512]{1,0:T(8,128)} fusion(f32[2048,512]{1,0:T(8,128)} %fusion.123, f32[2048,512]{1,0:T(8,128)} %fusion.122, f32[512,512]{1,0:T(8,128)S(1)} %copy-done.33, f32[512,512]{1,0:T(8,128)S(1)} %fusion.75), kind=kLoop, calls=%fused_computation.55 | loop fusion | flops 7864320 | bytes 20971520 | tf_op jit(solution)/shard_map/concatenate | solution.py:221
  490.6 12.5 %reshape.522 = f32[256,20,512]{2,1,0:T(8,128)} reshape(f32[5120,512]{1,0:T(8,128)} %pad_maximum_fusion) | data formatting | bytes 20971520 | tf_op jit(solution)/shard_map/reshape | solution.py:222
  503.1 10.6 %gather_fusion.1 = f32[256,20,512]{2,1,0:T(8,128)} fusion(f32[256,20,512]{2,1,0:T(8,128)} %reshape.522, s32[1024]{0:T(1024)S(1)} %pad_clamp_fusion), kind=kCustom, calls=%fused_computation.1 | custom fusion | bytes 20972544 | tf_op jit(solution)/shard_map/gather | solution.py:221
  513.6 12.7 %reshape.523 = f32[5120,512]{1,0:T(8,128)} reshape(f32[256,20,512]{2,1,0:T(8,128)} %gather_fusion.1) | data formatting | bytes 20971520 | tf_op jit(solution)/shard_map/reshape | solution.py:223
  528.3 3.8 subtract_convert_fusion
  532.4 46.6 %psum.7 = f32[1044]{0:T(1024)S(1)} all-reduce(f32[1044]{0:T(1024)S(1)} %concatenate.17), channel_id=1, replica_groups=mesh['dp'=8,'mode'=4] {'dp','mode'}, use_global_device_ids=true, to_apply=%region_24.25 | all-reduce | flops 1044 | bytes 8352 | tf_op jit(solution)/shard_map/psum | solution.py:219
  580.2 3.1 convolution_add_fusion
  587.5 90.7 %reduce-scatter.3.cloned.1.call-done = f32[160,512]{1,0:T(8,128)} async-done(((f32[5120,512]{1,0:T(8,128)}), f32[160,512]{1,0:T(8,128)}) %reduce-scatter.3.cloned.1.call-update) | async-done | bytes 327696 | tf_op jit(solution)/shard_map/reduce_scatter | solution.py:225
  (235 shorter events, 78.7 us)
Async XLA Ops:
  7.2 72.4 %all-gather.3.cloned.1.call-start = ((), (), s32[]{:S(2)}) async-start(), calls=%async_computation.6 | async-start | bytes 5406720 | tf_op jit(solution)/shard_map/all_gather | solution.py:98
  8.9 132.9 %all-gather.5.cloned.1.call-start = ((), (), s32[]{:S(2)}) async-start(), calls=%async_computation.7 | async-start | bytes 1769472 | tf_op jit(solution)/shard_map/all_gather | solution.py:99
  11.4 173.0 %copy-start.38 = (f32[16,96]{1,0:T(8,128)}, f32[16,96]{1,0:T(8,128)S(1)}, u32[]{:S(2)}) copy-start(f32[16,96]{1,0:T(8,128)S(1)} %convert_element_type.144) | copy-start | bytes 18436
  17.4 88.5 %copy-start.40 = (bf16[1,48,96]{2,1,0:T(8,128)(2,1)}, bf16[1,48,96]{2,1,0:T(8,128)(2,1)S(1)}, u32[]{:S(2)}) copy-start(bf16[1,48,96]{2,1,0:T(8,128)(2,1)S(1)} %get-tuple-element.55) | copy-start | bytes 27652
  17.4 88.5 %copy-start.42 = (bf16[1,48,96]{2,1,0:T(8,128)(2,1)}, bf16[1,48,96]{2,1,0:T(8,128)(2,1)S(1)}, u32[]{:S(2)}) copy-start(bf16[1,48,96]{2,1,0:T(8,128)(2,1)S(1)} %get-tuple-element.56) | copy-start | bytes 27652
  19.3 84.6 %copy-start.20 = (bf16[16,96,512]{2,1,0:T(8,128)(2,1)}, bf16[16,96,512]{2,1,0:T(8,128)(2,1)S(1)}, u32[]{:S(2)}) copy-start(bf16[16,96,512]{2,1,0:T(8,128)(2,1)S(1)} %fusion.46) | copy-start | bytes 4718596
  109.3 23.8 %all-to-all-start = ((bf16[16,2,48,512]{3,1,0,2:T(2,128)(2,1)}), bf16[16,2,48,512]{3,1,0,2:T(2,128)(2,1)S(1)}, u32[]{:S(2)}, u32[]{:S(2)}) async-start(bf16[16,2,48,512]{3,1,0,2:T(2,128)(2,1)} %copy.96), calls=%async_computation | async-start | bytes 3145728 | tf_op jit(solution)/shard_map/all_to_all | solution.py:126
  115.6 76.3 %copy-start.49 = (f32[5]{0:T(128)}, f32[5]{0:T(128)S(1)}, u32[]{:S(2)}) copy-start(f32[5]{0:T(128)S(1)} %get-tuple-element.48) | copy-start | bytes 64
  115.6 76.3 %copy-start.51 = (f32[5]{0:T(128)}, f32[5]{0:T(128)S(1)}, u32[]{:S(2)}) copy-start(f32[5]{0:T(128)S(1)} %get-tuple-element.49) | copy-start | bytes 64
  115.7 64.9 %copy-start.44 = (bf16[1,48,96]{2,1,0:T(8,128)(2,1)}, bf16[1,48,96]{2,1,0:T(8,128)(2,1)S(1)}, u32[]{:S(2)}) copy-start(bf16[1,48,96]{2,1,0:T(8,128)(2,1)S(1)} %get-tuple-element.53) | copy-start | bytes 27652
  115.7 64.9 %copy-start.46 = (bf16[1,48,96]{2,1,0:T(8,128)(2,1)}, bf16[1,48,96]{2,1,0:T(8,128)(2,1)S(1)}, u32[]{:S(2)}) copy-start(bf16[1,48,96]{2,1,0:T(8,128)(2,1)S(1)} %get-tuple-element.54) | copy-start | bytes 27652
  156.1 23.9 %all-to-all-start.1 = ((bf16[64,2,12,512]{3,1,2,0:T(2,128)(2,1)}), bf16[64,2,12,512]{3,1,2,0:T(2,128)(2,1)S(1)}, u32[]{:S(2)}, u32[]{:S(2)}) async-start(bf16[64,2,12,512]{3,1,2,0:T(2,128)(2,1)} %copy.102), calls=%async_computation.1 | async-start | bytes 3145728 | tf_op jit(solution)/shard_map/all_to_all | solution.py:140
  160.1 31.8 %copy-start.53 = (f32[5,96,96]{2,1,0:T(8,128)}, f32[5,96,96]{2,1,0:T(8,128)S(1)}, u32[]{:S(2)}) copy-start(f32[5,96,96]{2,1,0:T(8,128)S(1)} %bitcast_dynamic-update-slice_fusion) | copy-start | bytes 552964
  184.8 32.0 %copy-start = (f32[16,96,512]{2,1,0:T(8,128)}, f32[16,96,512]{2,1,0:T(8,128)S(1)}, u32[]{:S(2)}) copy-start(f32[16,96,512]{2,1,0:T(8,128)S(1)} %fusion.45) | copy-start | bytes 9437188
  186.6 5.4 copy-start.4
  189.8 29.7 %slice-start.4 = ((s8[5242880]{0:T(1024)(128)(4,1)}), s8[4194304]{0:T(1024)(128)(4,1)S(1)}, s32[]{:S(2)}) async-start(s8[5242880]{0:T(1024)(128)(4,1)} %bitcast.230), calls=%async_computation.14 | async-start | bytes 8388608
  193.0 26.5 %slice-start.5 = ((s8[5242880]{0:T(1024)(128)(4,1)}), s8[1048576]{0:T(1024)(128)(4,1)S(1)}, s32[]{:S(2)}) async-start(s8[5242880]{0:T(1024)(128)(4,1)} %bitcast.230), calls=%async_computation.15 | async-start | bytes 2097152
  219.5 31.7 %copy-start.29 = (bf16[16,96,512]{2,1,0:T(8,128)(2,1)}, bf16[16,96,512]{2,1,0:T(8,128)(2,1)S(1)}, u32[]{:S(2)}) copy-start(bf16[16,96,512]{2,1,0:T(8,128)(2,1)S(1)} %get-tuple-element.35) | copy-start | bytes 4718596
  255.4 61.4 %copy-start.2 = (f32[16,96,512]{2,1,0:T(8,128)}, f32[16,96,512]{2,1,0:T(8,128)S(1)}, u32[]{:S(2)}) copy-start(f32[16,96,512]{2,1,0:T(8,128)S(1)} %add.298) | copy-start | bytes 9437188
  260.4 4.5 copy-start.8
  260.4 4.5 copy-start.54
  298.9 17.9 %copy-start.22 = (f32[16,512,96]{1,2,0:T(8,128)S(1)}, f32[16,512,96]{1,2,0:T(8,128)}, u32[]{:S(2)}) copy-start(f32[16,512,96]{1,2,0:T(8,128)} %get-tuple-element.45) | copy-start | bytes 9437188
  298.9 17.9 %copy-start.25 = (bf16[16,96,512]{2,1,0:T(8,128)(2,1)S(1)}, bf16[16,96,512]{2,1,0:T(8,128)(2,1)}, u32[]{:S(2)}) copy-start(bf16[16,96,512]{2,1,0:T(8,128)(2,1)} %param.16) | copy-start | bytes 4718596
  298.9 35.3 %slice-start.6 = ((s8[5242880]{0:T(1024)(128)(4,1)}), s8[4194304]{0:T(1024)(128)(4,1)S(1)}, s32[]{:S(2)}) async-start(s8[5242880]{0:T(1024)(128)(4,1)} %bitcast.232), calls=%async_computation.16 | async-start | bytes 8388608
  316.8 17.4 %slice-start.7 = ((s8[5242880]{0:T(1024)(128)(4,1)}), s8[1048576]{0:T(1024)(128)(4,1)S(1)}, s32[]{:S(2)}) async-start(s8[5242880]{0:T(1024)(128)(4,1)} %bitcast.232), calls=%async_computation.17 | async-start | bytes 2097152
  347.6 5.9 copy-start.23
  347.6 10.1 %slice-start = ((s8[15728640]{0:T(1024)(128)(4,1)}), s8[4194304]{0:T(1024)(128)(4,1)S(1)}, s32[]{:S(2)}) async-start(s8[15728640]{0:T(1024)(128)(4,1)} %bitcast.221), calls=%async_computation.10 | async-start | bytes 8388608
  347.6 10.1 %slice-start.1 = ((s8[15728640]{0:T(1024)(128)(4,1)}), s8[4194304]{0:T(1024)(128)(4,1)S(1)}, s32[]{:S(2)}) async-start(s8[15728640]{0:T(1024)(128)(4,1)} %bitcast.221), calls=%async_computation.11 | async-start | bytes 8388608
  347.6 10.1 %slice-start.2 = ((s8[15728640]{0:T(1024)(128)(4,1)}), s8[4194304]{0:T(1024)(128)(4,1)S(1)}, s32[]{:S(2)}) async-start(s8[15728640]{0:T(1024)(128)(4,1)} %bitcast.221), calls=%async_computation.12 | async-start | bytes 8388608
  353.5 5.8 copy-start.14
  356.1 4.9 copy-start.5
  356.1 4.9 copy-start.50
  356.1 4.9 copy-start.52
  407.5 6.4 copy-start.57
  410.3 23.6 %all-to-all-start.2 = ((bf16[16,2,48,512]{3,1,0,2:T(2,128)(2,1)}), bf16[16,2,48,512]{3,1,0,2:T(2,128)(2,1)S(1)}, u32[]{:S(2)}, u32[]{:S(2)}) async-start(bf16[16,2,48,512]{3,1,0,2:T(2,128)(2,1)} %copy.108), calls=%async_computation.2 | async-start | bytes 3145728 | tf_op jit(solution)/shard_map/all_to_all | solution.py:183
  413.9 171.5 %reduce-scatter.5.cloned.1.call-start = ((), (), s32[]{:S(2)}) async-start(), calls=%async_computation.9 | async-start | bytes 1769472 | tf_op jit(solution)/shard_map/reduce_scatter | solution.py:202
  452.4 23.6 %all-to-all-start.3 = ((bf16[64,2,12,512]{3,1,2,0:T(2,128)(2,1)}), bf16[64,2,12,512]{3,1,2,0:T(2,128)(2,1)S(1)}, u32[]{:S(2)}, u32[]{:S(2)}) async-start(bf16[64,2,12,512]{3,1,2,0:T(2,128)(2,1)} %reshape.559), calls=%async_computation.3 | async-start | bytes 3145728 | tf_op jit(solution)/shard_map/all_to_all | solution.py:205
  456.0 4.6 copy-start.30
  456.0 222.2 %reduce-scatter.3.cloned.1.call-start = ((), (), s32[]{:S(2)}) async-start(), calls=%async_computation.8 | async-start | bytes 10813440 | tf_op jit(solution)/shard_map/reduce_scatter | solution.py:225
  469.0 7.7 %copy-start.41 = (bf16[1,48,96]{2,1,0:T(8,128)(2,1)S(1)}, bf16[1,48,96]{2,1,0:T(8,128)(2,1)}, u32[]{:S(2)}) copy-start(bf16[1,48,96]{2,1,0:T(8,128)(2,1)} %copy-done.40) | copy-start | bytes 27652
  469.0 7.7 %copy-start.43 = (bf16[1,48,96]{2,1,0:T(8,128)(2,1)S(1)}, bf16[1,48,96]{2,1,0:T(8,128)(2,1)}, u32[]{:S(2)}) copy-start(bf16[1,48,96]{2,1,0:T(8,128)(2,1)} %copy-done.42) | copy-start | bytes 27652
  532.1 47.5 %copy-start.48 = (f32[1044]{0:T(1024)S(1)}, f32[1044]{0:T(1024)}, u32[]{:S(2)}) copy-start(f32[1044]{0:T(1024)} %param.25) | copy-start | bytes 12532
  532.1 47.5 %copy-start.55 = (f32[1044]{0:T(1024)S(1)}, f32[1044]{0:T(1024)}, u32[]{:S(2)}) copy-start(f32[1044]{0:T(1024)} %param.27) | copy-start | bytes 12532
  532.1 47.5 %copy-start.56 = (f32[1044]{0:T(1024)S(1)}, f32[1044]{0:T(1024)}, u32[]{:S(2)}) copy-start(f32[1044]{0:T(1024)} %param.26) | copy-start | bytes 12532
  532.1 48.1 %copy-start.13 = (bf16[16,512,96]{1,2,0:T(8,128)(2,1)S(1)}, bf16[16,512,96]{1,2,0:T(8,128)(2,1)}, u32[]{:S(2)}) copy-start(bf16[16,512,96]{1,2,0:T(8,128)(2,1)} %copy-done.12) | copy-start | bytes 4718596
  583.4 94.9 %copy-start.32 = (f32[160,512]{1,0:T(8,128)S(1)}, f32[160,512]{1,0:T(8,128)}, u32[]{:S(2)}) copy-start(f32[160,512]{1,0:T(8,128)} %param.19) | copy-start | bytes 983044
  583.4 94.8 %copy-start.36 = (f32[160,512]{1,0:T(8,128)S(1)}, f32[160,512]{1,0:T(8,128)}, u32[]{:S(2)}) copy-start(f32[160,512]{1,0:T(8,128)} %param.21) | copy-start | bytes 983044
  583.4 94.8 %copy-start.37 = (f32[160,512]{1,0:T(8,128)S(1)}, f32[160,512]{1,0:T(8,128)}, u32[]{:S(2)}) copy-start(f32[160,512]{1,0:T(8,128)} %param.20) | copy-start | bytes 983044
  (30 other events, 77.5 us)
Sparse Core Ops, SparseCore 0:
  11.4 68.0 all-gather.2
  82.3 43.0 all-gather.4
  445.4 64.5 reduce-scatter.4
  526.5 151.6 reduce-scatter.2
where the time goes:
time: 694 us; the launch traced here: 687 us
  waiting for transfers between devices  206 us (30%)
  matrix products  188 us (27%)
  local copies, waits for them, and re-layouts  110 us (16%)
  other arithmetic  107 us (15%)
  blocking collectives  46.6 us (7%)
  between operations  15.4 us (2%)
  starting transfers between devices  14.9 us (2%)
    reduce_scatter x1, waiting for transfers between devices, shards(): lax.psum_scatter(dense_grad, ('dp', 'mode'), scatter_dimension=0, tiled=T...  90.7 us
    dot_general x4, matrix products, decompose(): averages = jnp.einsum('ktu,bud->kbtd', tables, series, precision=HIGH)  87 us
    all_gather x1, waiting for transfers between devices, shards(): lax.all_gather(dense_master.astype(jnp.bfloat16), ('dp', 'mode'), axis=0,...  60.2 us
    psum x1, blocking collectives, shards(): small_total = lax.psum(small_grad, ('dp', 'mode'))  46.6 us
    reduce_sum x2, other arithmetic, decompose(): params[:5, None, None, None] * series[None] + params[5:, None, None, None]  35.2 us
    dot_general x1, matrix products, shards(): lax.dot_general(first_low, w_up, CONTRACT_COLS, preferred_element_type=jn...  31.6 us
    reshape x2, local copies, waits for them, and re-layouts, shards(): dense_grad = jnp.concatenate([g_query, g_out, g_up, g_down], axis=0).resh...  25.2 us
    all_to_all x1, waiting for transfers between devices, shards(): lax.all_to_all(mixed_modes, 'mode', split_axis=0, concat_axis=2, tiled=True)  19.8 us
  transfers between devices with their start and end apart: 8, of which 6 were waited for; matrix products, arithmetic and copies ran while one was open for 21% of the time, Pallas kernels for 0%

commit v1 on v0

v1 whole, which is shorter than its diff:
```python
import functools
import math

import jax
import jax.numpy as jnp
import numpy as np
from jax import lax
from jax.experimental import pallas as pl
from jax.experimental.pallas import tpu as pltpu
from jax.sharding import PartitionSpec as P

STEP = 10
BETA_ONE = 0.9
BETA_TWO = 0.95
ADAM_EPS = 1e-08
DECAY_RATE = 0.1
RATE_DENSE = 0.03
RATE_MIXER = 0.03
RATE_SMALL = 0.5

KERNEL_SIZES = (7, 12, 14, 24, 48)
LOG2E = 1.4426950408889634
BF = jnp.bfloat16
F32 = jnp.float32
NT = (((1,), (1,)), ((), ()))
NN = (((1,), (0,)), ((), ()))
TN = (((0,), (0,)), ((), ()))


def dot(a, b, dims=NN):
    return lax.dot_general(a, b, dims, preferred_element_type=F32)


def average_counts(length):
    tables = []
    t = np.arange(length)
    for size in KERNEL_SIZES:
        u = np.clip(t[:, None] - (size - 1) // 2 + np.arange(size)[None, :], 0, length - 1)
        tables.append((u[:, :, None] == t[None, None, :]).sum(1))
    return np.stack(tables).astype(np.float32)


def gelu_parts(h):
    z = jnp.abs(h)
    e = jnp.exp2(h * h * (-0.5 * LOG2E))
    t = 1.0 / (1.0 + (0.3275911 * math.sqrt(0.5)) * z)
    poly = t * (0.5 * 0.254829592 + t * (-0.5 * 0.284496736 + t * (0.5 * 1.421413741 + t * (-0.5 * 1.453152027 + t * (0.5 * 1.061405429)))))
    tail = poly * e
    big = jnp.where(h < 0, tail, 1.0 - tail)
    return big, e * (1.0 / math.sqrt(2 * math.pi))


def middle_kernel(W, L, D, FF, steps,
                  mix_ref, acts_ref, sig_ref, og_ref, wq_ref, wup_ref, wdn_ref, bias_ref, invt_ref, cnt_ref, cntt_ref,
                  out_ref, gsum_ref, gmix_ref, gw_ref, gup_ref, gdn_ref, small_ref,
                  vs, base, avg1, c1, v1, active, dgelu, first, flow, gb, ghid, glow, avg2, stk, accs, accb):
    step = pl.program_id(0)
    T = W * L
    CH = 16
    CC = 256
    nc = D // CC
    nr = L // CH
    FT = 512

    @pl.when(step == 0)
    def _():
        vs[...] = jnp.zeros_like(vs)
        stk[...] = jnp.zeros_like(stk)
        accs[...] = jnp.zeros_like(accs)
        accb[...] = jnp.zeros_like(accb)
        gw_ref[...] = jnp.zeros_like(gw_ref)
        gup_ref[...] = jnp.zeros_like(gup_ref)
        gdn_ref[...] = jnp.zeros_like(gdn_ref)

    def fold(x):
        y = x[:, 0:128]
        for i in range(1, CC // 128):
            y = y + x[:, i * 128:(i + 1) * 128]
        return y[0:8] + y[8:16]

    def scaled_shares(v, base_at):
        logits = [mix_ref[base_at + k] * LOG2E * v + mix_ref[base_at + 5 + k] * LOG2E for k in range(5)]
        top = functools.reduce(jnp.maximum, logits)
        es = [jnp.exp2(l - top) for l in logits]
        r = 1.0 / functools.reduce(lambda a, b: a + b, es)
        return [e * (r * (1.0 / s)) for e, s in zip(es, KERNEL_SIZES)]

    def backward(v, g, cs, avs, mean, base_at):
        gv = g * v
        total = None
        for k in range(5):
            t = cs[k] * (KERNEL_SIZES[k] * mean - avs[k])
            total = mix_ref[base_at + k] * t if total is None else total + mix_ref[base_at + k] * t
            accs[base_at + k] += fold(gv * t)
            accs[base_at + 5 + k] += fold(g * t)
        return g, g * total

    def split(v, w, rows, cols):
        hi = v.astype(BF)
        vs[w, rows, cols] = hi
        return hi

    sig = sig_ref[...].reshape(T, D)
    base[...] = dot(sig, wq_ref[D:2 * D, :])

    def window_one(w, _):
        def rows_a(i, _):
            for c in range(nc):
                cols = slice(c * CC, (c + 1) * CC)
                rows = pl.ds(pl.multiple_of(w * L + i * CH, CH), CH)
                here = pl.ds(pl.multiple_of(i * CH, CH), CH)
                low_rows = pl.ds(pl.multiple_of(L + i * CH, CH), CH)
                v = base[rows, cols] + acts_ref[w, here, cols].astype(F32) + bias_ref[:, cols]
                v1[rows, cols] = v
                hi = v.astype(BF)
                vs[here, cols] = hi
                vs[low_rows, cols] = (v - hi.astype(F32)).astype(BF)
            return 0
        lax.fori_loop(0, nr, rows_a, 0)
        avg1[pl.ds(pl.multiple_of(w * 5 * L, 32), 5 * L), :] = dot(cnt_ref[...], vs[...])

        def rows_b(i, _):
            for c in range(nc):
                cols = slice(c * CC, (c + 1) * CC)
                rows = pl.ds(pl.multiple_of(w * L + i * CH, CH), CH)
                v = v1[rows, cols]
                cs = scaled_shares(v, 0)
                mean = None
                for k in range(5):
                    at = pl.ds(pl.multiple_of((w * 5 + k) * L + i * CH, CH), CH)
                    u = cs[k] * avg1[at, cols]
                    c1[at, cols] = cs[k]
                    mean = u if mean is None else mean + u
                f = v - mean
                first[rows, cols] = f
                flow[pl.ds(pl.multiple_of(step * T + w * L + i * CH, CH), CH), cols] = f.astype(BF)
            return 0
        lax.fori_loop(0, nr, rows_b, 0)
        return 0
    lax.fori_loop(0, W, window_one, 0)

    here_t = pl.ds(pl.multiple_of(step * T, CH), T)
    base[...] = first[...]

    def ffn(n, _):
        cols = pl.ds(pl.multiple_of(n * FT, FT), FT)
        h = dot(flow[here_t, :], wup_ref[cols, :], NT)
        big, small = gelu_parts(h)
        a = (h * big).astype(BF)
        active[here_t, cols] = a
        dgelu[:, cols] = (big + h * small).astype(BF)
        base[...] += dot(a, wdn_ref[cols, :])
        return 0
    lax.fori_loop(0, FF // FT, ffn, 0)

    def window_two(w, _):
        def rows_a(i, _):
            for c in range(nc):
                cols = slice(c * CC, (c + 1) * CC)
                rows = pl.ds(pl.multiple_of(w * L + i * CH, CH), CH)
                here = pl.ds(pl.multiple_of(i * CH, CH), CH)
                low_rows = pl.ds(pl.multiple_of(L + i * CH, CH), CH)
                v = base[rows, cols]
                hi = v.astype(BF)
                vs[here, cols] = hi
                vs[low_rows, cols] = (v - hi.astype(F32)).astype(BF)
            return 0
        lax.fori_loop(0, nr, rows_a, 0)
        avg2[...] = dot(cnt_ref[...], vs[...])

        def rows_b(i, _):
            for c in range(nc):
                cols = slice(c * CC, (c + 1) * CC)
                rows = pl.ds(pl.multiple_of(w * L + i * CH, CH), CH)
                here = pl.ds(pl.multiple_of(i * CH, CH), CH)
                v = base[rows, cols]
                cs = scaled_shares(v, 10)
                avs = [avg2[pl.ds(pl.multiple_of(k * L + i * CH, CH), CH), cols] for k in range(5)]
                mean = functools.reduce(lambda a, b: a + b, [c_ * a_ for c_, a_ in zip(cs, avs)])
                out_ref[w, here, cols] = (v - mean).astype(BF)
                g = og_ref[w, here, cols].astype(F32)
                for k in range(5):
                    stk[pl.ds(pl.multiple_of(k * L + i * CH, CH), CH), cols] = (cs[k] * g).astype(BF)
                g, extra = backward(v, g, cs, avs, mean, 10)
                base[rows, cols] = g + extra
            return 0
        lax.fori_loop(0, nr, rows_b, 0)
        rows = pl.ds(pl.multiple_of(w * L, L), L)
        gs = base[rows, :] - dot(cntt_ref[...], stk[...])
        base[rows, :] = gs
        gb[pl.ds(pl.multiple_of(step * T + w * L, 32), L), :] = gs.astype(BF)
        return 0
    lax.fori_loop(0, W, window_two, 0)

    def ffn_back(n, _):
        cols = pl.ds(pl.multiple_of(n * FT, FT), FT)
        ga = dot(gb[here_t, :], wdn_ref[cols, :], NT)
        gh = (ga * dgelu[:, cols].astype(F32)).astype(BF)
        ghid[here_t, cols] = gh
        base[...] += dot(gh, wup_ref[cols, :])
        return 0
    lax.fori_loop(0, FF // FT, ffn_back, 0)

    def window_three(w, _):
        def rows_b(i, _):
            for c in range(nc):
                cols = slice(c * CC, (c + 1) * CC)
                rows = pl.ds(pl.multiple_of(w * L + i * CH, CH), CH)
                v = v1[rows, cols]
                g = base[rows, cols]
                ats = [pl.ds(pl.multiple_of((w * 5 + k) * L + i * CH, CH), CH) for k in range(5)]
                cs = [c1[at, cols] for at in ats]
                avs = [avg1[at, cols] for at in ats]
                mean = v - first[rows, cols]
                for k in range(5):
                    stk[pl.ds(pl.multiple_of(k * L + i * CH, CH), CH), cols] = (cs[k] * g).astype(BF)
                g, extra = backward(v, g, cs, avs, mean, 0)
                base[rows, cols] = g + extra
                accb[:, cols] += extra[0:8] + extra[8:16]
            return 0
        lax.fori_loop(0, nr, rows_b, 0)
        rows = pl.ds(pl.multiple_of(w * L, L), L)
        gs = base[rows, :] - dot(cntt_ref[...], stk[...])
        gsum_ref[w] = gs
        glow[rows, :] = gs.astype(BF)
        return 0
    lax.fori_loop(0, W, window_three, 0)

    back = dot(glow[...], wq_ref[D:2 * D, :], NT).astype(BF)
    for w in range(W):
        gmix_ref[w] = dot(invt_ref[...], back[w * L:(w + 1) * L, :]).astype(BF)
    gw_ref[...] += dot(sig, glow[...], TN)

    @pl.when(step == steps - 1)
    def _():
        small_ref[0:8, :] = accb[...]
        for k in range(20):
            small_ref[8 + 8 * k:16 + 8 * k, 0:128] = accs[k]
            small_ref[8 + 8 * k:16 + 8 * k, 128:512] = jnp.zeros((8, 384), F32)

        def wgrad(n, _):
            cols = pl.ds(pl.multiple_of(n * FT, FT), FT)
            gup_ref[cols, :] = dot(ghid[:, cols], flow[...], TN)
            gdn_ref[cols, :] = dot(active[:, cols], gb[...], TN)
            return 0
        lax.fori_loop(0, FF // FT, wgrad, 0)


def middle(mix, acts, sig, og, wqo, wup, wdn, bias, inv, W=4):
    n, L, D = acts.shape
    FF = wup.shape[0]
    steps = n // W
    T = W * L
    A = average_counts(L)
    cnt = np.zeros((5 * L, 256), np.float32)
    cnt[:, :L] = A.reshape(5 * L, L)
    cnt[:, L:2 * L] = A.reshape(5 * L, L)
    cntt = np.zeros((L, 512), np.float32)
    cntt[:, :5 * L] = A.transpose(2, 0, 1).reshape(L, 5 * L)
    cnt = jnp.asarray(cnt, BF)
    cntt = jnp.asarray(cntt, BF)
    whole = lambda *s: pl.BlockSpec(s, lambda i: (0,) * len(s), pipeline_mode=pl.Buffered(1))
    piece = lambda *s: pl.BlockSpec(s, lambda i: (i,) + (0,) * (len(s) - 1))
    return pl.pallas_call(
        functools.partial(middle_kernel, W, L, D, FF, steps),
        grid=(steps,),
        out_shape=(
            jax.ShapeDtypeStruct((n, L, D), BF),
            jax.ShapeDtypeStruct((n, L, D), F32),
            jax.ShapeDtypeStruct((n, L, D), BF),
            jax.ShapeDtypeStruct((D, D), F32),
            jax.ShapeDtypeStruct((FF, D), F32),
            jax.ShapeDtypeStruct((FF, D), F32),
            jax.ShapeDtypeStruct((168, D), F32),
        ),
        in_specs=[
            pl.BlockSpec(memory_space=pltpu.SMEM),
            piece(W, L, D), piece(W, L, D), piece(W, L, D),
            whole(2 * D, D), whole(FF, D), whole(FF, D), whole(1, D), whole(L, L), whole(5 * L, 256), whole(L, 512),
        ],
        out_specs=(
            piece(W, L, D), piece(W, L, D), piece(W, L, D), whole(D, D), whole(FF, D), whole(FF, D), whole(168, D),
        ),
        scratch_shapes=[
            pltpu.VMEM((256, D), BF),
            pltpu.VMEM((T, D), F32),
            pltpu.VMEM((W * 5 * L, D), F32),
            pltpu.VMEM((W * 5 * L, D), F32),
            pltpu.VMEM((T, D), F32),
            pltpu.VMEM((n * L, FF), BF),
            pltpu.VMEM((T, FF), BF),
            pltpu.VMEM((T, D), F32),
            pltpu.VMEM((n * L, D), BF),
            pltpu.VMEM((n * L, D), BF),
            pltpu.VMEM((n * L, FF), BF),
            pltpu.VMEM((T, D), BF),
            pltpu.VMEM((5 * L, D), F32),
            pltpu.VMEM((512, D), BF),
            pltpu.VMEM((20, 8, 128), F32),
            pltpu.VMEM((8, D), F32),
        ],
        compiler_params=pltpu.CompilerParams(vmem_limit_bytes=60 * 1024 * 1024),
        name="middle",
    )(mix, acts, sig, og, wqo, wup, wdn, bias, inv.T, cnt, cntt)


def sign_lanes(rows, left, right):
    lane = lax.broadcasted_iota(jnp.int32, (rows, 128), 1)
    return jnp.where(lane < 64, left, right).astype(F32)


def interleave(real, imag, v):
    re, im = real[:, v * 128:(v + 1) * 128], imag[:, v * 128:(v + 1) * 128]
    low = lax.broadcasted_iota(jnp.int32, re.shape, 1) < 64
    return jnp.where(low, re, pltpu.roll(im, 64, 1)), jnp.where(low, pltpu.roll(re, 64, 1), im)


def gather_rows(tiles, w, slots, n):
    reals, imags = [], []
    for v in range(4):
        first = tiles[2 * v, pl.ds(w, slots, stride=n), :]
        second = tiles[2 * v + 1, pl.ds(w, slots, stride=n), :]
        low = lax.broadcasted_iota(jnp.int32, first.shape, 1) < 64
        reals.append(jnp.where(low, first, pltpu.roll(second, 64, 1)).astype(BF))
        imags.append(jnp.where(low, pltpu.roll(first, 64, 1), second).astype(BF))
    return jnp.concatenate([jnp.concatenate(reals, 1), jnp.concatenate(imags, 1)], 0)


def spread_rows(tiles, w, slots, n, spectrum):
    for v in range(4):
        one, two = interleave(spectrum[:slots], spectrum[slots:], v)
        tiles[2 * v, pl.ds(w, slots, stride=n), :] = one
        tiles[2 * v + 1, pl.ds(w, slots, stride=n), :] = two


def head_matrix(weights, h, pieces, mode, rows):
    top = jnp.concatenate([weights[h * pieces + q, mode, rows, :] for q in range(pieces)], 0)
    wide = top.astype(F32)
    low = pltpu.roll(wide, 64, 1) * sign_lanes(wide.shape[0], -1.0, 1.0)
    return jnp.concatenate([top, low.astype(BF)], 0)


def front_kernel(n, L, D, slots, in_ref, obs_ref, wq_ref, bias_ref, basis_ref, inv_ref, eye_ref, weights,
                 acts_ref, z_ref, sig_ref, query, tiles, outs):
    ndp, nmode = weights.shape[:2]
    per = slots // nmode
    heads = 8
    pieces = ndp // heads
    depth = 64 // pieces

    def mask(w, _):
        row = obs_ref[pl.ds(w, 1), :].astype(F32)
        rows = pl.ds(pl.multiple_of(w * L, 32), L)
        acts_ref[rows, :] = dot((eye_ref[...] * row).astype(BF), in_ref[rows, :]).astype(BF)
        return 0
    lax.fori_loop(0, n, mask, 0)
    T = 384

    def project(i, _):
        rows = pl.ds(pl.multiple_of(i * T, T), T)
        query[rows, :] = (dot(acts_ref[rows, :], wq_ref[...]) + bias_ref[...]).astype(BF)
        return 0
    lax.fori_loop(0, n * L // T, project, 0)

    def spectra(w, _):
        rows = pl.ds(pl.multiple_of(w * L, 32), L)
        spread_rows(tiles, w, slots, n, dot(basis_ref[...], query[rows, :]))
        return 0
    lax.fori_loop(0, n, spectra, 0)

    for mode in range(nmode):
        def slot(jl, _):
            at = pl.ds(pl.multiple_of((mode * per + jl) * n, n), n)
            rows = pl.ds(pl.multiple_of(jl * depth, depth), depth)
            for h in range(heads):
                x = tiles[h, at, :].astype(BF)
                z_ref[h, at, :] = x
                outs[h, at, :] = dot(x, head_matrix(weights, h, pieces, mode, rows))
            return 0
        lax.fori_loop(0, per, slot, 0)

    def signal(w, _):
        rows = pl.ds(pl.multiple_of(w * L, 32), L)
        sig_ref[rows, :] = dot(inv_ref[...], gather_rows(outs, w, slots, n)).astype(BF)
        return 0
    lax.fori_loop(0, n, signal, 0)


def front(inputs, observed, wqo, bias, basis, inv, weights):
    n, L, D = inputs.shape
    slots = basis.shape[0] // 2
    vm = pl.BlockSpec(memory_space=pltpu.VMEM)
    whole = lambda *s: pl.BlockSpec(s, lambda i: (0,) * len(s), pipeline_mode=pl.Buffered(1))
    return pl.pallas_call(
        functools.partial(front_kernel, n, L, D, slots),
        grid=(1,),
        out_shape=(
            jax.ShapeDtypeStruct((n * L, D), BF),
            jax.ShapeDtypeStruct((8, slots * n, 128), BF),
            jax.ShapeDtypeStruct((n * L, D), BF),
        ),
        in_specs=[whole(n * L, D), whole(n, L), whole(D, D), whole(1, D), whole(2 * slots, L), whole(L, 2 * slots), whole(L, L),
                  whole(*weights.shape)],
        out_specs=(whole(n * L, D), whole(8, slots * n, 128), whole(n * L, D)),
        scratch_shapes=[
            pltpu.VMEM((n * L, D), BF),
            pltpu.VMEM((8, slots * n, 128), F32),
            pltpu.VMEM((8, slots * n, 128), F32),
        ],
        compiler_params=pltpu.CompilerParams(vmem_limit_bytes=60 * 1024 * 1024),
        name="front",
    )(inputs.reshape(n * L, D), observed, wqo, bias, basis, inv, jnp.eye(L, dtype=F32), weights)


def back_kernel(n, L, D, slots, gmix_ref, z_ref, acts_ref, gsum_ref, obs_ref, wq_ref, basist_ref, eye_ref, weights,
                gin_ref, gq_ref, gbias_ref, gmixer_ref, tiles, outs, glow):
    ndp, nmode = weights.shape[:2]
    per = slots // nmode
    heads = 8
    pieces = ndp // heads
    depth = 64 // pieces

    def spectra(w, _):
        rows = pl.ds(pl.multiple_of(w * L, 32), L)
        spread_rows(tiles, w, slots, n, gmix_ref[rows, :].astype(F32))
        return 0
    lax.fori_loop(0, n, spectra, 0)

    for mode in range(nmode):
        def slot(jl, _):
            at = pl.ds(pl.multiple_of((mode * per + jl) * n, n), n)
            rows = pl.ds(pl.multiple_of(jl * depth, depth), depth)
            for h in range(heads):
                y = tiles[h, at, :].astype(BF)
                outs[h, at, :] = dot(y, head_matrix(weights, h, pieces, mode, rows), NT)
                g = dot(z_ref[h, at, :], y, TN)
                g = (g[:64] + pltpu.roll(g[64:], 64, 1) * sign_lanes(64, 1.0, -1.0)).astype(BF)
                for q in range(pieces):
                    gmixer_ref[h * pieces + q, mode, rows, :] = g[q * depth:(q + 1) * depth]
            return 0
        lax.fori_loop(0, per, slot, 0)
    gbias_ref[...] = jnp.zeros_like(gbias_ref)

    def query(w, _):
        rows = pl.ds(pl.multiple_of(w * L, 32), L)
        g = dot(basist_ref[...], gather_rows(outs, w, slots, n))
        glow[rows, :] = g.astype(BF)
        gbias_ref[...] += functools.reduce(lambda a, b: a + b, [g[i * 8:(i + 1) * 8] for i in range(L // 8)])
        return 0
    lax.fori_loop(0, n, query, 0)
    gq_ref[...] = dot(acts_ref[...], glow[...], TN)

    def input_grad(w, _):
        rows = pl.ds(pl.multiple_of(w * L, 32), L)
        row = obs_ref[pl.ds(w, 1), :].astype(F32)
        mask = dot((eye_ref[...] * row).astype(BF), jnp.ones((L, 128), BF))
        g = gsum_ref[rows, :] + dot(glow[rows, :], wq_ref[...], NT)
        for c in range(D // 128):
            gin_ref[rows, c * 128:(c + 1) * 128] = g[:, c * 128:(c + 1) * 128] * mask
        return 0
    lax.fori_loop(0, n, input_grad, 0)


def back(gmix, z, acts, gsum, observed, wqo, basist, weights):
    n, L = observed.shape
    D = acts.shape[1]
    slots = basist.shape[1] // 2
    whole = lambda *s: pl.BlockSpec(s, lambda i: (0,) * len(s), pipeline_mode=pl.Buffered(1))
    return pl.pallas_call(
        functools.partial(back_kernel, n, L, D, slots),
        grid=(1,),
        out_shape=(
            jax.ShapeDtypeStruct((n * L, D), F32),
            jax.ShapeDtypeStruct((D, D), F32),
            jax.ShapeDtypeStruct((8, D), F32),
            jax.ShapeDtypeStruct(weights.shape, BF),
        ),
        in_specs=[whole(n * L, D), whole(8, slots * n, 128), whole(n * L, D), whole(n * L, D), whole(n, L), whole(D, D),
                  whole(L, 2 * slots), whole(L, L), whole(*weights.shape)],
        out_specs=(whole(n * L, D), whole(D, D), whole(8, D), whole(*weights.shape)),
        scratch_shapes=[
            pltpu.VMEM((8, slots * n, 128), F32),
            pltpu.VMEM((8, slots * n, 128), F32),
            pltpu.VMEM((n * L, D), BF),
        ],
        compiler_params=pltpu.CompilerParams(vmem_limit_bytes=60 * 1024 * 1024),
        name="back",
    )(gmix, z, acts, gsum, observed, wqo, basist, jnp.eye(L, dtype=F32), weights)


def table_kernel(blocks, owner, in_ref, wqo_ref, wup_ref, wdn_ref, src, dst):
    rows = in_ref.shape[0]
    size = rows // blocks
    step = 256

    def widen(i, _):
        at = pl.ds(pl.multiple_of(i * step, step), step)
        src[at, :] = in_ref[at, :].astype(F32)
        return 0
    lax.fori_loop(0, rows // step, widen, 0)

    def move(j, _):
        dst[pl.ds(owner[j] * size, size), :] = src[pl.ds(j * size, size), :]
        return 0
    lax.fori_loop(0, blocks, move, 0, unroll=4)
    start = 0
    for ref in (wqo_ref, wup_ref, wdn_ref):
        def narrow(i, _):
            to = pl.ds(pl.multiple_of(i * step, step), step)
            at = pl.ds(pl.multiple_of(start + i * step, step), step)
            ref[to, :] = dst[at, :].astype(BF)
            return 0
        lax.fori_loop(0, ref.shape[0] // step, narrow, 0)
        start += ref.shape[0]


def to_table(gathered, owner_list, ff):
    rows, D = gathered.shape
    blocks = owner_list.shape[0]
    cols = lambda r: pl.BlockSpec((r, 128), lambda i, o: (0, i))
    return pl.pallas_call(
        functools.partial(table_kernel, blocks),
        grid_spec=pltpu.PrefetchScalarGridSpec(
            num_scalar_prefetch=1,
            grid=(D // 128,),
            in_specs=[cols(rows)],
            out_specs=(cols(2 * D), cols(ff), cols(ff)),
            scratch_shapes=[pltpu.VMEM((rows + 8, 128), F32), pltpu.VMEM((rows + 8, 128), F32)],
        ),
        out_shape=(
            jax.ShapeDtypeStruct((2 * D, D), BF),
            jax.ShapeDtypeStruct((ff, D), BF),
            jax.ShapeDtypeStruct((ff, D), BF),
        ),
        compiler_params=pltpu.CompilerParams(vmem_limit_bytes=40 * 1024 * 1024),
        name="to_table",
    )(owner_list, gathered)


def owners_kernel(blocks, owner, *refs):
    parts, out_ref, src, dst = refs[:4], refs[4], refs[5], refs[6]
    rows = out_ref.shape[0]
    size = rows // blocks
    step = 256
    start = 0
    for ref in parts:
        def take(i, _):
            to = pl.ds(pl.multiple_of(start + i * step, step), step)
            at = pl.ds(pl.multiple_of(i * step, step), step)
            src[to, :] = ref[at, :]
            return 0
        lax.fori_loop(0, ref.shape[0] // step, take, 0)
        start += ref.shape[0]

    def move(j, _):
        dst[pl.ds(j * size, size), :] = src[pl.ds(owner[j] * size, size), :]
        return 0
    lax.fori_loop(0, blocks, move, 0, unroll=4)

    def narrow(i, _):
        at = pl.ds(pl.multiple_of(i * step, step), step)
        out_ref[at, :] = dst[at, :].astype(BF)
        return 0
    lax.fori_loop(0, rows // step, narrow, 0)


def to_owners(parts, owner_list):
    D = parts[0].shape[1]
    rows = sum(p.shape[0] for p in parts)
    blocks = owner_list.shape[0]
    cols = lambda r: pl.BlockSpec((r, 128), lambda i, o: (0, i))
    return pl.pallas_call(
        functools.partial(owners_kernel, blocks),
        grid_spec=pltpu.PrefetchScalarGridSpec(
            num_scalar_prefetch=1,
            grid=(D // 128,),
            in_specs=[cols(p.shape[0]) for p in parts],
            out_specs=cols(rows),
            scratch_shapes=[pltpu.VMEM((rows + 8, 128), F32), pltpu.VMEM((rows + 8, 128), F32)],
        ),
        out_shape=jax.ShapeDtypeStruct((rows, D), BF),
        compiler_params=pltpu.CompilerParams(vmem_limit_bytes=40 * 1024 * 1024),
        name="to_owners",
    )(owner_list, *parts)


MESH = pl.DeviceIdType.MESH


def places():
    ndp, nmode = lax.axis_size("dp"), lax.axis_size("mode")
    sizes = {"a": ndp // 2, "b": 2, "y": nmode // 2, "c": 2}
    dp, mode = lax.axis_index("dp"), lax.axis_index("mode")
    here = {"a": dp // 2, "b": lax.rem(dp, 2), "y": mode // 2, "c": lax.rem(mode, 2)}
    return sizes, here


def number(sizes, at):
    return ((at["a"] * sizes["b"] + at["b"]) * sizes["y"] + at["y"]) * 2 + at["c"]


def device(sizes, at):
    return {"dp": at["a"] * sizes["b"] + at["b"], "mode": at["y"] * 2 + at["c"]}


def move(sizes, at, axis, d):
    return {**at, axis: lax.rem(at[axis] + d, sizes[axis])}


def greet():
    ndp, nmode = lax.axis_size("dp"), lax.axis_size("mode")
    dp, mode = lax.axis_index("dp"), lax.axis_index("mode")
    barrier = pltpu.get_barrier_semaphore()
    for d in range(1, nmode):
        pl.semaphore_signal(barrier, 1, device_id={"dp": dp, "mode": lax.rem(mode + d, nmode)}, device_id_type=MESH)
    for d in range(1, ndp):
        pl.semaphore_signal(barrier, 1, device_id={"dp": lax.rem(dp + d, ndp), "mode": mode}, device_id_type=MESH)
    pl.semaphore_wait(barrier, ndp + nmode - 2)


def staggered(count, *stages):
    k = len(stages)
    if count < k:
        for stage in stages:
            for t in range(count):
                stage(t)
        return
    for t in range(k - 1):
        for s in range(t + 1):
            stages[s](t - s)

    def body(t, _):
        for s in range(k):
            stages[s](t - s)
        return 0
    lax.fori_loop(k - 1, count, body, 0)
    for t in range(count, count + k - 1):
        for s in range(t - count + 1, k):
            stages[s](t - s)


def gather_kernel(*refs):
    kinds = 2
    ins, outs = refs[:kinds], refs[kinds:2 * kinds]
    recv, send, local = refs[2 * kinds:]
    sizes, here = places()
    greet()

    def copy(kind, at, to, stage, own=False):
        n = number(sizes, at)
        return pltpu.make_async_remote_copy(
            src_ref=ins[kind] if own else outs[kind].at[n], dst_ref=outs[kind].at[n],
            send_sem=send.at[kind, stage], recv_sem=recv.at[kind, n],
            device_id=device(sizes, to), device_id_type=MESH)

    def arrived(kind, at):
        copy(kind, at, here, 0).wait_recv()

    def drain(kind, stage, count):
        ref = outs[kind].at[pl.ds(0, count)]
        pltpu.make_async_copy(ref, ref, send.at[kind, stage]).wait()

    mine = [pltpu.make_async_copy(ins[k], outs[k].at[number(sizes, here)], local.at[k]) for k in range(kinds)]
    for c in mine:
        c.start()

    def run(u, v):
        na, nu, nv = sizes["a"], sizes[u], sizes[v]

        def onward(kind, at, axes, own=False):
            for axis, stage in axes:
                for d in range(1, sizes[axis]):
                    copy(kind, at, move(sizes, here, axis, d), stage, own).start()

        for kind in range(kinds):
            onward(kind, here, (("a", 0), (u, 1), (v, 2), ("c", 3)), True)

        def line(t):
            at = move(sizes, here, "a", t + 1)
            for kind in range(kinds):
                arrived(kind, at)
                onward(kind, at, ((u, 1), (v, 2), ("c", 3)))

        def second(t):
            for d in range(1, nu):
                at = move(sizes, move(sizes, here, "a", t), u, d)
                for kind in range(kinds):
                    arrived(kind, at)
                    onward(kind, at, ((v, 2), ("c", 3)))

        def third(t):
            for e in range(nu):
                for d in range(1, nv):
                    at = move(sizes, move(sizes, move(sizes, here, "a", t), u, e), v, d)
                    for kind in range(kinds):
                        arrived(kind, at)
                        onward(kind, at, (("c", 3),))

        second(0)
        staggered(na - 1, line, lambda t: second(t + 1), third)
        third(na - 1)
        for kind in range(kinds):
            drain(kind, 0, na - 1)
            drain(kind, 1, na * (nu - 1))
            drain(kind, 2, na * nu * (nv - 1))

    pl.when(here["c"] == 0)(lambda: run("b", "y"))
    pl.when(here["c"] == 1)(lambda: run("y", "b"))
    group = sizes["a"] * sizes["b"] * sizes["y"]
    other = move(sizes, here, "c", 1)

    def partner(i, _):
        for kind in range(kinds):
            copy(kind, {"a": i // (sizes["b"] * sizes["y"]), "b": lax.rem(i // sizes["y"], sizes["b"]),
                        "y": lax.rem(i, sizes["y"]), "c": other["c"]}, here, 0).wait_recv()
        return 0
    lax.fori_loop(0, group, partner, 0)
    for kind in range(kinds):
        drain(kind, 3, group)
    for c in mine:
        c.wait()


def gather(dense, mixer):
    nd = lax.axis_size("dp") * lax.axis_size("mode")
    anywhere = pl.BlockSpec(memory_space=pl.ANY)
    return pl.pallas_call(
        gather_kernel,
        out_shape=tuple(jax.ShapeDtypeStruct((nd,) + x.shape, x.dtype) for x in (dense, mixer)),
        in_specs=[anywhere] * 2,
        out_specs=(anywhere,) * 2,
        scratch_shapes=[pltpu.SemaphoreType.DMA((2, nd)), pltpu.SemaphoreType.DMA((2, 4)), pltpu.SemaphoreType.DMA((2,))],
        compiler_params=pltpu.CompilerParams(collective_id=0, has_side_effects=True),
        name="gather",
    )(dense, mixer)


def reduce_kernel(*refs):
    kinds = 2
    ins, small_in = refs[:2], refs[2]
    outs, small_out = refs[3:5], refs[5]
    acc, from_c, from_v, from_u, from_a = (refs[6 + 2 * i:8 + 2 * i] for i in range(5))
    small_one, small_two, local, recv_c, recv_v, recv_u, recv_a, send, small_send, small_recv = refs[16:]
    sizes, here = places()
    ndp, nmode = lax.axis_size("dp"), lax.axis_size("mode")
    dp, mode = lax.axis_index("dp"), lax.axis_index("mode")
    na, nb, ny = sizes["a"], sizes["b"], sizes["y"]
    group = na * nb * ny
    other = move(sizes, here, "c", 1)
    greet()

    def spot(at):
        return (at["a"] * nb + at["b"]) * ny + at["y"]

    loads = [pltpu.make_async_copy(ins[k].at[:, here["c"]], acc[k], local.at[k]) for k in range(kinds)]
    for load in loads:
        load.start()

    def to_partner(kind, at):
        n = spot(at)
        return pltpu.make_async_remote_copy(
            src_ref=ins[kind].at[n, other["c"]], dst_ref=from_c[kind].at[n],
            send_sem=send.at[kind, 0], recv_sem=recv_c.at[kind, n], device_id=device(sizes, other), device_id_type=MESH)

    small_one[mode] = small_in[...]

    def small_copy(buffer, axis, index, count, d, base):
        return pltpu.make_async_remote_copy(
            src_ref=buffer.at[index], dst_ref=buffer.at[index], send_sem=small_send.at[base + d - 1], recv_sem=small_recv.at[base + d - 1],
            device_id={**{"dp": dp, "mode": mode}, axis: lax.rem(index + d, count)}, device_id_type=MESH)
    ones = [small_copy(small_one, "mode", mode, nmode, d, 0) for d in range(1, nmode)]
    twos = [small_copy(small_two, "dp", dp, ndp, d, nmode - 1) for d in range(1, ndp)]
    for c in ones:
        c.start()

    def run(u, v):
        nu, nv = sizes[u], sizes[v]

        def owner(t, e, d):
            return move(sizes, move(sizes, move(sizes, here, "a", t + 1), u, e), v, d)

        for t in range(na):
            for d in list(range(1, nv)) + [0]:
                for e in list(range(1, nu)) + [0]:
                    for kind in range(kinds):
                        to_partner(kind, owner(t, e, d)).start()
        for load in loads:
            load.wait()

        def add(kind, n, terms):
            rows = acc[kind].shape[1]
            step = 16 if rows % 16 == 0 else rows

            def chunk(i, _):
                at = pl.ds(pl.multiple_of(i * step, step), step) if step != rows else slice(None)
                total = acc[kind][n, at, :].astype(F32)
                for ref, k in terms:
                    total = total + ref[k, at, :].astype(F32)
                acc[kind][n, at, :] = total.astype(BF)
                return 0
            lax.fori_loop(0, rows // step, chunk, 0)

        def slot_v(t, e, d):
            return (t * nu + e) * (nv - 1) + d - 1

        def copy_v(kind, t, e, d):
            at = owner(t, e, d)
            s = slot_v(t, e, d)
            return pltpu.make_async_remote_copy(
                src_ref=acc[kind].at[spot(at)], dst_ref=from_v[kind].at[s], send_sem=send.at[kind, 1], recv_sem=recv_v.at[kind, s],
                device_id=device(sizes, move(sizes, here, v, d)), device_id_type=MESH)

        def copy_u(kind, t, e):
            at = owner(t, e, 0)
            s = t * (nu - 1) + e - 1
            return pltpu.make_async_remote_copy(
                src_ref=acc[kind].at[spot(at)], dst_ref=from_u[kind].at[s], send_sem=send.at[kind, 2], recv_sem=recv_u.at[kind, s],
                device_id=device(sizes, move(sizes, here, u, e)), device_id_type=MESH)

        def copy_a(kind, t):
            at = owner(t, 0, 0)
            return pltpu.make_async_remote_copy(
                src_ref=acc[kind].at[spot(at)], dst_ref=from_a[kind].at[t], send_sem=send.at[kind, 3], recv_sem=recv_a.at[kind, t],
                device_id=device(sizes, at), device_id_type=MESH)

        def first(t):
            for d in range(1, nv):
                for e in list(range(1, nu)) + [0]:
                    at = owner(t, e, d)
                    for kind in range(kinds):
                        to_partner(kind, at).wait_recv()
                        add(kind, spot(at), [(from_c[kind], spot(at))])
                        copy_v(kind, t, e, d).start()

        def gathered(kind, t, e):
            at = owner(t, e, 0)
            to_partner(kind, at).wait_recv()
            terms = [(from_c[kind], spot(at))]
            for d in range(1, nv):
                copy_v(kind, t, e, d).wait_recv()
                terms.append((from_v[kind], slot_v(t, e, d)))
            return at, terms

        def second(t):
            for e in range(1, nu):
                for kind in range(kinds):
                    at, terms = gathered(kind, t, e)
                    add(kind, spot(at), terms)
                    copy_u(kind, t, e).start()

        def terms_of(kind, t):
            at, terms = gathered(kind, t, 0)
            for e in range(1, nu):
                copy_u(kind, t, e).wait_recv()
                terms.append((from_u[kind], t * (nu - 1) + e - 1))
            return at, terms

        def third(t):
            for kind in range(kinds):
                at, terms = terms_of(kind, t)
                add(kind, spot(at), terms)
                copy_a(kind, t).start()

        staggered(na - 1, first, second, third)
        first(na - 1)
        second(na - 1)
        for kind in range(kinds):
            at, terms = terms_of(kind, na - 1)
            for t in range(na - 1):
                copy_a(kind, t).wait_recv()
                terms.append((from_a[kind], t))
            n = spot(at)
            rows = acc[kind].shape[1]
            step = 16 if rows % 16 == 0 else rows

            def chunk(i, _):
                rows_at = pl.ds(pl.multiple_of(i * step, step), step) if step != rows else slice(None)
                total = acc[kind][n, rows_at, :].astype(F32)
                for ref, k in terms:
                    total = total + ref[k, rows_at, :].astype(F32)
                outs[kind][rows_at, :] = total
                return 0
            lax.fori_loop(0, rows // step, chunk, 0)

        def drain(kind, stage, count):
            ref = from_c[kind].at[pl.ds(0, count)]
            pltpu.make_async_copy(ref, ref, send.at[kind, stage]).wait()
        for kind in range(kinds):
            drain(kind, 0, group)
            drain(kind, 1, na * nu * (nv - 1))
            drain(kind, 2, na * (nu - 1))
            drain(kind, 3, na - 1)

    pl.when(here["c"] == 0)(lambda: run("b", "y"))
    pl.when(here["c"] == 1)(lambda: run("y", "b"))

    for c in ones:
        c.wait()
    small_two[dp] = functools.reduce(lambda p, q: p + q, [small_one[i] for i in range(nmode)])
    for c in twos:
        c.start()
    for c in twos:
        c.wait()
    small_out[...] = functools.reduce(lambda p, q: p + q, [small_two[i] for i in range(ndp)])


def reduce_scatter(dense, mixer, small):
    ndp, nmode = lax.axis_size("dp"), lax.axis_size("mode")
    nd = ndp * nmode
    group = nd // 2
    na, ny = ndp // 2, nmode // 2
    anywhere = pl.BlockSpec(memory_space=pl.ANY)
    vmem = pl.BlockSpec(memory_space=pltpu.VMEM)
    shapes = [x.shape[1:] for x in (dense, mixer)]
    count_v = max(na * 2 * (ny - 1), na * ny)
    count_u = na * max(ny - 1, 1)
    buffers = [pltpu.VMEM((count,) + s, BF) for count in (group, group, count_v, count_u, na - 1) for s in shapes]
    sem = lambda *s: pltpu.SemaphoreType.DMA(s)
    return pl.pallas_call(
        reduce_kernel,
        out_shape=tuple(jax.ShapeDtypeStruct(s, F32) for s in shapes) + (jax.ShapeDtypeStruct(small.shape, F32),),
        in_specs=[anywhere, anywhere, vmem],
        out_specs=(vmem,) * 3,
        scratch_shapes=buffers + [
            pltpu.VMEM((nmode,) + small.shape, F32), pltpu.VMEM((ndp,) + small.shape, F32),
            sem(2), sem(2, group), sem(2, count_v), sem(2, count_u), sem(2, na - 1), sem(2, 4),
            sem(ndp + nmode - 2), sem(ndp + nmode - 2),
        ],
        compiler_params=pltpu.CompilerParams(collective_id=1, has_side_effects=True, vmem_limit_bytes=60 * 1024 * 1024),
        name="reduce_scatter",
    )(dense.reshape((group, 2) + shapes[0]), mixer.reshape((group, 2) + shapes[1]), small)


def fourier_tables(mode_index, length):
    positions = jnp.arange(length, dtype=jnp.int32)
    phases = mode_index[:, None] * positions[None, :] % length
    angles = phases.astype(jnp.float32) * (2.0 * jnp.pi / length)
    forward = jnp.stack([jnp.cos(angles), -jnp.sin(angles)])
    slot_ids = jnp.arange(mode_index.shape[0], dtype=jnp.int32)
    back_phase = slot_ids[:, None] * positions[None, :] % length
    back_angle = back_phase.astype(jnp.float32) * (2.0 * jnp.pi / length)
    coefs = jnp.where(slot_ids == 0, 1.0, 2.0).astype(jnp.float32) / length
    inverse = jnp.stack(
        [jnp.cos(back_angle) * coefs[:, None], -jnp.sin(back_angle) * coefs[:, None]]
    )
    return (forward, jnp.transpose(inverse, (2, 0, 1)))


def adam_update(weight, gradient, moment, second, step_rate):
    moment_new = BETA_ONE * moment + (1.0 - BETA_ONE) * gradient
    second_new = BETA_TWO * second + (1.0 - BETA_TWO) * gradient * gradient
    scaled_m = moment_new / (1.0 - BETA_ONE**STEP)
    scaled_v = second_new / (1.0 - BETA_TWO**STEP)
    weight_new = weight - step_rate * (
        scaled_m / (jnp.sqrt(scaled_v) + ADAM_EPS) + DECAY_RATE * weight
    )
    return (moment_new, second_new, weight_new)


def shards(
    inputs,
    observed,
    out_grad,
    mode_index,
    owner_list,
    dense_master,
    dense_first,
    dense_second,
    mixer_master,
    mixer_first,
    mixer_second,
    small_master,
    small_first,
    small_second,
):
    ndp, nmode = lax.axis_size("dp"), lax.axis_size("mode")
    length, width = inputs.shape[1:]
    slots = mode_index.shape[0]
    hidden = (dense_master.shape[0] * ndp * nmode - 2 * width) // 2
    dense_all, mixer_all = gather(dense_master.astype(BF), mixer_master.astype(BF).reshape(-1, mixer_master.shape[2]))
    weights = mixer_all.reshape((ndp, nmode) + mixer_all.shape[1:])
    forward, inverse = fourier_tables(mode_index, length)
    basis = forward.astype(BF).reshape(2 * slots, length)
    inv = inverse.astype(BF).reshape(length, 2 * slots)
    wqo, wup, wdn = to_table(dense_all.reshape(-1, width), owner_list, hidden)
    acts, spectra, sig = front(inputs, observed, wqo, small_master[None, :width], basis, inv, weights)
    output, grad_summed, grad_mixed, g_out, g_up, g_down, sums = middle(
        small_master[2 * width :], acts.reshape(inputs.shape), sig.reshape(inputs.shape), out_grad, wqo, wup, wdn,
        small_master[None, width : 2 * width], inv,
    )
    input_grad, g_query, sum_query, g_mixer = back(
        grad_mixed.reshape(-1, width), spectra, acts, grad_summed.reshape(-1, width), observed, wqo, basis.T, weights
    )
    small_grad = jnp.concatenate(
        [
            jnp.sum(sum_query, axis=0).reshape(-1, 128),
            jnp.sum(sums[:8], axis=0).reshape(-1, 128),
            jnp.sum(sums[8:, :128].reshape(20, 8, 128), axis=1),
            jnp.zeros((4, 128), F32),
        ]
    )
    dense_grad = to_owners((g_query, g_out, g_up, g_down), owner_list)
    dense_mine, mixer_mine, small_all = reduce_scatter(
        dense_grad.reshape((ndp * nmode,) + dense_master.shape), g_mixer.reshape((ndp * nmode,) + g_mixer.shape[2:]), small_grad
    )
    small_total = jnp.concatenate([small_all[:8].reshape(-1), jnp.sum(small_all[8:28], axis=1)])
    dense_first_new, dense_second_new, dense_new = adam_update(
        dense_master, dense_mine, dense_first, dense_second, RATE_DENSE
    )
    mixer_first_new, mixer_second_new, mixer_new = adam_update(
        mixer_master, mixer_mine.reshape(mixer_master.shape), mixer_first, mixer_second, RATE_MIXER
    )
    small_first_new, small_second_new, small_new = adam_update(
        small_master, small_total, small_first, small_second, RATE_SMALL
    )
    return (
        output,
        input_grad.reshape(inputs.shape),
        dense_first_new,
        dense_second_new,
        dense_new,
        mixer_first_new,
        mixer_second_new,
        mixer_new,
        small_first_new,
        small_second_new,
        small_new,
        small_total[width : 2 * width],
    )


def solution(mesh):
    placed = (
        P(("dp", "mode"), None, None),
        P(("dp", "mode"), None),
        P(("dp", "mode"), None, None),
        P(),
        P(),
        P(("dp", "mode"), None),
        P(("dp", "mode"), None),
        P(("dp", "mode"), None),
        P("mode", "dp", None),
        P("mode", "dp", None),
        P("mode", "dp", None),
        P(),
        P(),
        P(),
    )
    return jax.shard_map(
        shards,
        mesh=mesh,
        in_specs=placed,
        out_specs=(
            P(("dp", "mode"), None, None),
            P(("dp", "mode"), None, None),
            P(("dp", "mode"), None),
            P(("dp", "mode"), None),
            P(("dp", "mode"), None),
            P("mode", "dp", None),
            P("mode", "dp", None),
            P("mode", "dp", None),
            P(),
            P(),
            P(),
            P(),
        ),
        check_vma=False,
    )
```

time: 694 us -> 356 us (0.51)
  Pallas kernels: 0 us -> 325 us
  waiting for transfers between devices: 206 us -> 0 us
  matrix products: 188 us -> 0 us
  other arithmetic: 107 us -> 12.8 us
  local copies, waits for them, and re-layouts: 110 us -> 17.2 us
  blocking collectives: 46.6 us -> 0 us
  starting transfers between devices: 14.9 us -> 0 us
  between operations: 15.4 us -> 0.82 us
    pallas_call x0 -> x7, Pallas kernels: none -> 325 us  [the longest x1 93.6 us: middle(): pl.pallas_call(functools.partial(middle_kernel, W, L, D, FF, steps), grid...]
    dot_general x23 -> x0, matrix products: 188 us -> none  [the longest x4 87 us: decompose(): averages = jnp.einsum('ktu,bud->kbtd', tables, series, precision=HIGH)]
    reduce_scatter x2 -> x0, waiting for transfers between devices: 90.7 us -> none  [the longest x1 90.7 us: shards(): lax.psum_scatter(dense_grad, ('dp', 'mode'), scatter_dimension=0, tiled=T...]
    all_gather x2 -> x0, waiting for transfers between devices: 60.2 us -> none  [the longest x1 60.2 us: shards(): lax.all_gather(dense_master.astype(jnp.bfloat16), ('dp', 'mode'), axis=0,...]
    all_to_all x4 -> x0, waiting for transfers between devices: 55.5 us -> none  [the longest x1 19.8 us: shards(): lax.all_to_all(mixed_modes, 'mode', split_axis=0, concat_axis=2, tiled=True)]
    reshape x7 -> x2, local copies, waits for them, and re-layouts: 54.3 us -> 1.49 us  [the longest x1 0.78 us: shards(): small_all[:8].reshape(-1)]
    reduce_sum x12 -> x4, other arithmetic: 50.1 us -> 3.2 us  [the longest x1 0.91 us: shards(): jnp.sum(sums[8:, :128].reshape(20, 8, 128), axis=1)]
    psum x1 -> x0, blocking collectives: 46.6 us -> none  [shards(): small_total = lax.psum(small_grad, ('dp', 'mode'))]
  transfers between devices with their start and end apart: 8 -> 0, of which waited for: 6 -> 0; matrix products, arithmetic and copies ran while one was open for 21% -> 0% of each run, Pallas kernels for 0% -> 0%
where the time goes in v1:
time: 356 us; the launch traced here: 355 us
  Pallas kernels  325 us (91%)
  local copies, waits for them, and re-layouts  17.2 us (5%)
  other arithmetic  12.8 us (4%)
    pallas_call x1, Pallas kernels, middle(): pl.pallas_call(functools.partial(middle_kernel, W, L, D, FF, steps), grid...  93.6 us
    pallas_call x1, Pallas kernels, reduce_scatter(): pl.pallas_call(reduce_kernel, out_shape=tuple((jax.ShapeDtypeStruct(s, F3...  78.3 us
    pallas_call x1, Pallas kernels, gather(): pl.pallas_call(gather_kernel, out_shape=tuple((jax.ShapeDtypeStruct((nd,)...  62.3 us
    pallas_call x1, Pallas kernels, back(): pl.pallas_call(functools.partial(back_kernel, n, L, D, slots), grid=(1,),...  44.3 us
    pallas_call x1, Pallas kernels, front(): pl.pallas_call(functools.partial(front_kernel, n, L, D, slots), grid=(1,)...  31.6 us
    unnamed x46, local copies, waits for them, and re-layouts  12.6 us
    pallas_call x1, Pallas kernels, to_owners(): pl.pallas_call(functools.partial(owners_kernel, blocks), grid_spec=pltpu....  7.56 us

profile of v1, /device:TPU:0, one launch (start us, length us, event | category | flops | bytes accessed | tf_op | source)
XLA Modules:
  0.0 355.3 jit_solution(7531709167416516758)
XLA Ops:
  0.6 1.7 convert_element_type.52
  2.4 1.7 convert_element_type.51.refs_0_
  4.0 62.3 %gather.1 = (bf16[32,160,512]{2,1,0:T(8,128)(2,1)}, bf16[32,768,128]{2,1,0:T(8,128)(2,1)}) custom-call(bf16[160,512]{1,0:T(8,128)(2,1)} %convert_element_type.51.refs_0_, bf16[768,128]{1,0:T(8,128)(2,1)} %bitcast.39), custom_call_target="tpu_custom_call" | custom-call | tf_op jit(solution)/shard_map/gather/pallas_call | solution.py:727
  66.4 2.5 copy-done.1
  68.8 0.7 copy-done.8
  69.5 6.9 %to_table.1 = (bf16[1024,512]{1,0:T(8,128)(2,1)S(1)}, bf16[2048,512]{1,0:T(8,128)(2,1)S(1)}, bf16[2048,512]{1,0:T(8,128)(2,1)S(1)}) custom-call(s32[256]{0:T(256)S(1)} %copy-done.8, bf16[5120,512]{1,0:T(8,128)(2,1)S(1)} %bitcast.29), custom_call_target="tpu_custom_call" | custom-call | tf_op jit(solution)/shard_map/to_table/pallas_call | solution.py:521
  76.5 0.0 copy-start
  76.5 1.0 copy-done
  77.5 1.3 copy-done.4
  78.8 1.4 copy-done.5
  80.2 0.1 multiply_convert_fusion.1
  80.3 0.0 copy-start.17
  80.4 0.7 copy.31.inv_ref
  81.1 0.2 cosine_convert_fusion
  81.3 0.6 pad_maximum_fusion
  81.9 0.6 fusion.2.eye_ref
  82.5 0.6 fusion.21
  83.1 31.6 %front.1 = (bf16[1536,512]{1,0:T(8,128)(2,1)}, bf16[8,768,128]{2,1,0:T(8,128)(2,1)}, bf16[1536,512]{1,0:T(8,128)(2,1)}) custom-call(bf16[1536,512]{1,0:T(8,128)(2,1)} %bitcast.38, s32[16,96]{1,0:T(8,128)} %obs_ref.3, bf16[1024,512]{1,0:T(8,128)(2,1)} %copy-done, f32[1,512]{1,0:T(1,128)} %bitcast.49, bf16[96,96]{1,0:T(8,128)(2,1)} %bitcast.43, ...), custom_call_target="tpu_custom_call" | custom-call | tf_op jit(solution)/shard_map/front/pallas_call | solution.py:394
  114.7 0.0 copy-done.17
  114.7 0.5 slice.28.mix_ref
  115.2 93.6 %middle.1 = (bf16[16,96,512]{2,1,0:T(8,128)(2,1)}, f32[16,96,512]{2,1,0:T(8,128)}, bf16[16,96,512]{2,1,0:T(8,128)(2,1)}, f32[512,512]{1,0:T(8,128)}, f32[2048,51...) custom-call(f32[20]{0:T(128)} %slice.28.mix_ref, bf16[16,96,512]{2,1,0:T(8,128)(2,1)} %bitcast.33, ...), custom_call_target="tpu_custom_call" | custom-call | tf_op jit(solution)/shard_map/middle/pallas_call | solution.py:264
  208.7 0.0 copy-done.18
  208.8 0.7 copy.32
  209.5 44.3 %back.1 = (f32[1536,512]{1,0:T(8,128)}, f32[512,512]{1,0:T(8,128)}, f32[8,512]{1,0:T(8,128)}, bf16[8,4,768,128]{3,2,1,0:T(8,128)(2,1)}) custom-call(bf16[1536,512]{1,0:T(8,128)(2,1)} %bitcast.36, bf16[8,768,128]{2,1,0:T(8,128)(2,1)} %get-tuple-element.43.z_ref, bf16[1536,512]{1,0:T(8,128)(2,1)} %get-tuple-element.37.acts_ref, f32[1536,512]{1,0:T(8,128)} %bitcast.35, ...), custom_call_target="tpu_custom_call" | custom-call | tf_op jit(solution)/shard_map/back/pallas_call | solution.py:469
  253.8 0.7 reduce_sum.36
  254.5 0.9 bitcast_reduce_fusion
  255.4 0.7 slice_reduce_fusion
  256.2 0.1 pad.5.clone
  256.2 0.7 maximum_maximum_fusion.refs_2_
  256.9 0.0 copy-done.6
  256.9 2.2 copy-done.2
  259.1 2.2 copy-done.3
  261.3 1.2 copy-done.7
  262.5 7.6 %to_owners.1 = bf16[5120,512]{1,0:T(8,128)(2,1)} custom-call(s32[256]{0:T(256)S(1)} %copy-done.9, f32[512,512]{1,0:T(8,128)S(1)} %copy-done.7, f32[512,512]{1,0:T(8,128)S(1)} %copy-done.6, f32[2048,512]{1,0:T(8,128)S(1)} %copy-done.2, f32[2048,512]{1,0:T(8,128)S(1)} %copy-done.3), custom_call_target="tpu_custom_call" | custom-call | tf_op jit(solution)/shard_map/to_owners/pallas_call | solution.py:572
  270.1 0.0 copy-start.13
  270.1 78.3 %reduce_scatter.1 = (f32[160,512]{1,0:T(8,128)}, f32[768,128]{1,0:T(8,128)}, f32[32,128]{1,0:T(8,128)}) custom-call(bf16[16,2,160,512]{3,2,1,0:T(8,128)(2,1)} %bitcast.32, bf16[16,2,768,128]{3,2,1,0:T(8,128)(2,1)} %bitcast.34, f32[32,128]{1,0:T(8,128)} %maximum_maximum_fusion.refs_2_), custom_call_target="tpu_custom_call" | custom-call | tf_op jit(solution)/shard_map/reduce_scatter/pallas_call | solution.py:919
  348.4 0.0 copy-start.11
  348.4 0.0 copy-start.14
  348.4 0.0 copy-start.15
  348.5 0.8 slice_bitcast_fusion
  349.2 0.8 slice_reduce_fusion.1
  350.1 0.6 multiply_subtract_fusion.2
  350.7 0.0 copy-done.10
  350.7 2.2 multiply_subtract_fusion
  352.9 0.0 copy-done.15
  352.9 0.0 copy-done.16
  352.9 1.1 multiply_subtract_fusion.1
  354.0 1.3 slice_bitcast_fusion.1
  (29 shorter events, 0.1 us)
Async XLA Ops:
  66.4 2.5 copy-start.1
  68.8 0.7 copy-start.8
  69.5 11.5 %copy-start.22 = (s32[48]{0:T(128)S(1)}, s32[48]{0:T(128)}, u32[]{:S(2)}) copy-start(s32[48]{0:T(128)} %param.19) | copy-start | bytes 580
  69.5 13.0 %copy-start.19 = (f32[1044]{0:T(1024)S(1)}, f32[1044]{0:T(1024)}, u32[]{:S(2)}) copy-start(f32[1044]{0:T(1024)} %param.27) | copy-start | bytes 12532
  76.5 1.0 copy-start
  77.5 1.3 copy-start.4
  78.8 1.4 copy-start.5
  80.3 34.3 %copy-start.17 = (bf16[2,48,96]{2,1,0:T(8,128)(2,1)}, bf16[2,48,96]{2,1,0:T(8,128)(2,1)S(1)}, u32[]{:S(2)}) copy-start(bf16[2,48,96]{2,1,0:T(8,128)(2,1)S(1)} %pad_maximum_fusion.1) | copy-start | bytes 55300
  115.2 93.6 %copy-start.18 = (bf16[2,48,96]{2,1,0:T(8,128)(2,1)S(1)}, bf16[2,48,96]{2,1,0:T(8,128)(2,1)}, u32[]{:S(2)}) copy-start(bf16[2,48,96]{2,1,0:T(8,128)(2,1)} %pad_maximum_fusion) | copy-start | bytes 55300
  209.5 47.5 %copy-start.6 = (f32[512,512]{1,0:T(8,128)S(1)}, f32[512,512]{1,0:T(8,128)}, u32[]{:S(2)}) copy-start(f32[512,512]{1,0:T(8,128)} %get-tuple-element.47.refs_1_) | copy-start | bytes 3145732
  209.5 47.5 %copy-start.9 = (s32[256]{0:T(256)S(1)}, s32[256]{0:T(256)}, u32[]{:S(2)}) copy-start(s32[256]{0:T(256)} %owner.3) | copy-start | bytes 3076
  256.9 2.2 copy-start.2
  259.1 2.2 copy-start.3
  261.3 1.2 copy-start.7
  270.1 80.0 %copy-start.20 = (f32[1044]{0:T(1024)S(1)}, f32[1044]{0:T(1024)}, u32[]{:S(2)}) copy-start(f32[1044]{0:T(1024)} %param.29) | copy-start | bytes 12532
  270.1 80.0 %copy-start.21 = (f32[1044]{0:T(1024)S(1)}, f32[1044]{0:T(1024)}, u32[]{:S(2)}) copy-start(f32[1044]{0:T(1024)} %param.28) | copy-start | bytes 12532
  270.1 80.6 %copy-start.10 = (f32[12,64,128]{2,1,0:T(8,128)S(1)}, f32[12,64,128]{2,1,0:T(8,128)}, u32[]{:S(2)}) copy-start(f32[12,64,128]{2,1,0:T(8,128)} %param.24) | copy-start | bytes 1179652
  270.1 80.6 %copy-start.12 = (f32[12,64,128]{2,1,0:T(8,128)S(1)}, f32[12,64,128]{2,1,0:T(8,128)}, u32[]{:S(2)}) copy-start(f32[12,64,128]{2,1,0:T(8,128)} %param.26) | copy-start | bytes 1179652
  270.1 80.6 %copy-start.13 = (f32[12,64,128]{2,1,0:T(8,128)S(1)}, f32[12,64,128]{2,1,0:T(8,128)}, u32[]{:S(2)}) copy-start(f32[12,64,128]{2,1,0:T(8,128)} %param.25) | copy-start | bytes 1179652
  348.4 4.5 %copy-start.11 = (f32[160,512]{1,0:T(8,128)S(1)}, f32[160,512]{1,0:T(8,128)}, u32[]{:S(2)}) copy-start(f32[160,512]{1,0:T(8,128)} %param.21) | copy-start | bytes 983044
  348.4 4.5 %copy-start.14 = (f32[160,512]{1,0:T(8,128)S(1)}, f32[160,512]{1,0:T(8,128)}, u32[]{:S(2)}) copy-start(f32[160,512]{1,0:T(8,128)} %param.23) | copy-start | bytes 983044
  348.4 4.5 %copy-start.15 = (f32[160,512]{1,0:T(8,128)S(1)}, f32[160,512]{1,0:T(8,128)}, u32[]{:S(2)}) copy-start(f32[160,512]{1,0:T(8,128)} %param.22) | copy-start | bytes 983044
  348.5 4.5 %copy-start.16 = (f32[160,512]{1,0:T(8,128)S(1)}, f32[160,512]{1,0:T(8,128)}, u32[]{:S(2)}) copy-start(f32[160,512]{1,0:T(8,128)} %get-tuple-element.53) | copy-start | bytes 983044

commit v2 on v1

--- a/solution.py
+++ b/solution.py
@@ -304,6 +304,9 @@
     )(mix, acts, sig, og, wqo, wup, wdn, bias, inv.T, cnt, cntt)
 
 
+UNROLL = 4
+
+
 def sign_lanes(rows, left, right):
     lane = lax.broadcasted_iota(jnp.int32, (rows, 128), 1)
     return jnp.where(lane < 64, left, right).astype(F32)
@@ -333,11 +336,12 @@
         tiles[2 * v + 1, pl.ds(w, slots, stride=n), :] = two
 
 
-def head_matrix(weights, h, pieces, mode, rows):
-    top = jnp.concatenate([weights[h * pieces + q, mode, rows, :] for q in range(pieces)], 0)
-    wide = top.astype(F32)
-    low = pltpu.roll(wide, 64, 1) * sign_lanes(wide.shape[0], -1.0, 1.0)
-    return jnp.concatenate([top, low.astype(BF)], 0)
+def swap_halves(x):
+    return pltpu.roll(x, 64, 1)
+
+
+def head_weights(weights, h, pieces, mode, rows):
+    return jnp.concatenate([weights[h * pieces + q, mode, rows, :] for q in range(pieces)], 0)
 
 
 def front_kernel(n, L, D, slots, in_ref, obs_ref, wq_ref, bias_ref, basis_ref, inv_ref, eye_ref, weights,
@@ -373,11 +377,13 @@
             at = pl.ds(pl.multiple_of((mode * per + jl) * n, n), n)
             rows = pl.ds(pl.multiple_of(jl * depth, depth), depth)
             for h in range(heads):
-                x = tiles[h, at, :].astype(BF)
-                z_ref[h, at, :] = x
-                outs[h, at, :] = dot(x, head_matrix(weights, h, pieces, mode, rows))
+                x = tiles[h, at, :]
+                both = jnp.concatenate([x, swap_halves(x)], 0)[:, :64].astype(BF)
+                z_ref[h, pl.ds(pl.multiple_of((mode * per + jl) * 2 * n, 2 * n), 2 * n), :] = both
+                y = dot(both, head_weights(weights, h, pieces, mode, rows))
+                outs[h, at, :] = y[:n] + swap_halves(y[n:]) * sign_lanes(n, -1.0, 1.0)
             return 0
-        lax.fori_loop(0, per, slot, 0)
+        lax.fori_loop(0, per, slot, 0, unroll=UNROLL)
 
     def signal(w, _):
         rows = pl.ds(pl.multiple_of(w * L, 32), L)
@@ -396,12 +402,12 @@
         grid=(1,),
         out_shape=(
             jax.ShapeDtypeStruct((n * L, D), BF),
-            jax.ShapeDtypeStruct((8, slots * n, 128), BF),
+            jax.ShapeDtypeStruct((8, 2 * slots * n, 64), BF),
             jax.ShapeDtypeStruct((n * L, D), BF),
         ),
         in_specs=[whole(n * L, D), whole(n, L), whole(D, D), whole(1, D), whole(2 * slots, L), whole(L, 2 * slots), whole(L, L),
                   whole(*weights.shape)],
-        out_specs=(whole(n * L, D), whole(8, slots * n, 128), whole(n * L, D)),
+        out_specs=(whole(n * L, D), whole(8, 2 * slots * n, 64), whole(n * L, D)),
         scratch_shapes=[
             pltpu.VMEM((n * L, D), BF),
             pltpu.VMEM((8, slots * n, 128), F32),
@@ -410,82 +416,6 @@
         compiler_params=pltpu.CompilerParams(vmem_limit_bytes=60 * 1024 * 1024),
         name="front",
     )(inputs.reshape(n * L, D), observed, wqo, bias, basis, inv, jnp.eye(L, dtype=F32), weights)
-
-
-def back_kernel(n, L, D, slots, gmix_ref, z_ref, acts_ref, gsum_ref, obs_ref, wq_ref, basist_ref, eye_ref, weights,
-                gin_ref, gq_ref, gbias_ref, gmixer_ref, tiles, outs, glow):
-    ndp, nmode = weights.shape[:2]
-    per = slots // nmode
-    heads = 8
-    pieces = ndp // heads
-    depth = 64 // pieces
-
-    def spectra(w, _):
-        rows = pl.ds(pl.multiple_of(w * L, 32), L)
-        spread_rows(tiles, w, slots, n, gmix_ref[rows, :].astype(F32))
-        return 0
-    lax.fori_loop(0, n, spectra, 0)
-
-    for mode in range(nmode):
-        def slot(jl, _):
-            at = pl.ds(pl.multiple_of((mode * per + jl) * n, n), n)
-            rows = pl.ds(pl.multiple_of(jl * depth, depth), depth)
-            for h in range(heads):
-                y = tiles[h, at, :].astype(BF)
-                outs[h, at, :] = dot(y, head_matrix(weights, h, pieces, mode, rows), NT)
-                g = dot(z_ref[h, at, :], y, TN)
-                g = (g[:64] + pltpu.roll(g[64:], 64, 1) * sign_lanes(64, 1.0, -1.0)).astype(BF)
-                for q in range(pieces):
-                    gmixer_ref[h * pieces + q, mode, rows, :] = g[q * depth:(q + 1) * depth]
-            return 0
-        lax.fori_loop(0, per, slot, 0)
-    gbias_ref[...] = jnp.zeros_like(gbias_ref)
-
-    def query(w, _):
-        rows = pl.ds(pl.multiple_of(w * L, 32), L)
-        g = dot(basist_ref[...], gather_rows(outs, w, slots, n))
-        glow[rows, :] = g.astype(BF)
-        gbias_ref[...] += functools.reduce(lambda a, b: a + b, [g[i * 8:(i + 1) * 8] for i in range(L // 8)])
-        return 0
-    lax.fori_loop(0, n, query, 0)
-    gq_ref[...] = dot(acts_ref[...], glow[...], TN)
-
-    def input_grad(w, _):
-        rows = pl.ds(pl.multiple_of(w * L, 32), L)
-        row = obs_ref[pl.ds(w, 1), :].astype(F32)
-        mask = dot((eye_ref[...] * row).astype(BF), jnp.ones((L, 128), BF))
-        g = gsum_ref[rows, :] + dot(glow[rows, :], wq_ref[...], NT)
-        for c in range(D // 128):
-            gin_ref[rows, c * 128:(c + 1) * 128] = g[:, c * 128:(c + 1) * 128] * mask
-        return 0
-    lax.fori_loop(0, n, input_grad, 0)
-
-
-def back(gmix, z, acts, gsum, observed, wqo, basist, weights):
-    n, L = observed.shape
-    D = acts.shape[1]
-    slots = basist.shape[1] // 2
-    whole = lambda *s: pl.BlockSpec(s, lambda i: (0,) * len(s), pipeline_mode=pl.Buffered(1))
-    return pl.pallas_call(
-        functools.partial(back_kernel, n, L, D, slots),
-        grid=(1,),
-        out_shape=(
-            jax.ShapeDtypeStruct((n * L, D), F32),
-            jax.ShapeDtypeStruct((D, D), F32),
-            jax.ShapeDtypeStruct((8, D), F32),
-            jax.ShapeDtypeStruct(weights.shape, BF),
-        ),
-        in_specs=[whole(n * L, D), whole(8, slots * n, 128), whole(n * L, D), whole(n * L, D), whole(n, L), whole(D, D),
-                  whole(L, 2 * slots), whole(L, L), whole(*weights.shape)],
-        out_specs=(whole(n * L, D), whole(D, D), whole(8, D), whole(*weights.shape)),
-        scratch_shapes=[
-            pltpu.VMEM((8, slots * n, 128), F32),
-            pltpu.VMEM((8, slots * n, 128), F32),
-            pltpu.VMEM((n * L, D), BF),
-        ],
-        compiler_params=pltpu.CompilerParams(vmem_limit_bytes=60 * 1024 * 1024),
-        name="back",
-    )(gmix, z, acts, gsum, observed, wqo, basist, jnp.eye(L, dtype=F32), weights)
 
 
 def table_kernel(blocks, owner, in_ref, wqo_ref, wup_ref, wdn_ref, src, dst):
@@ -537,53 +467,6 @@
     )(owner_list, gathered)
 
 
-def owners_kernel(blocks, owner, *refs):
-    parts, out_ref, src, dst = refs[:4], refs[4], refs[5], refs[6]
-    rows = out_ref.shape[0]
-    size = rows // blocks
-    step = 256
-    start = 0
-    for ref in parts:
-        def take(i, _):
-            to = pl.ds(pl.multiple_of(start + i * step, step), step)
-            at = pl.ds(pl.multiple_of(i * step, step), step)
-            src[to, :] = ref[at, :]
-            return 0
-        lax.fori_loop(0, ref.shape[0] // step, take, 0)
-        start += ref.shape[0]
-
-    def move(j, _):
-        dst[pl.ds(j * size, size), :] = src[pl.ds(owner[j] * size, size), :]
-        return 0
-    lax.fori_loop(0, blocks, move, 0, unroll=4)
-
-    def narrow(i, _):
-        at = pl.ds(pl.multiple_of(i * step, step), step)
-        out_ref[at, :] = dst[at, :].astype(BF)
-        return 0
-    lax.fori_loop(0, rows // step, narrow, 0)
-
-
-def to_owners(parts, owner_list):
-    D = parts[0].shape[1]
-    rows = sum(p.shape[0] for p in parts)
-    blocks = owner_list.shape[0]
-    cols = lambda r: pl.BlockSpec((r, 128), lambda i, o: (0, i))
-    return pl.pallas_call(
-        functools.partial(owners_kernel, blocks),
-        grid_spec=pltpu.PrefetchScalarGridSpec(
-            num_scalar_prefetch=1,
-            grid=(D // 128,),
-            in_specs=[cols(p.shape[0]) for p in parts],
-            out_specs=cols(rows),
-            scratch_shapes=[pltpu.VMEM((rows + 8, 128), F32), pltpu.VMEM((rows + 8, 128), F32)],
-        ),
-        out_shape=jax.ShapeDtypeStruct((rows, D), BF),
-        compiler_params=pltpu.CompilerParams(vmem_limit_bytes=40 * 1024 * 1024),
-        name="to_owners",
-    )(owner_list, *parts)
-
-
 MESH = pl.DeviceIdType.MESH
 
 
@@ -735,34 +618,246 @@
     )(dense, mixer)
 
 
-def reduce_kernel(*refs):
-    kinds = 2
-    ins, small_in = refs[:2], refs[2]
-    outs, small_out = refs[3:5], refs[5]
-    acc, from_c, from_v, from_u, from_a = (refs[6 + 2 * i:8 + 2 * i] for i in range(5))
-    small_one, small_two, local, recv_c, recv_v, recv_u, recv_a, send, small_send, small_recv = refs[16:]
-    sizes, here = places()
+def roles():
+    ndp, nmode = lax.axis_size("dp"), lax.axis_size("mode")
+    half = nmode // 2
+    dp, mode = lax.axis_index("dp"), lax.axis_index("mode")
+    b, y, c = lax.rem(dp, half), mode // 2, lax.rem(mode, 2)
+    here = {"a": dp // half, "u": jnp.where(c == 0, b, y), "v": jnp.where(c == 0, y, b), "c": c}
+    return {"a": ndp // half, "u": half, "v": half, "c": 2}, here
+
+
+def place_of(sizes, at):
+    b = jnp.where(at["c"] == 0, at["u"], at["v"])
+    y = jnp.where(at["c"] == 0, at["v"], at["u"])
+    return at["a"] * sizes["u"] + b, y * 2 + at["c"]
+
+
+def device_of(sizes, at):
+    dp, mode = place_of(sizes, at)
+    return {"dp": dp, "mode": mode}
+
+
+def partner_of(at):
+    return {"a": at["a"], "u": at["v"], "v": at["u"], "c": 1 - at["c"]}
+
+
+def reducer(sizes, here, own, from_c, from_v, from_u, from_a, out, send, recv_c, recv_v, recv_u, recv_a):
+    na, nu, nv = sizes["a"], sizes["u"], sizes["v"]
+    rows = from_c.shape[1]
+    step = next(s for s in (96, 32, rows) if rows % s == 0)
+
+    def owner(t, e, d):
+        return move(sizes, move(sizes, move(sizes, here, "a", t + 1), "u", e), "v", d)
+
+    def spot(at):
+        dp, mode = place_of(sizes, at)
+        return dp * sizes["v"] + mode // 2
+
+    def to_partner(at):
+        n = spot(at)
+        return pltpu.make_async_remote_copy(
+            src_ref=own(at), dst_ref=from_c.at[n], send_sem=send.at[0], recv_sem=recv_c.at[n],
+            device_id=device_of(sizes, partner_of(here)), device_id_type=MESH)
+
+    def chunks(at, terms, store):
+        mine = own(at)
+
+        def chunk(i, _):
+            part = pl.ds(pl.multiple_of(i * step, step), step) if step != rows else slice(None)
+            total = mine[part, :].astype(F32)
+            for ref, k in terms:
+                total = total + ref[k, part, :].astype(F32)
+            store(mine, part, total)
+            return 0
+        lax.fori_loop(0, rows // step, chunk, 0)
+
+    def keep(mine, part, total):
+        mine[part, :] = total.astype(BF)
+
+    def finish(mine, part, total):
+        out[part, :] = total
+
+    def slot_v(t, e, d):
+        return (t * nu + e) * (nv - 1) + d - 1
+
+    def copy(at, buffer, s, stage, sems, to):
+        return pltpu.make_async_remote_copy(
+            src_ref=own(at), dst_ref=buffer.at[s], send_sem=send.at[stage], recv_sem=sems.at[s],
+            device_id=device_of(sizes, to), device_id_type=MESH)
+
+    def copy_v(t, e, d):
+        s = slot_v(t, e, d)
+        return copy(owner(t, e, d), from_v, s, 1, recv_v, move(sizes, here, "v", d))
+
+    def copy_u(t, e):
+        return copy(owner(t, e, 0), from_u, t * (nu - 1) + e - 1, 2, recv_u, move(sizes, here, "u", e))
+
+    def copy_a(t):
+        return copy(owner(t, 0, 0), from_a, t, 3, recv_a, owner(t, 0, 0))
+
+    def heard(at):
+        n = spot(at)
+        pltpu.make_async_remote_copy(
+            src_ref=own(at), dst_ref=from_c.at[n], send_sem=send.at[0], recv_sem=recv_c.at[n],
+            device_id=device_of(sizes, partner_of(here)), device_id_type=MESH).wait_recv()
+        return [(from_c, n)]
+
+    def first(t):
+        for d in range(1, nv):
+            for e in range(nu):
+                at = owner(t, e, d)
+                chunks(at, heard(at), keep)
+                copy_v(t, e, d).start()
+
+    def after_v(t, e):
+        terms = heard(owner(t, e, 0))
+        for d in range(1, nv):
+            copy_v(t, e, d).wait_recv()
+            terms.append((from_v, slot_v(t, e, d)))
+        return terms
+
+    def second(t):
+        for e in range(1, nu):
+            chunks(owner(t, e, 0), after_v(t, e), keep)
+            copy_u(t, e).start()
+
+    def after_u(t):
+        terms = after_v(t, 0)
+        for e in range(1, nu):
+            copy_u(t, e).wait_recv()
+            terms.append((from_u, t * (nu - 1) + e - 1))
+        return terms
+
+    def third(t):
+        chunks(owner(t, 0, 0), after_u(t), keep)
+        copy_a(t).start()
+
+    def last():
+        terms = after_u(na - 1)
+        for t in range(na - 1):
+            copy_a(t).wait_recv()
+            terms.append((from_a, t))
+        chunks(here, terms, finish)
+
+    def drain():
+        for stage, count in ((0, from_c.shape[0]), (1, na * nu * (nv - 1)), (2, na * (nu - 1)), (3, na - 1)):
+            ref = from_c.at[pl.ds(0, count)]
+            pltpu.make_async_copy(ref, ref, send.at[stage]).wait()
+
+    return to_partner, first, second, third, last, drain
+
+
+def each(start, stop, *steps):
+    def body(t, _):
+        for s in steps:
+            s(t)
+        return 0
+    lax.fori_loop(start, stop, body, 0)
+
+
+def tail_kernel(n, L, D, slots, blocks, owner, gmix_h, z_h, acts_h, gsum_h, weights_h, gout_h, gup_h, gdn_h,
+                obs_ref, wq_ref, basist_ref, eye_ref, sums_ref,
+                dense_out, mixer_out, small_out, gin_h,
+                gmix, z, acts, gsum, mix, src, tiles, glow, gbias, tmp, con,
+                fc0, fc1, fv0, fv1, fu0, fu1, fa0, fa1, small_one, small_two,
+                loads, send, recv_c, recv_v, recv_u, recv_a, small_send, small_recv):
+    sizes, here = roles()
     ndp, nmode = lax.axis_size("dp"), lax.axis_size("mode")
     dp, mode = lax.axis_index("dp"), lax.axis_index("mode")
-    na, nb, ny = sizes["a"], sizes["b"], sizes["y"]
-    group = na * nb * ny
-    other = move(sizes, here, "c", 1)
+    na = sizes["a"]
+    per = slots // nmode
+    heads = 8
+    pieces = ndp // heads
+    depth = 64 // pieces
+    rows = con.shape[1]
+    size = con.shape[0] * rows // blocks
+
+    def load(i, a, b):
+        return pltpu.make_async_copy(a, b, loads.at[i])
+    firsts = [load(0, gmix_h, gmix), load(1, z_h, z), load(2, weights_h, mix)]
+    later = [load(3, acts_h, acts), load(4, gsum_h, gsum)]
+    grads = []
+    start = D
+    for i, ref in enumerate((gout_h, gup_h, gdn_h)):
+        for c in range(D // 128):
+            grads.append(load(5 + i * 4 + c, ref.at[:, pl.ds(c * 128, 128)], src.at[c, pl.ds(start, ref.shape[0]), :]))
+        start += ref.shape[0]
+    for c in firsts + later + grads:
+        c.start()
     greet()
 
-    def spot(at):
-        return (at["a"] * nb + at["b"]) * ny + at["y"]
-
-    loads = [pltpu.make_async_copy(ins[k].at[:, here["c"]], acc[k], local.at[k]) for k in range(kinds)]
-    for load in loads:
-        load.start()
-
-    def to_partner(kind, at):
-        n = spot(at)
-        return pltpu.make_async_remote_copy(
-            src_ref=ins[kind].at[n, other["c"]], dst_ref=from_c[kind].at[n],
-            send_sem=send.at[kind, 0], recv_sem=recv_c.at[kind, n], device_id=device(sizes, other), device_id_type=MESH)
-
-    small_one[mode] = small_in[...]
+    send_m, first_m, second_m, third_m, last_m, drain_m = reducer(
+        sizes, here, lambda at: mix.at[place_of(sizes, at)], fc1, fv1, fu1, fa1, mixer_out,
+        send.at[1], recv_c.at[1], recv_v.at[1], recv_u.at[1], recv_a.at[1])
+
+    def con_at(at):
+        p, m = place_of(sizes, at)
+        return con.at[p * nmode + m]
+    send_d, first_d, second_d, third_d, last_d, drain_d = reducer(
+        sizes, here, con_at, fc0, fv0, fu0, fa0, dense_out,
+        send.at[0], recv_c.at[0], recv_v.at[0], recv_u.at[0], recv_a.at[0])
+
+    firsts[0].wait()
+
+    def spectra(w):
+        part = pl.ds(pl.multiple_of(w * L, 32), L)
+        spread_rows(tiles, w, slots, n, gmix[part, :].astype(F32))
+    each(0, n, spectra)
+    firsts[1].wait()
+    firsts[2].wait()
+
+    def mix_mode(m):
+        def slot(jl, _):
+            at = pl.ds(pl.multiple_of((m * per + jl) * n, n), n)
+            at2 = pl.ds(pl.multiple_of((m * per + jl) * 2 * n, 2 * n), 2 * n)
+            part = pl.ds(pl.multiple_of(jl * depth, depth), depth)
+            for h in range(heads):
+                y = tiles[h, at, :]
+                both = jnp.concatenate([y, swap_halves(y) * sign_lanes(n, 1.0, -1.0)], 0).astype(BF)
+                x = dot(both, head_weights(mix, h, pieces, m, part), NT)
+                tiles[h, at, :] = jnp.concatenate([x[:n], x[n:]], 1)
+                g = dot(z[h, at2, :], both, TN).astype(BF)
+                for q in range(pieces):
+                    mix[h * pieces + q, m, part, :] = g[q * depth:(q + 1) * depth]
+            return 0
+        lax.fori_loop(0, per, slot, 0, unroll=2)
+
+    mine_y = mode // 2
+
+    def mode_at(i, core):
+        return lax.rem(mine_y + 1 + i, nmode // 2) * 2 + core
+
+    def other_modes(i):
+        m = mode_at(i, 1 - here["c"])
+        mix_mode(m)
+
+        def hand(p):
+            half = sizes["u"]
+            b, y = lax.rem(p, half), m // 2
+            core = 1 - here["c"]
+            send_m({"a": p // half, "u": jnp.where(core == 0, b, y), "v": jnp.where(core == 0, y, b), "c": core}).start()
+        each(0, ndp, hand)
+    each(0, nmode // 2, other_modes)
+    each(0, nmode // 2, lambda i: mix_mode(mode_at(i, here["c"])))
+    each(0, na, first_m)
+
+    gbias[...] = jnp.zeros_like(gbias)
+
+    def query(w):
+        part = pl.ds(pl.multiple_of(w * L, 32), L)
+        g = dot(basist_ref[...], gather_rows(tiles, w, slots, n))
+        glow[part, :] = g.astype(BF)
+        gbias[...] += functools.reduce(lambda p, q: p + q, [g[i * 8:(i + 1) * 8] for i in range(L // 8)])
+    each(0, n, query)
+
+    for k, sums in ((0, gbias[...]), (4, sums_ref[0:8, :])):
+        total = jnp.sum(sums, axis=0, keepdims=True)
+        for c in range(D // 128):
+            small_one[mode, k + c:k + c + 1, :] = total[:, c * 128:(c + 1) * 128]
+    for k in range(20):
+        small_one[mode, 8 + k:9 + k, :] = jnp.sum(sums_ref[8 + 8 * k:16 + 8 * k, 0:128], axis=0, keepdims=True)
+    small_one[mode, 28:32, :] = jnp.zeros((4, 128), F32)
 
     def small_copy(buffer, axis, index, count, d, base):
         return pltpu.make_async_remote_copy(
@@ -773,162 +868,115 @@
     for c in ones:
         c.start()
 
-    def run(u, v):
-        nu, nv = sizes[u], sizes[v]
-
-        def owner(t, e, d):
-            return move(sizes, move(sizes, move(sizes, here, "a", t + 1), u, e), v, d)
-
-        for t in range(na):
-            for d in list(range(1, nv)) + [0]:
-                for e in list(range(1, nu)) + [0]:
-                    for kind in range(kinds):
-                        to_partner(kind, owner(t, e, d)).start()
-        for load in loads:
-            load.wait()
-
-        def add(kind, n, terms):
-            rows = acc[kind].shape[1]
-            step = 16 if rows % 16 == 0 else rows
-
-            def chunk(i, _):
-                at = pl.ds(pl.multiple_of(i * step, step), step) if step != rows else slice(None)
-                total = acc[kind][n, at, :].astype(F32)
-                for ref, k in terms:
-                    total = total + ref[k, at, :].astype(F32)
-                acc[kind][n, at, :] = total.astype(BF)
-                return 0
-            lax.fori_loop(0, rows // step, chunk, 0)
-
-        def slot_v(t, e, d):
-            return (t * nu + e) * (nv - 1) + d - 1
-
-        def copy_v(kind, t, e, d):
-            at = owner(t, e, d)
-            s = slot_v(t, e, d)
-            return pltpu.make_async_remote_copy(
-                src_ref=acc[kind].at[spot(at)], dst_ref=from_v[kind].at[s], send_sem=send.at[kind, 1], recv_sem=recv_v.at[kind, s],
-                device_id=device(sizes, move(sizes, here, v, d)), device_id_type=MESH)
-
-        def copy_u(kind, t, e):
-            at = owner(t, e, 0)
-            s = t * (nu - 1) + e - 1
-            return pltpu.make_async_remote_copy(
-                src_ref=acc[kind].at[spot(at)], dst_ref=from_u[kind].at[s], send_sem=send.at[kind, 2], recv_sem=recv_u.at[kind, s],
-                device_id=device(sizes, move(sizes, here, u, e)), device_id_type=MESH)
-
-        def copy_a(kind, t):
-            at = owner(t, 0, 0)
-            return pltpu.make_async_remote_copy(
-                src_ref=acc[kind].at[spot(at)], dst_ref=from_a[kind].at[t], send_sem=send.at[kind, 3], recv_sem=recv_a.at[kind, t],
-                device_id=device(sizes, at), device_id_type=MESH)
-
-        def first(t):
-            for d in range(1, nv):
-                for e in list(range(1, nu)) + [0]:
-                    at = owner(t, e, d)
-                    for kind in range(kinds):
-                        to_partner(kind, at).wait_recv()
-                        add(kind, spot(at), [(from_c[kind], spot(at))])
-                        copy_v(kind, t, e, d).start()
-
-        def gathered(kind, t, e):
-            at = owner(t, e, 0)
-            to_partner(kind, at).wait_recv()
-            terms = [(from_c[kind], spot(at))]
-            for d in range(1, nv):
-                copy_v(kind, t, e, d).wait_recv()
-                terms.append((from_v[kind], slot_v(t, e, d)))
-            return at, terms
-
-        def second(t):
-            for e in range(1, nu):
-                for kind in range(kinds):
-                    at, terms = gathered(kind, t, e)
-                    add(kind, spot(at), terms)
-                    copy_u(kind, t, e).start()
-
-        def terms_of(kind, t):
-            at, terms = gathered(kind, t, 0)
-            for e in range(1, nu):
-                copy_u(kind, t, e).wait_recv()
-                terms.append((from_u[kind], t * (nu - 1) + e - 1))
-            return at, terms
-
-        def third(t):
-            for kind in range(kinds):
-                at, terms = terms_of(kind, t)
-                add(kind, spot(at), terms)
-                copy_a(kind, t).start()
-
-        staggered(na - 1, first, second, third)
-        first(na - 1)
-        second(na - 1)
-        for kind in range(kinds):
-            at, terms = terms_of(kind, na - 1)
-            for t in range(na - 1):
-                copy_a(kind, t).wait_recv()
-                terms.append((from_a[kind], t))
-            n = spot(at)
-            rows = acc[kind].shape[1]
-            step = 16 if rows % 16 == 0 else rows
-
-            def chunk(i, _):
-                rows_at = pl.ds(pl.multiple_of(i * step, step), step) if step != rows else slice(None)
-                total = acc[kind][n, rows_at, :].astype(F32)
-                for ref, k in terms:
-                    total = total + ref[k, rows_at, :].astype(F32)
-                outs[kind][rows_at, :] = total
-                return 0
-            lax.fori_loop(0, rows // step, chunk, 0)
-
-        def drain(kind, stage, count):
-            ref = from_c[kind].at[pl.ds(0, count)]
-            pltpu.make_async_copy(ref, ref, send.at[kind, stage]).wait()
-        for kind in range(kinds):
-            drain(kind, 0, group)
-            drain(kind, 1, na * nu * (nv - 1))
-            drain(kind, 2, na * (nu - 1))
-            drain(kind, 3, na - 1)
-
-    pl.when(here["c"] == 0)(lambda: run("b", "y"))
-    pl.when(here["c"] == 1)(lambda: run("y", "b"))
-
+    for c in later:
+        c.wait()
+    g = dot(acts[...], glow[...], TN)
+    for c in range(D // 128):
+        src[c, 0:D, :] = g[:, c * 128:(c + 1) * 128]
+    each(0, na // 2, second_m)
+    for c in grads:
+        c.wait()
+
+    per_shard = rows // size
+    join = 4 if per_shard % 4 == 0 else 1
+    units = per_shard // join
+
+    def pick(s):
+        for k in range(units):
+            for c in range(D // 128):
+                for i in range(join):
+                    row = owner[(s * units + k) * join + i] * size
+                    tmp[c, i * size:(i + 1) * size, :] = src[c, pl.ds(row, size), :]
+                part = slice(k * join * size, (k + 1) * join * size)
+                con[s, part, c * 128:(c + 1) * 128] = tmp[c, 0:join * size, :].astype(BF)
+    shards = con.shape[0]
+    each(0, shards // 2, pick)
+    each(na // 2, na, second_m)
+    each(0, na // 2, third_m)
+    each(shards // 2, shards, pick)
+
+    def hand_line(t):
+        other = partner_of(here)
+        for d in list(range(1, sizes["v"])) + [0]:
+            for e in range(sizes["u"]):
+                send_d(move(sizes, move(sizes, move(sizes, other, "a", t + 1), "u", e), "v", d)).start()
+    each(0, na, hand_line)
+    each(na // 2, na - 1, third_m)
+
+    def input_grad(w):
+        part = pl.ds(pl.multiple_of(w * L, 32), L)
+        row = obs_ref[pl.ds(w, 1), :].astype(F32)
+        mask = dot((eye_ref[...] * row).astype(BF), jnp.ones((L, 128), BF))
+        g = gsum[part, :] + dot(glow[part, :], wq_ref[...], NT)
+        for c in range(D // 128):
+            gsum[part, c * 128:(c + 1) * 128] = g[:, c * 128:(c + 1) * 128] * mask
     for c in ones:
         c.wait()
     small_two[dp] = functools.reduce(lambda p, q: p + q, [small_one[i] for i in range(nmode)])
     for c in twos:
         c.start()
+    each(0, na, first_d)
+    each(0, n, input_grad)
+    result = load(17, gsum, gin_h)
+    result.start()
+    each(0, 1, second_d)
+    each(1, na - 1, second_d, lambda t: third_d(t - 1))
+    last_m()
+    second_d(na - 1)
+    third_d(na - 2)
+    last_d()
     for c in twos:
         c.wait()
     small_out[...] = functools.reduce(lambda p, q: p + q, [small_two[i] for i in range(ndp)])
-
-
-def reduce_scatter(dense, mixer, small):
-    ndp, nmode = lax.axis_size("dp"), lax.axis_size("mode")
+    drain_m()
+    drain_d()
+    result.wait()
+
+
+def tail(gmix, z, acts, gsum, observed, wqo, basist, weights, gout, gup, gdn, sums, owner_list, shard_rows):
+    n, L = observed.shape
+    D = acts.shape[1]
+    slots = basist.shape[1] // 2
+    ndp, nmode, mixer_rows = weights.shape[:3]
     nd = ndp * nmode
+    total = nd * shard_rows
+    half = nmode // 2
+    na = ndp // half
     group = nd // 2
-    na, ny = ndp // 2, nmode // 2
     anywhere = pl.BlockSpec(memory_space=pl.ANY)
     vmem = pl.BlockSpec(memory_space=pltpu.VMEM)
-    shapes = [x.shape[1:] for x in (dense, mixer)]
-    count_v = max(na * 2 * (ny - 1), na * ny)
-    count_u = na * max(ny - 1, 1)
-    buffers = [pltpu.VMEM((count,) + s, BF) for count in (group, group, count_v, count_u, na - 1) for s in shapes]
+    shapes = ((shard_rows, D), (mixer_rows, 128))
+    counts = (group, na * half * (half - 1), na * (half - 1), na - 1)
     sem = lambda *s: pltpu.SemaphoreType.DMA(s)
     return pl.pallas_call(
-        reduce_kernel,
-        out_shape=tuple(jax.ShapeDtypeStruct(s, F32) for s in shapes) + (jax.ShapeDtypeStruct(small.shape, F32),),
-        in_specs=[anywhere, anywhere, vmem],
-        out_specs=(vmem,) * 3,
-        scratch_shapes=buffers + [
-            pltpu.VMEM((nmode,) + small.shape, F32), pltpu.VMEM((ndp,) + small.shape, F32),
-            sem(2), sem(2, group), sem(2, count_v), sem(2, count_u), sem(2, na - 1), sem(2, 4),
+        functools.partial(tail_kernel, n, L, D, slots, owner_list.shape[0]),
+        out_shape=(
+            jax.ShapeDtypeStruct(shapes[0], F32), jax.ShapeDtypeStruct(shapes[1], F32), jax.ShapeDtypeStruct((32, 128), F32),
+            jax.ShapeDtypeStruct((n * L, D), F32),
+        ),
+        in_specs=[pl.BlockSpec(memory_space=pltpu.SMEM)] + [anywhere] * 8 + [
+            vmem, pl.BlockSpec(memory_space=pltpu.VMEM), vmem, vmem, vmem],
+        out_specs=(vmem, vmem, vmem, anywhere),
+        scratch_shapes=[
+            pltpu.VMEM((n * L, D), BF),
+            pltpu.VMEM(z.shape, BF),
+            pltpu.VMEM((n * L, D), BF),
+            pltpu.VMEM((n * L, D), F32),
+            pltpu.VMEM(weights.shape, BF),
+            pltpu.VMEM((D // 128, total + 8, 128), F32),
+            pltpu.VMEM((8, slots * n, 128), F32),
+            pltpu.VMEM((n * L, D), BF),
+            pltpu.VMEM((8, D), F32),
+            pltpu.VMEM((D // 128, 80, 128), F32),
+            pltpu.VMEM((nd, shard_rows, D), BF),
+        ] + [pltpu.VMEM((count,) + s, BF) for count in counts for s in shapes] + [
+            pltpu.VMEM((nmode, 32, 128), F32), pltpu.VMEM((ndp, 32, 128), F32),
+            sem(18), sem(2, 4), sem(2, counts[0]), sem(2, counts[1]), sem(2, counts[2]), sem(2, counts[3]),
             sem(ndp + nmode - 2), sem(ndp + nmode - 2),
         ],
-        compiler_params=pltpu.CompilerParams(collective_id=1, has_side_effects=True, vmem_limit_bytes=60 * 1024 * 1024),
-        name="reduce_scatter",
-    )(dense.reshape((group, 2) + shapes[0]), mixer.reshape((group, 2) + shapes[1]), small)
+        compiler_params=pltpu.CompilerParams(collective_id=1, has_side_effects=True, vmem_limit_bytes=62 * 1024 * 1024),
+        name="tail",
+    )(owner_list, gmix, z, acts, gsum, weights, gout, gup, gdn, observed, wqo[:D], basist, jnp.eye(L, dtype=F32), sums)
 
 
 def fourier_tables(mode_index, length):
@@ -988,20 +1036,9 @@
         small_master[2 * width :], acts.reshape(inputs.shape), sig.reshape(inputs.shape), out_grad, wqo, wup, wdn,
         small_master[None, width : 2 * width], inv,
     )
-    input_grad, g_query, sum_query, g_mixer = back(
-        grad_mixed.reshape(-1, width), spectra, acts, grad_summed.reshape(-1, width), observed, wqo, basis.T, weights
-    )
-    small_grad = jnp.concatenate(
-        [
-            jnp.sum(sum_query, axis=0).reshape(-1, 128),
-            jnp.sum(sums[:8], axis=0).reshape(-1, 128),
-            jnp.sum(sums[8:, :128].reshape(20, 8, 128), axis=1),
-            jnp.zeros((4, 128), F32),
-        ]
-    )
-    dense_grad = to_owners((g_query, g_out, g_up, g_down), owner_list)
-    dense_mine, mixer_mine, small_all = reduce_scatter(
-        dense_grad.reshape((ndp * nmode,) + dense_master.shape), g_mixer.reshape((ndp * nmode,) + g_mixer.shape[2:]), small_grad
+    dense_mine, mixer_mine, small_all, input_grad = tail(
+        grad_mixed.reshape(-1, width), spectra, acts, grad_summed.reshape(-1, width), observed, wqo, basis.T, weights,
+        g_out, g_up, g_down, sums, owner_list, dense_master.shape[0],
     )
     small_total = jnp.concatenate([small_all[:8].reshape(-1), jnp.sum(small_all[8:28], axis=1)])
     dense_first_new, dense_second_new, dense_new = adam_update(

time: 356 us -> 309 us (0.87)
  Pallas kernels: 325 us -> 283 us
    pallas_call x3 -> x1, Pallas kernels: 130 us -> 95.1 us  [tail(): pl.pallas_call(functools.partial(tail_kernel, n, L, D, slots, owner_list....]
    pallas_call x1, Pallas kernels: 31.6 us -> 24.7 us  [front(): pl.pallas_call(functools.partial(front_kernel, n, L, D, slots), grid=(1,)...]
    unnamed x46 -> x37, local copies, waits for them, and re-layouts: 12.6 us -> 8.52 us
where the time goes in v2:
time: 309 us; the launch traced here: 308 us
  Pallas kernels  283 us (92%)
  local copies, waits for them, and re-layouts  14 us (5%)
  other arithmetic  10.9 us (4%)
    pallas_call x1, Pallas kernels, tail(): pl.pallas_call(functools.partial(tail_kernel, n, L, D, slots, owner_list....  95.1 us
    pallas_call x1, Pallas kernels, middle(): pl.pallas_call(functools.partial(middle_kernel, W, L, D, FF, steps), grid...  93.7 us
    pallas_call x1, Pallas kernels, gather(): pl.pallas_call(gather_kernel, out_shape=tuple((jax.ShapeDtypeStruct((nd,)...  62.3 us
    pallas_call x1, Pallas kernels, front(): pl.pallas_call(functools.partial(front_kernel, n, L, D, slots), grid=(1,)...  24.7 us
    unnamed x37, local copies, waits for them, and re-layouts  8.52 us
    pallas_call x1, Pallas kernels, to_table(): pl.pallas_call(functools.partial(table_kernel, blocks), grid_spec=pltpu.P...  6.92 us

profile of v2, /device:TPU:0, one launch (start us, length us, event | category | flops | bytes accessed | tf_op | source)
XLA Modules:
  0.0 308.5 jit_solution(7482300068110682224)
XLA Ops:
  0.6 1.7 convert_element_type.52
  2.4 1.7 convert_element_type.51.refs_0_
  4.0 62.3 %gather.1 = (bf16[32,160,512]{2,1,0:T(8,128)(2,1)}, bf16[32,768,128]{2,1,0:T(8,128)(2,1)}) custom-call(bf16[160,512]{1,0:T(8,128)(2,1)} %convert_element_type.51.refs_0_, bf16[768,128]{1,0:T(8,128)(2,1)} %bitcast.32), custom_call_target="tpu_custom_call" | custom-call | tf_op jit(solution)/shard_map/gather/pallas_call | solution.py:610
  66.4 0.0 copy-start.2
  66.4 2.5 copy-done.2
  68.9 0.7 copy-done.5
  69.6 6.9 %to_table.1 = (bf16[1024,512]{1,0:T(8,128)(2,1)S(1)}, bf16[2048,512]{1,0:T(8,128)(2,1)S(1)}, bf16[2048,512]{1,0:T(8,128)(2,1)S(1)}) custom-call(s32[256]{0:T(256)S(1)} %copy-done.5, bf16[5120,512]{1,0:T(8,128)(2,1)S(1)} %bitcast.23), custom_call_target="tpu_custom_call" | custom-call | tf_op jit(solution)/shard_map/to_table/pallas_call | solution.py:451
  76.5 0.0 copy-start
  76.5 0.9 copy-done
  77.4 1.3 copy-done.3
  78.7 1.4 copy-done.4
  80.1 0.1 multiply_convert_fusion.1
  80.3 0.0 copy-start.12
  80.3 0.7 copy.31.inv_ref
  81.0 0.0 copy-done.17
  81.0 0.2 cosine_convert_fusion
  81.2 0.6 pad_maximum_fusion
  81.8 0.6 fusion.2.eye_ref
  82.4 0.0 copy-done.14
  82.4 0.6 fusion.21
  83.0 24.7 %front.1 = (bf16[1536,512]{1,0:T(8,128)(2,1)}, bf16[8,1536,64]{2,1,0:T(8,128)(2,1)}, bf16[1536,512]{1,0:T(8,128)(2,1)}) custom-call(bf16[1536,512]{1,0:T(8,128)(2,1)} %bitcast.31, s32[16,96]{1,0:T(8,128)} %obs_ref.3, bf16[1024,512]{1,0:T(8,128)(2,1)} %copy-done, f32[1,512]{1,0:T(1,128)} %bitcast.40, bf16[96,96]{1,0:T(8,128)(2,1)} %bitcast.36, ...), custom_call_target="tpu_custom_call" | custom-call | tf_op jit(solution)/shard_map/front/pallas_call | solution.py:400
  107.7 0.0 copy-done.12
  107.7 0.5 slice.25.mix_ref
  108.2 93.7 %middle.1 = (bf16[16,96,512]{2,1,0:T(8,128)(2,1)}, f32[16,96,512]{2,1,0:T(8,128)}, bf16[16,96,512]{2,1,0:T(8,128)(2,1)}, f32[512,512]{1,0:T(8,128)}, f32[2048,51...) custom-call(f32[20]{0:T(128)} %slice.25.mix_ref, bf16[16,96,512]{2,1,0:T(8,128)(2,1)} %bitcast.26, ...), custom_call_target="tpu_custom_call" | custom-call | tf_op jit(solution)/shard_map/middle/pallas_call | solution.py:264
  202.0 0.0 copy-done.1
  202.0 0.8 slice.28.wq_ref
  202.8 0.0 copy-done.13
  202.8 0.7 copy.32
  203.6 0.0 copy-start.10
  203.6 0.0 copy-start.8
  203.6 0.0 copy-start.11
  203.6 95.1 %tail.1 = (f32[160,512]{1,0:T(8,128)}, f32[768,128]{1,0:T(8,128)}, f32[32,128]{1,0:T(8,128)}, f32[1536,512]{1,0:T(8,128)}) custom-call(s32[256]{0:T(256)} %owner.3, bf16[1536,512]{1,0:T(8,128)(2,1)} %bitcast.29, bf16[8,1536,64]{2,1,0:T(8,128)(2,1)} %get-tuple-element.40.z_h, bf16[1536,512]{1,0:T(8,128)(2,1)} %get-tuple-element.34.acts_h, ...), custom_call_target="tpu_custom_call" | custom-call | tf_op jit(solution)/shard_map/tail/pallas_call | solution.py:951
  298.7 0.0 copy-start.6
  298.7 0.8 slice_bitcast_fusion
  299.6 0.9 slice_reduce_fusion
  300.5 0.0 copy-done.15
  300.5 0.0 copy-done.16
  300.5 0.6 multiply_subtract_fusion.2
  301.1 0.0 copy-done.7
  301.1 0.0 copy-done.9
  301.1 0.0 copy-done.10
  301.1 2.2 multiply_subtract_fusion
  303.3 0.0 copy-done.8
  303.3 0.0 copy-done.11
  303.3 2.2 multiply_subtract_fusion.1
  305.5 1.3 slice_bitcast_fusion.1
  306.8 0.0 copy-done.6
  306.8 1.7 copy.34
  (13 shorter events, 0.0 us)
Async XLA Ops:
  2.4 78.6 %copy-start.17 = (s32[48]{0:T(128)S(1)}, s32[48]{0:T(128)}, u32[]{:S(2)}) copy-start(s32[48]{0:T(128)} %param.19) | copy-start | bytes 580
  2.4 80.1 %copy-start.14 = (f32[1044]{0:T(1024)S(1)}, f32[1044]{0:T(1024)}, u32[]{:S(2)}) copy-start(f32[1044]{0:T(1024)} %param.27) | copy-start | bytes 12532
  66.4 2.5 copy-start.2
  68.9 0.7 copy-start.5
  76.5 1.0 copy-start
  77.4 1.3 copy-start.3
  78.7 1.4 copy-start.4
  80.3 27.5 %copy-start.12 = (bf16[2,48,96]{2,1,0:T(8,128)(2,1)}, bf16[2,48,96]{2,1,0:T(8,128)(2,1)S(1)}, u32[]{:S(2)}) copy-start(bf16[2,48,96]{2,1,0:T(8,128)(2,1)S(1)} %pad_maximum_fusion.1) | copy-start | bytes 55300
  108.2 93.7 %copy-start.1 = (bf16[1024,512]{1,0:T(8,128)(2,1)S(1)}, bf16[1024,512]{1,0:T(8,128)(2,1)}, u32[]{:S(2)}) copy-start(bf16[1024,512]{1,0:T(8,128)(2,1)} %copy-done) | copy-start | bytes 3145732
  108.2 94.6 %copy-start.13 = (bf16[2,48,96]{2,1,0:T(8,128)(2,1)S(1)}, bf16[2,48,96]{2,1,0:T(8,128)(2,1)}, u32[]{:S(2)}) copy-start(bf16[2,48,96]{2,1,0:T(8,128)(2,1)} %pad_maximum_fusion) | copy-start | bytes 55300
  203.5 96.9 %copy-start.15 = (f32[1044]{0:T(1024)S(1)}, f32[1044]{0:T(1024)}, u32[]{:S(2)}) copy-start(f32[1044]{0:T(1024)} %param.29) | copy-start | bytes 12532
  203.5 97.0 %copy-start.16 = (f32[1044]{0:T(1024)S(1)}, f32[1044]{0:T(1024)}, u32[]{:S(2)}) copy-start(f32[1044]{0:T(1024)} %param.28) | copy-start | bytes 12532
  203.5 97.6 %copy-start.7 = (f32[12,64,128]{2,1,0:T(8,128)S(1)}, f32[12,64,128]{2,1,0:T(8,128)}, u32[]{:S(2)}) copy-start(f32[12,64,128]{2,1,0:T(8,128)} %param.24) | copy-start | bytes 1179652
  203.5 97.6 %copy-start.9 = (f32[12,64,128]{2,1,0:T(8,128)S(1)}, f32[12,64,128]{2,1,0:T(8,128)}, u32[]{:S(2)}) copy-start(f32[12,64,128]{2,1,0:T(8,128)} %param.26) | copy-start | bytes 1179652
  203.6 97.6 %copy-start.10 = (f32[12,64,128]{2,1,0:T(8,128)S(1)}, f32[12,64,128]{2,1,0:T(8,128)}, u32[]{:S(2)}) copy-start(f32[12,64,128]{2,1,0:T(8,128)} %param.25) | copy-start | bytes 1179652
  203.6 99.8 %copy-start.8 = (f32[160,512]{1,0:T(8,128)S(1)}, f32[160,512]{1,0:T(8,128)}, u32[]{:S(2)}) copy-start(f32[160,512]{1,0:T(8,128)} %param.21) | copy-start | bytes 983044
  203.6 99.8 %copy-start.11 = (f32[160,512]{1,0:T(8,128)S(1)}, f32[160,512]{1,0:T(8,128)}, u32[]{:S(2)}) copy-start(f32[160,512]{1,0:T(8,128)} %param.23) | copy-start | bytes 983044
  298.7 8.1 %copy-start.6 = (f32[1536,512]{1,0:T(8,128)S(1)}, f32[1536,512]{1,0:T(8,128)}, u32[]{:S(2)}) copy-start(f32[1536,512]{1,0:T(8,128)} %get-tuple-element.46) | copy-start | bytes 9437188

commit v3 on v2

--- a/solution.py
+++ b/solution.py
@@ -304,9 +304,6 @@
     )(mix, acts, sig, og, wqo, wup, wdn, bias, inv.T, cnt, cntt)
 
 
-UNROLL = 4
-
-
 def sign_lanes(rows, left, right):
     lane = lax.broadcasted_iota(jnp.int32, (rows, 128), 1)
     return jnp.where(lane < 64, left, right).astype(F32)
@@ -344,146 +341,7 @@
     return jnp.concatenate([weights[h * pieces + q, mode, rows, :] for q in range(pieces)], 0)
 
 
-def front_kernel(n, L, D, slots, in_ref, obs_ref, wq_ref, bias_ref, basis_ref, inv_ref, eye_ref, weights,
-                 acts_ref, z_ref, sig_ref, query, tiles, outs):
-    ndp, nmode = weights.shape[:2]
-    per = slots // nmode
-    heads = 8
-    pieces = ndp // heads
-    depth = 64 // pieces
-
-    def mask(w, _):
-        row = obs_ref[pl.ds(w, 1), :].astype(F32)
-        rows = pl.ds(pl.multiple_of(w * L, 32), L)
-        acts_ref[rows, :] = dot((eye_ref[...] * row).astype(BF), in_ref[rows, :]).astype(BF)
-        return 0
-    lax.fori_loop(0, n, mask, 0)
-    T = 384
-
-    def project(i, _):
-        rows = pl.ds(pl.multiple_of(i * T, T), T)
-        query[rows, :] = (dot(acts_ref[rows, :], wq_ref[...]) + bias_ref[...]).astype(BF)
-        return 0
-    lax.fori_loop(0, n * L // T, project, 0)
-
-    def spectra(w, _):
-        rows = pl.ds(pl.multiple_of(w * L, 32), L)
-        spread_rows(tiles, w, slots, n, dot(basis_ref[...], query[rows, :]))
-        return 0
-    lax.fori_loop(0, n, spectra, 0)
-
-    for mode in range(nmode):
-        def slot(jl, _):
-            at = pl.ds(pl.multiple_of((mode * per + jl) * n, n), n)
-            rows = pl.ds(pl.multiple_of(jl * depth, depth), depth)
-            for h in range(heads):
-                x = tiles[h, at, :]
-                both = jnp.concatenate([x, swap_halves(x)], 0)[:, :64].astype(BF)
-                z_ref[h, pl.ds(pl.multiple_of((mode * per + jl) * 2 * n, 2 * n), 2 * n), :] = both
-                y = dot(both, head_weights(weights, h, pieces, mode, rows))
-                outs[h, at, :] = y[:n] + swap_halves(y[n:]) * sign_lanes(n, -1.0, 1.0)
-            return 0
-        lax.fori_loop(0, per, slot, 0, unroll=UNROLL)
-
-    def signal(w, _):
-        rows = pl.ds(pl.multiple_of(w * L, 32), L)
-        sig_ref[rows, :] = dot(inv_ref[...], gather_rows(outs, w, slots, n)).astype(BF)
-        return 0
-    lax.fori_loop(0, n, signal, 0)
-
-
-def front(inputs, observed, wqo, bias, basis, inv, weights):
-    n, L, D = inputs.shape
-    slots = basis.shape[0] // 2
-    vm = pl.BlockSpec(memory_space=pltpu.VMEM)
-    whole = lambda *s: pl.BlockSpec(s, lambda i: (0,) * len(s), pipeline_mode=pl.Buffered(1))
-    return pl.pallas_call(
-        functools.partial(front_kernel, n, L, D, slots),
-        grid=(1,),
-        out_shape=(
-            jax.ShapeDtypeStruct((n * L, D), BF),
-            jax.ShapeDtypeStruct((8, 2 * slots * n, 64), BF),
-            jax.ShapeDtypeStruct((n * L, D), BF),
-        ),
-        in_specs=[whole(n * L, D), whole(n, L), whole(D, D), whole(1, D), whole(2 * slots, L), whole(L, 2 * slots), whole(L, L),
-                  whole(*weights.shape)],
-        out_specs=(whole(n * L, D), whole(8, 2 * slots * n, 64), whole(n * L, D)),
-        scratch_shapes=[
-            pltpu.VMEM((n * L, D), BF),
-            pltpu.VMEM((8, slots * n, 128), F32),
-            pltpu.VMEM((8, slots * n, 128), F32),
-        ],
-        compiler_params=pltpu.CompilerParams(vmem_limit_bytes=60 * 1024 * 1024),
-        name="front",
-    )(inputs.reshape(n * L, D), observed, wqo, bias, basis, inv, jnp.eye(L, dtype=F32), weights)
-
-
-def table_kernel(blocks, owner, in_ref, wqo_ref, wup_ref, wdn_ref, src, dst):
-    rows = in_ref.shape[0]
-    size = rows // blocks
-    step = 256
-
-    def widen(i, _):
-        at = pl.ds(pl.multiple_of(i * step, step), step)
-        src[at, :] = in_ref[at, :].astype(F32)
-        return 0
-    lax.fori_loop(0, rows // step, widen, 0)
-
-    def move(j, _):
-        dst[pl.ds(owner[j] * size, size), :] = src[pl.ds(j * size, size), :]
-        return 0
-    lax.fori_loop(0, blocks, move, 0, unroll=4)
-    start = 0
-    for ref in (wqo_ref, wup_ref, wdn_ref):
-        def narrow(i, _):
-            to = pl.ds(pl.multiple_of(i * step, step), step)
-            at = pl.ds(pl.multiple_of(start + i * step, step), step)
-            ref[to, :] = dst[at, :].astype(BF)
-            return 0
-        lax.fori_loop(0, ref.shape[0] // step, narrow, 0)
-        start += ref.shape[0]
-
-
-def to_table(gathered, owner_list, ff):
-    rows, D = gathered.shape
-    blocks = owner_list.shape[0]
-    cols = lambda r: pl.BlockSpec((r, 128), lambda i, o: (0, i))
-    return pl.pallas_call(
-        functools.partial(table_kernel, blocks),
-        grid_spec=pltpu.PrefetchScalarGridSpec(
-            num_scalar_prefetch=1,
-            grid=(D // 128,),
-            in_specs=[cols(rows)],
-            out_specs=(cols(2 * D), cols(ff), cols(ff)),
-            scratch_shapes=[pltpu.VMEM((rows + 8, 128), F32), pltpu.VMEM((rows + 8, 128), F32)],
-        ),
-        out_shape=(
-            jax.ShapeDtypeStruct((2 * D, D), BF),
-            jax.ShapeDtypeStruct((ff, D), BF),
-            jax.ShapeDtypeStruct((ff, D), BF),
-        ),
-        compiler_params=pltpu.CompilerParams(vmem_limit_bytes=40 * 1024 * 1024),
-        name="to_table",
-    )(owner_list, gathered)
-
-
 MESH = pl.DeviceIdType.MESH
-
-
-def places():
-    ndp, nmode = lax.axis_size("dp"), lax.axis_size("mode")
-    sizes = {"a": ndp // 2, "b": 2, "y": nmode // 2, "c": 2}
-    dp, mode = lax.axis_index("dp"), lax.axis_index("mode")
-    here = {"a": dp // 2, "b": lax.rem(dp, 2), "y": mode // 2, "c": lax.rem(mode, 2)}
-    return sizes, here
-
-
-def number(sizes, at):
-    return ((at["a"] * sizes["b"] + at["b"]) * sizes["y"] + at["y"]) * 2 + at["c"]
-
-
-def device(sizes, at):
-    return {"dp": at["a"] * sizes["b"] + at["b"], "mode": at["y"] * 2 + at["c"]}
 
 
 def move(sizes, at, axis, d):
@@ -520,102 +378,6 @@
     for t in range(count, count + k - 1):
         for s in range(t - count + 1, k):
             stages[s](t - s)
-
-
-def gather_kernel(*refs):
-    kinds = 2
-    ins, outs = refs[:kinds], refs[kinds:2 * kinds]
-    recv, send, local = refs[2 * kinds:]
-    sizes, here = places()
-    greet()
-
-    def copy(kind, at, to, stage, own=False):
-        n = number(sizes, at)
-        return pltpu.make_async_remote_copy(
-            src_ref=ins[kind] if own else outs[kind].at[n], dst_ref=outs[kind].at[n],
-            send_sem=send.at[kind, stage], recv_sem=recv.at[kind, n],
-            device_id=device(sizes, to), device_id_type=MESH)
-
-    def arrived(kind, at):
-        copy(kind, at, here, 0).wait_recv()
-
-    def drain(kind, stage, count):
-        ref = outs[kind].at[pl.ds(0, count)]
-        pltpu.make_async_copy(ref, ref, send.at[kind, stage]).wait()
-
-    mine = [pltpu.make_async_copy(ins[k], outs[k].at[number(sizes, here)], local.at[k]) for k in range(kinds)]
-    for c in mine:
-        c.start()
-
-    def run(u, v):
-        na, nu, nv = sizes["a"], sizes[u], sizes[v]
-
-        def onward(kind, at, axes, own=False):
-            for axis, stage in axes:
-                for d in range(1, sizes[axis]):
-                    copy(kind, at, move(sizes, here, axis, d), stage, own).start()
-
-        for kind in range(kinds):
-            onward(kind, here, (("a", 0), (u, 1), (v, 2), ("c", 3)), True)
-
-        def line(t):
-            at = move(sizes, here, "a", t + 1)
-            for kind in range(kinds):
-                arrived(kind, at)
-                onward(kind, at, ((u, 1), (v, 2), ("c", 3)))
-
-        def second(t):
-            for d in range(1, nu):
-                at = move(sizes, move(sizes, here, "a", t), u, d)
-                for kind in range(kinds):
-                    arrived(kind, at)
-                    onward(kind, at, ((v, 2), ("c", 3)))
-
-        def third(t):
-            for e in range(nu):
-                for d in range(1, nv):
-                    at = move(sizes, move(sizes, move(sizes, here, "a", t), u, e), v, d)
-                    for kind in range(kinds):
-                        arrived(kind, at)
-                        onward(kind, at, (("c", 3),))
-
-        second(0)
-        staggered(na - 1, line, lambda t: second(t + 1), third)
-        third(na - 1)
-        for kind in range(kinds):
-            drain(kind, 0, na - 1)
-            drain(kind, 1, na * (nu - 1))
-            drain(kind, 2, na * nu * (nv - 1))
-
-    pl.when(here["c"] == 0)(lambda: run("b", "y"))
-    pl.when(here["c"] == 1)(lambda: run("y", "b"))
-    group = sizes["a"] * sizes["b"] * sizes["y"]
-    other = move(sizes, here, "c", 1)
-
-    def partner(i, _):
-        for kind in range(kinds):
-            copy(kind, {"a": i // (sizes["b"] * sizes["y"]), "b": lax.rem(i // sizes["y"], sizes["b"]),
-                        "y": lax.rem(i, sizes["y"]), "c": other["c"]}, here, 0).wait_recv()
-        return 0
-    lax.fori_loop(0, group, partner, 0)
-    for kind in range(kinds):
-        drain(kind, 3, group)
-    for c in mine:
-        c.wait()
-
-
-def gather(dense, mixer):
-    nd = lax.axis_size("dp") * lax.axis_size("mode")
-    anywhere = pl.BlockSpec(memory_space=pl.ANY)
-    return pl.pallas_call(
-        gather_kernel,
-        out_shape=tuple(jax.ShapeDtypeStruct((nd,) + x.shape, x.dtype) for x in (dense, mixer)),
-        in_specs=[anywhere] * 2,
-        out_specs=(anywhere,) * 2,
-        scratch_shapes=[pltpu.SemaphoreType.DMA((2, nd)), pltpu.SemaphoreType.DMA((2, 4)), pltpu.SemaphoreType.DMA((2,))],
-        compiler_params=pltpu.CompilerParams(collective_id=0, has_side_effects=True),
-        name="gather",
-    )(dense, mixer)
 
 
 def roles():
@@ -979,6 +741,271 @@
     )(owner_list, gmix, z, acts, gsum, weights, gout, gup, gdn, observed, wqo[:D], basist, jnp.eye(L, dtype=F32), sums)
 
 
+def gatherer(sizes, here, slot_of, whole_of, send, send_a, recv):
+    na, nu, nv = sizes["a"], sizes["u"], sizes["v"]
+
+    def spot(at):
+        dp, mode = place_of(sizes, at)
+        return dp * sizes["v"] * 2 + mode
+
+    def copy(at, to, sem):
+        ref = slot_of(at)
+        return pltpu.make_async_remote_copy(
+            src_ref=ref, dst_ref=ref, send_sem=sem, recv_sem=recv.at[spot(at)],
+            device_id=device_of(sizes, to), device_id_type=MESH)
+
+    def onward(at, axes):
+        for axis, stage in axes:
+            for d in range(1, sizes[axis]):
+                copy(at, move(sizes, here, axis, d), send.at[stage]).start()
+        copy(at, partner_of(here), send.at[2]).start()
+
+    def hop(k, side):
+        first, to = here["a"] - side * k, here["a"] + side
+        there = (first >= 0) & (first < na) & (to >= 0) & (to < na)
+        way = 0 if side == 1 else 1
+        inside = lambda x: jnp.clip(x, 0, na - 1)
+        return there, lambda: copy({**here, "a": inside(first)}, {**here, "a": inside(to)}, send_a.at[way, k])
+
+    def hops(k, side):
+        there, make = hop(k, side)
+        pl.when(there)(lambda: make().start())
+
+    def arrived(at):
+        copy(at, here, send.at[0]).wait_recv()
+        return at
+
+    def lines(k, act):
+        for side in ((1, -1) if k else (1,)):
+            to = here["a"] - side * k
+            pl.when((to >= 0) & (to < na))(lambda side=side, to=to: act({**here, "a": to}, side))
+
+    def start():
+        for side in (1, -1):
+            hops(0, side)
+        onward(here, (("u", 0), ("v", 1)))
+
+    def line(k, then=lambda at: None):
+        def act(at, side):
+            arrived(at)
+            hops(k, side)
+            onward(at, (("u", 0), ("v", 1)))
+            then(at)
+        lines(k, act)
+
+    def second(k, then=lambda at: None):
+        def act(at, side):
+            for d in range(1, nu):
+                to = arrived(move(sizes, at, "u", d))
+                onward(to, (("v", 1),))
+                then(to)
+        lines(k, act)
+
+    def third(k, then=lambda at: None):
+        def act(at, side):
+            for e in range(nu):
+                for d in range(1, nv):
+                    to = arrived(move(sizes, move(sizes, at, "u", e), "v", d))
+                    onward(to, ())
+                    then(to)
+        lines(k, act)
+
+    def partner(t, then=lambda at: None):
+        other = partner_of(here)
+        for e in range(nu):
+            for d in range(nv):
+                then(arrived(move(sizes, move(sizes, move(sizes, other, "a", t), "u", e), "v", d)))
+
+    def drain():
+        for stage, count in ((0, na * (nu - 1)), (1, na * nu * (nv - 1)), (2, na * nu * nv)):
+            ref = whole_of(count)
+            pltpu.make_async_copy(ref, ref, send.at[stage]).wait()
+        for k in range(na):
+            for side in (1, -1):
+                there, make = hop(k, side)
+                pl.when(there)(lambda make=make: make().wait_send())
+
+    return start, line, second, third, partner, drain
+
+
+def head_kernel(n, L, D, slots, blocks, restore, in_h, dense_ref, mixer_ref, obs_ref, bias_ref, basis_ref, inv_ref, eye_ref,
+                acts_h, z_h, sig_h, wqo_h, wup_h, wdn_h, weights_h,
+                inputs, acts, query, tiles, z, sig, buf, src, table, mix, tmp,
+                loads, send, send_a, recv):
+    sizes, here = roles()
+    ndp, nmode = lax.axis_size("dp"), lax.axis_size("mode")
+    dp, mode = lax.axis_index("dp"), lax.axis_index("mode")
+    na = sizes["a"]
+    per = slots // nmode
+    heads = 8
+    pieces = ndp // heads
+    depth = 64 // pieces
+    rows = buf.shape[1]
+    total = buf.shape[0] * rows
+    size = total // blocks
+    join = 4
+    units = blocks // join
+
+    def load(i, a, b):
+        return pltpu.make_async_copy(a, b, loads.at[i])
+    load_in = load(0, in_h, inputs)
+    load_in.start()
+    buf[dp * nmode + mode] = dense_ref[...].astype(BF)
+    mix[dp, mode] = mixer_ref[...].astype(BF)
+    greet()
+
+    def buf_at(at):
+        p, m = place_of(sizes, at)
+        return buf.at[p * nmode + m]
+
+    start_d, line_d, second_d, third_d, partner_d, drain_d = gatherer(
+        sizes, here, buf_at, lambda count: buf.at[pl.ds(0, count)], send.at[0], send_a.at[0], recv.at[0])
+    mix_at = lambda at: mix.at[place_of(sizes, at)]
+
+    def mix_many(count):
+        if count % nmode == 0:
+            return mix.at[pl.ds(0, count // nmode)]
+        return mix.at[pl.ds(0, count), 0] if count <= ndp else mix.at[pl.ds(0, count // 2), pl.ds(0, 2)]
+    start_m, line_m, second_m, third_m, partner_m, drain_m = gatherer(
+        sizes, here, mix_at, mix_many, send.at[1], send_a.at[1], recv.at[1])
+    start_d()
+
+    def widen(at):
+        p, m = place_of(sizes, at)
+        k = p * nmode + m
+        for c in range(D // 128):
+            src[c, pl.ds(k * rows, rows), :] = buf[k, :, c * 128:(c + 1) * 128].astype(F32)
+    widen(here)
+    load_in.wait()
+
+    def mask(w):
+        row = obs_ref[pl.ds(w, 1), :].astype(F32)
+        part = pl.ds(pl.multiple_of(w * L, 32), L)
+        acts[part, :] = dot((eye_ref[...] * row).astype(BF), inputs[part, :]).astype(BF)
+    each(0, n, mask)
+    outs = [load(1, acts, acts_h)]
+    outs[0].start()
+    for k in range(na + 2):
+        if k < na - 1:
+            line_d(k + 1, widen)
+        if k < na:
+            second_d(k, widen)
+        if 1 <= k <= na:
+            third_d(k - 1, widen)
+        if k == 0:
+            start_m()
+        if 1 <= k < na:
+            line_m(k)
+        if 1 <= k <= na:
+            second_m(k - 1)
+        if 2 <= k <= na:
+            third_m(k - 2)
+    each(0, na, lambda t: partner_d(t, widen))
+
+    def pick(p):
+        for c in range(D // 128):
+            for i in range(join):
+                tmp[c, i * size:(i + 1) * size, :] = src[c, pl.ds(restore[p * join + i] * size, size), :]
+            part = pl.ds(pl.multiple_of(p * join * size, 16), join * size)
+            table[part, c * 128:(c + 1) * 128] = tmp[c].astype(BF)
+    early = -(-D // (join * size))
+    each(0, early, pick)
+    T = 384
+
+    def project(i):
+        part = pl.ds(pl.multiple_of(i * T, T), T)
+        query[part, :] = (dot(acts[part, :], table[0:D, :]) + bias_ref[...]).astype(BF)
+
+    def spectra(w):
+        part = pl.ds(pl.multiple_of(w * L, 32), L)
+        spread_rows(tiles, w, slots, n, dot(basis_ref[...], query[part, :]))
+
+    work = [lambda i=i: project(i) for i in range(n * L // T)]
+    work += [lambda i=i: each(i * n // 4, (i + 1) * n // 4, spectra) for i in range(4)]
+    cuts = [early + (units - early) * i // 4 for i in range(5)]
+    work += [lambda i=i: each(cuts[i], cuts[i + 1], pick) for i in range(4)]
+    for i, w in enumerate(work):
+        w()
+        if i == 1:
+            third_m(na - 1)
+    at = 0
+    for i, ref in enumerate((wqo_h, wup_h, wdn_h)):
+        outs.append(load(2 + i, table.at[pl.ds(at, ref.shape[0])], ref))
+        outs[-1].start()
+        at += ref.shape[0]
+    each(0, na, partner_m)
+    outs.append(load(5, mix, weights_h))
+    outs[-1].start()
+
+    def slot(j, _):
+        m, jl = j // per, lax.rem(j, per)
+        at = pl.ds(pl.multiple_of(j * n, n), n)
+        part = pl.ds(pl.multiple_of(jl * depth, depth), depth)
+        for h in range(heads):
+            x = tiles[h, at, :]
+            both = jnp.concatenate([x, swap_halves(x)], 0)[:, :64].astype(BF)
+            z[h, pl.ds(pl.multiple_of(j * 2 * n, 2 * n), 2 * n), :] = both
+            y = dot(both, head_weights(mix, h, pieces, m, part))
+            tiles[h, at, :] = y[:n] + swap_halves(y[n:]) * sign_lanes(n, -1.0, 1.0)
+        return 0
+    lax.fori_loop(0, slots, slot, 0, unroll=4)
+    outs.append(load(6, z, z_h))
+    outs[-1].start()
+
+    def signal(w):
+        part = pl.ds(pl.multiple_of(w * L, 32), L)
+        sig[part, :] = dot(inv_ref[...], gather_rows(tiles, w, slots, n)).astype(BF)
+    each(0, n, signal)
+    outs.append(load(7, sig, sig_h))
+    outs[-1].start()
+    drain_d()
+    drain_m()
+    for o in outs:
+        o.wait()
+
+
+def head(inputs, observed, dense, mixer, restore, bias, basis, inv, ff):
+    n, L, D = inputs.shape
+    slots = basis.shape[0] // 2
+    ndp, nmode = lax.axis_size("dp"), lax.axis_size("mode")
+    nd = ndp * nmode
+    rows, mixer_rows = dense.shape[0], mixer.shape[0]
+    anywhere = pl.BlockSpec(memory_space=pl.ANY)
+    vmem = pl.BlockSpec(memory_space=pltpu.VMEM)
+    sem = lambda *s: pltpu.SemaphoreType.DMA(s)
+    tokens = n * L
+    return pl.pallas_call(
+        functools.partial(head_kernel, n, L, D, slots, restore.shape[0]),
+        out_shape=(
+            jax.ShapeDtypeStruct((tokens, D), BF),
+            jax.ShapeDtypeStruct((8, 2 * slots * n, 64), BF),
+            jax.ShapeDtypeStruct((tokens, D), BF),
+            jax.ShapeDtypeStruct((2 * D, D), BF),
+            jax.ShapeDtypeStruct((ff, D), BF),
+            jax.ShapeDtypeStruct((ff, D), BF),
+            jax.ShapeDtypeStruct((ndp, nmode, mixer_rows, 128), BF),
+        ),
+        in_specs=[pl.BlockSpec(memory_space=pltpu.SMEM), anywhere] + [vmem] * 7,
+        out_specs=(anywhere,) * 7,
+        scratch_shapes=[
+            pltpu.VMEM((tokens, D), BF),
+            pltpu.VMEM((tokens, D), BF),
+            pltpu.VMEM((tokens, D), BF),
+            pltpu.VMEM((8, slots * n, 128), F32),
+            pltpu.VMEM((8, 2 * slots * n, 64), BF),
+            pltpu.VMEM((tokens, D), BF),
+            pltpu.VMEM((nd, rows, D), BF),
+            pltpu.VMEM((D // 128, nd * rows + 8, 128), F32),
+            pltpu.VMEM((nd * rows, D), BF),
+            pltpu.VMEM((ndp, nmode, mixer_rows, 128), BF),
+            pltpu.VMEM((D // 128, 4 * (nd * rows // restore.shape[0]), 128), F32),
+            sem(8), sem(2, 3), sem(2, 2, ndp // (nmode // 2)), sem(2, nd),
+        ],
+        compiler_params=pltpu.CompilerParams(collective_id=0, has_side_effects=True, vmem_limit_bytes=62 * 1024 * 1024),
+        name="head",
+    )(restore, inputs.reshape(tokens, D), dense, mixer, observed, bias, basis, inv, jnp.eye(L, dtype=F32))
+
+
 def fourier_tables(mode_index, length):
     positions = jnp.arange(length, dtype=jnp.int32)
     phases = mode_index[:, None] * positions[None, :] % length
@@ -1025,13 +1052,15 @@
     length, width = inputs.shape[1:]
     slots = mode_index.shape[0]
     hidden = (dense_master.shape[0] * ndp * nmode - 2 * width) // 2
-    dense_all, mixer_all = gather(dense_master.astype(BF), mixer_master.astype(BF).reshape(-1, mixer_master.shape[2]))
-    weights = mixer_all.reshape((ndp, nmode) + mixer_all.shape[1:])
     forward, inverse = fourier_tables(mode_index, length)
     basis = forward.astype(BF).reshape(2 * slots, length)
     inv = inverse.astype(BF).reshape(length, 2 * slots)
-    wqo, wup, wdn = to_table(dense_all.reshape(-1, width), owner_list, hidden)
-    acts, spectra, sig = front(inputs, observed, wqo, small_master[None, :width], basis, inv, weights)
+    places = jnp.arange(owner_list.shape[0], dtype=jnp.int32)
+    restore = jnp.sum(jnp.where(owner_list[None, :] == places[:, None], places[None, :], 0), axis=1)
+    acts, spectra, sig, wqo, wup, wdn, weights = head(
+        inputs, observed, dense_master, mixer_master.reshape(-1, mixer_master.shape[2]), restore, small_master[None, :width],
+        basis, inv, hidden,
+    )
     output, grad_summed, grad_mixed, g_out, g_up, g_down, sums = middle(
         small_master[2 * width :], acts.reshape(inputs.shape), sig.reshape(inputs.shape), out_grad, wqo, wup, wdn,
         small_master[None, width : 2 * width], inv,

time: 309 us -> 270 us (0.87)
  Pallas kernels: 283 us -> 251 us
  local copies, waits for them, and re-layouts: 14 us -> 7.86 us
    pallas_call x3 -> x1, Pallas kernels: 94 us -> 74.9 us  [head(): pl.pallas_call(functools.partial(head_kernel, n, L, D, slots, restore.sha...]
    pallas_call x1, Pallas kernels: 95.1 us -> 82.8 us  [tail(): pl.pallas_call(functools.partial(tail_kernel, n, L, D, slots, owner_list....]
    unnamed x37 -> x29, local copies, waits for them, and re-layouts: 8.52 us -> 1.73 us
    convert_element_type x3 -> x1, other arithmetic: 4.02 us -> 0.63 us  [head(): jnp.eye(L, dtype=F32)]
where the time goes in v3:
time: 270 us; the launch traced here: 269 us
  Pallas kernels  251 us (93%)
  other arithmetic  8.49 us (3%)
  local copies, waits for them, and re-layouts  7.86 us (3%)
    pallas_call x1, Pallas kernels, middle(): pl.pallas_call(functools.partial(middle_kernel, W, L, D, FF, steps), grid...  93.7 us
    pallas_call x1, Pallas kernels, tail(): pl.pallas_call(functools.partial(tail_kernel, n, L, D, slots, owner_list....  82.8 us
    pallas_call x1, Pallas kernels, head(): pl.pallas_call(functools.partial(head_kernel, n, L, D, slots, restore.sha...  74.9 us

profile of v3, /device:TPU:0, one launch (start us, length us, event | category | flops | bytes accessed | tf_op | source)
XLA Modules:
  0.0 268.6 jit_solution(1741541701293781455)
XLA Ops:
  0.6 0.0 copy-start.11
  0.7 0.1 multiply_convert_fusion.1
  0.8 0.0 copy-start.10
  0.8 0.7 copy.33.inv_ref
  1.5 0.8 cosine_convert_fusion
  2.4 0.6 pad_maximum_fusion
  3.0 0.6 fusion.2.eye_ref
  3.6 1.3 fusion.21
  5.0 1.4 select_reduce_fusion.restore
  6.3 74.9 %head.1 = (bf16[1536,512]{1,0:T(8,128)(2,1)}, bf16[8,1536,64]{2,1,0:T(8,128)(2,1)}, bf16[1536,512]{1,0:T(8,128)(2,1)}, bf16[1024,512]{1,0:T(8,128)(2,1)}, bf16[2...) custom-call(s32[256]{0:T(256)} %select_reduce_fusion.restore, ...), custom_call_target="tpu_custom_call" | custom-call | tf_op jit(solution)/shard_map/head/pallas_call | solution.py:977
  81.3 0.0 copy-done.11
  81.3 0.5 slice.25.mix_ref
  81.8 0.0 copy-done.10
  81.8 0.0 copy-start.1
  81.8 0.0 copy-start.9
  81.8 93.7 %middle.1 = (bf16[16,96,512]{2,1,0:T(8,128)(2,1)}, f32[16,96,512]{2,1,0:T(8,128)}, bf16[16,96,512]{2,1,0:T(8,128)(2,1)}, f32[512,512]{1,0:T(8,128)}, f32[2048,51...) custom-call(f32[20]{0:T(128)} %slice.25.mix_ref, bf16[16,96,512]{2,1,0:T(8,128)(2,1)} %bitcast.21, ...), custom_call_target="tpu_custom_call" | custom-call | tf_op jit(solution)/shard_map/middle/pallas_call | solution.py:264
  175.5 0.0 copy-done.1
  175.5 0.8 slice.28.wq_ref
  176.4 0.0 copy-done.9
  176.4 0.7 copy.34
  177.1 0.0 copy-start.12
  177.1 0.0 copy-start.13
  177.1 0.0 copy-start.2
  177.1 0.0 copy-start.4
  177.1 0.0 copy-start.5
  177.1 82.8 %tail.1 = (f32[160,512]{1,0:T(8,128)}, f32[768,128]{1,0:T(8,128)}, f32[32,128]{1,0:T(8,128)}, f32[1536,512]{1,0:T(8,128)}) custom-call(s32[256]{0:T(256)} %owner.1, bf16[1536,512]{1,0:T(8,128)(2,1)} %bitcast.24, bf16[8,1536,64]{2,1,0:T(8,128)(2,1)} %get-tuple-element.37.z_h, bf16[1536,512]{1,0:T(8,128)(2,1)} %get-tuple-element.30.acts_h, ...), custom_call_target="tpu_custom_call" | custom-call | tf_op jit(solution)/shard_map/tail/pallas_call | solution.py:713
  259.9 0.0 copy-start.3
  259.9 0.0 copy-start.6
  259.9 0.0 copy-start.7
  260.0 0.0 copy-start.8
  260.0 0.8 slice_bitcast_fusion
  260.7 0.8 slice_reduce_fusion
  261.6 0.0 copy-done.12
  261.6 0.0 copy-done.13
  261.6 0.6 multiply_subtract_fusion.2
  262.2 0.0 copy-done.2
  262.2 0.0 copy-done.4
  262.2 0.0 copy-done.5
  262.2 0.0 copy-start
  262.2 2.3 multiply_subtract_fusion
  264.6 0.0 copy-done.3
  264.6 0.0 copy-done.6
  264.6 0.0 copy-done.7
  264.6 0.0 copy-done.8
  264.6 1.1 multiply_subtract_fusion.1
  265.7 1.3 slice_bitcast_fusion.1
  267.0 0.0 copy-done
  267.0 1.7 copy.36
  (2 shorter events, 0.0 us)
Async XLA Ops:
  0.6 80.6 %copy-start.11 = (f32[1044]{0:T(1024)S(1)}, f32[1044]{0:T(1024)}, u32[]{:S(2)}) copy-start(f32[1044]{0:T(1024)} %param.27) | copy-start | bytes 12532
  0.8 81.0 %copy-start.10 = (bf16[2,48,96]{2,1,0:T(8,128)(2,1)}, bf16[2,48,96]{2,1,0:T(8,128)(2,1)S(1)}, u32[]{:S(2)}) copy-start(bf16[2,48,96]{2,1,0:T(8,128)(2,1)S(1)} %pad_maximum_fusion.1) | copy-start | bytes 55300
  81.8 93.7 %copy-start.1 = (bf16[1024,512]{1,0:T(8,128)(2,1)S(1)}, bf16[1024,512]{1,0:T(8,128)(2,1)}, u32[]{:S(2)}) copy-start(bf16[1024,512]{1,0:T(8,128)(2,1)} %get-tuple-element.32.wq_ref) | copy-start | bytes 3145732
  81.8 94.6 %copy-start.9 = (bf16[2,48,96]{2,1,0:T(8,128)(2,1)S(1)}, bf16[2,48,96]{2,1,0:T(8,128)(2,1)}, u32[]{:S(2)}) copy-start(bf16[2,48,96]{2,1,0:T(8,128)(2,1)} %pad_maximum_fusion) | copy-start | bytes 55300
  177.1 84.5 %copy-start.12 = (f32[1044]{0:T(1024)S(1)}, f32[1044]{0:T(1024)}, u32[]{:S(2)}) copy-start(f32[1044]{0:T(1024)} %param.29) | copy-start | bytes 12532
  177.1 84.5 %copy-start.13 = (f32[1044]{0:T(1024)S(1)}, f32[1044]{0:T(1024)}, u32[]{:S(2)}) copy-start(f32[1044]{0:T(1024)} %param.28) | copy-start | bytes 12532
  177.1 85.1 %copy-start.2 = (f32[12,64,128]{2,1,0:T(8,128)S(1)}, f32[12,64,128]{2,1,0:T(8,128)}, u32[]{:S(2)}) copy-start(f32[12,64,128]{2,1,0:T(8,128)} %param.24) | copy-start | bytes 1179652
  177.1 85.1 %copy-start.4 = (f32[12,64,128]{2,1,0:T(8,128)S(1)}, f32[12,64,128]{2,1,0:T(8,128)}, u32[]{:S(2)}) copy-start(f32[12,64,128]{2,1,0:T(8,128)} %param.26) | copy-start | bytes 1179652
  177.1 85.1 %copy-start.5 = (f32[12,64,128]{2,1,0:T(8,128)S(1)}, f32[12,64,128]{2,1,0:T(8,128)}, u32[]{:S(2)}) copy-start(f32[12,64,128]{2,1,0:T(8,128)} %param.25) | copy-start | bytes 1179652
  259.9 4.7 %copy-start.3 = (f32[160,512]{1,0:T(8,128)S(1)}, f32[160,512]{1,0:T(8,128)}, u32[]{:S(2)}) copy-start(f32[160,512]{1,0:T(8,128)} %dense_ref.1) | copy-start | bytes 983044
  259.9 4.6 %copy-start.6 = (f32[160,512]{1,0:T(8,128)S(1)}, f32[160,512]{1,0:T(8,128)}, u32[]{:S(2)}) copy-start(f32[160,512]{1,0:T(8,128)} %param.23) | copy-start | bytes 983044
  259.9 4.6 %copy-start.7 = (f32[160,512]{1,0:T(8,128)S(1)}, f32[160,512]{1,0:T(8,128)}, u32[]{:S(2)}) copy-start(f32[160,512]{1,0:T(8,128)} %param.22) | copy-start | bytes 983044
  260.0 4.6 %copy-start.8 = (f32[160,512]{1,0:T(8,128)S(1)}, f32[160,512]{1,0:T(8,128)}, u32[]{:S(2)}) copy-start(f32[160,512]{1,0:T(8,128)} %get-tuple-element.45) | copy-start | bytes 983044
  262.2 4.7 %copy-start = (f32[1536,512]{1,0:T(8,128)S(1)}, f32[1536,512]{1,0:T(8,128)}, u32[]{:S(2)}) copy-start(f32[1536,512]{1,0:T(8,128)} %get-tuple-element.44) | copy-start | bytes 9437188

commit v4 on v3

--- a/solution.py
+++ b/solution.py
@@ -19,6 +19,7 @@
 RATE_SMALL = 0.5
 
 KERNEL_SIZES = (7, 12, 14, 24, 48)
+ODD = (7, 3, 7, 3, 3)
 LOG2E = 1.4426950408889634
 BF = jnp.bfloat16
 F32 = jnp.float32
@@ -36,7 +37,7 @@
     t = np.arange(length)
     for size in KERNEL_SIZES:
         u = np.clip(t[:, None] - (size - 1) // 2 + np.arange(size)[None, :], 0, length - 1)
-        tables.append((u[:, :, None] == t[None, None, :]).sum(1))
+        tables.append((u[:, :, None] == t[None, None, :]).sum(1) * (ODD[len(tables)] / size))
     return np.stack(tables).astype(np.float32)
 
 
@@ -53,7 +54,7 @@
 def middle_kernel(W, L, D, FF, steps,
                   mix_ref, acts_ref, sig_ref, og_ref, wq_ref, wup_ref, wdn_ref, bias_ref, invt_ref, cnt_ref, cntt_ref,
                   out_ref, gsum_ref, gmix_ref, gw_ref, gup_ref, gdn_ref, small_ref,
-                  vs, base, avg1, c1, v1, active, dgelu, first, flow, gb, ghid, glow, avg2, stk, accs, accb):
+                  vs, base, avg1, c1, v1, active, dgelu, first, flow, gb, ghid, glow, avg2, stk, accs, accb, hs, wg, wsem):
     step = pl.program_id(0)
     T = W * L
     CH = 16
@@ -69,8 +70,6 @@
         accs[...] = jnp.zeros_like(accs)
         accb[...] = jnp.zeros_like(accb)
         gw_ref[...] = jnp.zeros_like(gw_ref)
-        gup_ref[...] = jnp.zeros_like(gup_ref)
-        gdn_ref[...] = jnp.zeros_like(gdn_ref)
 
     def fold(x):
         y = x[:, 0:128]
@@ -79,152 +78,171 @@
         return y[0:8] + y[8:16]
 
     def scaled_shares(v, base_at):
-        logits = [mix_ref[base_at + k] * LOG2E * v + mix_ref[base_at + 5 + k] * LOG2E for k in range(5)]
-        top = functools.reduce(jnp.maximum, logits)
-        es = [jnp.exp2(l - top) for l in logits]
+        p = [mix_ref[2 * D + base_at + k] for k in range(10)]
+        logits = [((p[k] - p[4]) * LOG2E) * v + (p[5 + k] - p[9]) * LOG2E for k in range(4)]
+        top = jnp.maximum(functools.reduce(jnp.maximum, logits), 0.0)
+        es = [jnp.exp2(l - top) for l in logits] + [jnp.exp2(-top)]
         r = 1.0 / functools.reduce(lambda a, b: a + b, es)
-        return [e * (r * (1.0 / s)) for e, s in zip(es, KERNEL_SIZES)]
-
-    def backward(v, g, cs, avs, mean, base_at):
-        gv = g * v
+        scale = {7: r * (1.0 / 7.0), 3: r * (1.0 / 3.0)}
+        return [e * scale[o] for e, o in zip(es, ODD)]
+
+    def backward(v, g, cs, avs, mean, base_at, store):
+        means = {7: 7.0 * mean, 3: 3.0 * mean}
         total = None
         for k in range(5):
-            t = cs[k] * (KERNEL_SIZES[k] * mean - avs[k])
-            total = mix_ref[base_at + k] * t if total is None else total + mix_ref[base_at + k] * t
-            accs[base_at + k] += fold(gv * t)
-            accs[base_at + 5 + k] += fold(g * t)
-        return g, g * total
-
-    def split(v, w, rows, cols):
-        hi = v.astype(BF)
-        vs[w, rows, cols] = hi
-        return hi
+            cg = cs[k] * g
+            store(k, cg)
+            if k < 4:
+                t = cg * (means[ODD[k]] - avs[k])
+                term = (mix_ref[2 * D + base_at + k] - mix_ref[2 * D + base_at + 4]) * t
+                total = term if total is None else total + term
+                accs[base_at + k] += fold(t * v)
+                accs[base_at + 5 + k] += fold(t)
+        return total
 
     sig = sig_ref[...].reshape(T, D)
     base[...] = dot(sig, wq_ref[D:2 * D, :])
 
-    def window_one(w, _):
-        def rows_a(i, _):
+    def cut(w, source):
+        for i in range(nr):
             for c in range(nc):
                 cols = slice(c * CC, (c + 1) * CC)
-                rows = pl.ds(pl.multiple_of(w * L + i * CH, CH), CH)
-                here = pl.ds(pl.multiple_of(i * CH, CH), CH)
-                low_rows = pl.ds(pl.multiple_of(L + i * CH, CH), CH)
-                v = base[rows, cols] + acts_ref[w, here, cols].astype(F32) + bias_ref[:, cols]
-                v1[rows, cols] = v
+                v = source(w, i, cols)
                 hi = v.astype(BF)
-                vs[here, cols] = hi
-                vs[low_rows, cols] = (v - hi.astype(F32)).astype(BF)
-            return 0
-        lax.fori_loop(0, nr, rows_a, 0)
-        avg1[pl.ds(pl.multiple_of(w * 5 * L, 32), 5 * L), :] = dot(cnt_ref[...], vs[...])
-
-        def rows_b(i, _):
+                vs[w % 2, i * CH:(i + 1) * CH, cols] = hi
+                vs[w % 2, L + i * CH:L + (i + 1) * CH, cols] = (v - hi.astype(F32)).astype(BF)
+
+    def summed(w, i, cols):
+        rows = slice(w * L + i * CH, w * L + (i + 1) * CH)
+        v = base[rows, cols] + acts_ref[w, i * CH:(i + 1) * CH, cols].astype(F32) + bias_ref[:, D + cols.start:D + cols.stop]
+        v1[rows, cols] = v
+        return v
+
+    def averages_one(w):
+        cut(w, summed)
+        avg1[w * 5 * L:(w + 1) * 5 * L, :] = dot(cnt_ref[...], vs[w % 2])
+
+    def decompose_one(w):
+        for i in range(nr):
             for c in range(nc):
                 cols = slice(c * CC, (c + 1) * CC)
-                rows = pl.ds(pl.multiple_of(w * L + i * CH, CH), CH)
+                rows = slice(w * L + i * CH, w * L + (i + 1) * CH)
                 v = v1[rows, cols]
                 cs = scaled_shares(v, 0)
                 mean = None
                 for k in range(5):
-                    at = pl.ds(pl.multiple_of((w * 5 + k) * L + i * CH, CH), CH)
+                    at = slice((w * 5 + k) * L + i * CH, (w * 5 + k) * L + (i + 1) * CH)
                     u = cs[k] * avg1[at, cols]
                     c1[at, cols] = cs[k]
                     mean = u if mean is None else mean + u
                 f = v - mean
                 first[rows, cols] = f
                 flow[pl.ds(pl.multiple_of(step * T + w * L + i * CH, CH), CH), cols] = f.astype(BF)
-            return 0
-        lax.fori_loop(0, nr, rows_b, 0)
-        return 0
-    lax.fori_loop(0, W, window_one, 0)
+
+    averages_one(0)
+    for w in range(W):
+        if w + 1 < W:
+            averages_one(w + 1)
+        decompose_one(w)
 
     here_t = pl.ds(pl.multiple_of(step * T, CH), T)
     base[...] = first[...]
 
-    def ffn(n, _):
-        cols = pl.ds(pl.multiple_of(n * FT, FT), FT)
-        h = dot(flow[here_t, :], wup_ref[cols, :], NT)
-        big, small = gelu_parts(h)
-        a = (h * big).astype(BF)
-        active[here_t, cols] = a
-        dgelu[:, cols] = (big + h * small).astype(BF)
-        base[...] += dot(a, wdn_ref[cols, :])
-        return 0
-    lax.fori_loop(0, FF // FT, ffn, 0)
-
-    def window_two(w, _):
-        def rows_a(i, _):
+    def up(n):
+        return dot(flow[here_t, :], wup_ref[n * FT:(n + 1) * FT, :], NT)
+
+    tiles = FF // FT
+    hs[0] = up(0)
+    for n in range(tiles + 1):
+        if n + 1 < tiles:
+            hs[(n + 1) % 2] = up(n + 1)
+        if n < tiles:
+            h = hs[n % 2]
+            big, small = gelu_parts(h)
+            active[here_t, n * FT:(n + 1) * FT] = (h * big).astype(BF)
+            dgelu[:, n * FT:(n + 1) * FT] = (big + h * small).astype(BF)
+        if n:
+            base[...] += dot(active[here_t, (n - 1) * FT:n * FT], wdn_ref[(n - 1) * FT:n * FT, :])
+
+    def branch(w, i, cols):
+        return base[w * L + i * CH:w * L + (i + 1) * CH, cols]
+
+    def averages_two(w):
+        cut(w, branch)
+        avg2[w % 2] = dot(cnt_ref[...], vs[w % 2])
+
+    def keep_at(w, i, cols):
+        def keep(k, cg):
+            stk[w % 2, k * L + i * CH:k * L + (i + 1) * CH, cols] = cg.astype(BF)
+        return keep
+
+    def decompose_two(w):
+        for i in range(nr):
             for c in range(nc):
                 cols = slice(c * CC, (c + 1) * CC)
-                rows = pl.ds(pl.multiple_of(w * L + i * CH, CH), CH)
-                here = pl.ds(pl.multiple_of(i * CH, CH), CH)
-                low_rows = pl.ds(pl.multiple_of(L + i * CH, CH), CH)
-                v = base[rows, cols]
-                hi = v.astype(BF)
-                vs[here, cols] = hi
-                vs[low_rows, cols] = (v - hi.astype(F32)).astype(BF)
-            return 0
-        lax.fori_loop(0, nr, rows_a, 0)
-        avg2[...] = dot(cnt_ref[...], vs[...])
-
-        def rows_b(i, _):
-            for c in range(nc):
-                cols = slice(c * CC, (c + 1) * CC)
-                rows = pl.ds(pl.multiple_of(w * L + i * CH, CH), CH)
-                here = pl.ds(pl.multiple_of(i * CH, CH), CH)
+                rows = slice(w * L + i * CH, w * L + (i + 1) * CH)
+                here = slice(i * CH, (i + 1) * CH)
                 v = base[rows, cols]
                 cs = scaled_shares(v, 10)
-                avs = [avg2[pl.ds(pl.multiple_of(k * L + i * CH, CH), CH), cols] for k in range(5)]
+                avs = [avg2[w % 2, k * L + i * CH:k * L + (i + 1) * CH, cols] for k in range(5)]
                 mean = functools.reduce(lambda a, b: a + b, [c_ * a_ for c_, a_ in zip(cs, avs)])
                 out_ref[w, here, cols] = (v - mean).astype(BF)
                 g = og_ref[w, here, cols].astype(F32)
-                for k in range(5):
-                    stk[pl.ds(pl.multiple_of(k * L + i * CH, CH), CH), cols] = (cs[k] * g).astype(BF)
-                g, extra = backward(v, g, cs, avs, mean, 10)
-                base[rows, cols] = g + extra
-            return 0
-        lax.fori_loop(0, nr, rows_b, 0)
-        rows = pl.ds(pl.multiple_of(w * L, L), L)
-        gs = base[rows, :] - dot(cntt_ref[...], stk[...])
+                base[rows, cols] = g + backward(v, g, cs, avs, mean, 10, keep_at(w, i, cols))
+
+    def back_two(w):
+        rows = slice(w * L, (w + 1) * L)
+        gs = base[rows, :] - dot(cntt_ref[...], stk[w % 2])
         base[rows, :] = gs
         gb[pl.ds(pl.multiple_of(step * T + w * L, 32), L), :] = gs.astype(BF)
-        return 0
-    lax.fori_loop(0, W, window_two, 0)
-
-    def ffn_back(n, _):
-        cols = pl.ds(pl.multiple_of(n * FT, FT), FT)
-        ga = dot(gb[here_t, :], wdn_ref[cols, :], NT)
-        gh = (ga * dgelu[:, cols].astype(F32)).astype(BF)
-        ghid[here_t, cols] = gh
-        base[...] += dot(gh, wup_ref[cols, :])
-        return 0
-    lax.fori_loop(0, FF // FT, ffn_back, 0)
-
-    def window_three(w, _):
-        def rows_b(i, _):
+
+    averages_two(0)
+    for w in range(W):
+        if w + 1 < W:
+            averages_two(w + 1)
+        decompose_two(w)
+        if w:
+            back_two(w - 1)
+    back_two(W - 1)
+
+    def down(n):
+        return dot(gb[here_t, :], wdn_ref[n * FT:(n + 1) * FT, :], NT)
+
+    hs[0] = down(0)
+    for n in range(tiles + 1):
+        if n + 1 < tiles:
+            hs[(n + 1) % 2] = down(n + 1)
+        if n < tiles:
+            ghid[here_t, n * FT:(n + 1) * FT] = (hs[n % 2] * dgelu[:, n * FT:(n + 1) * FT].astype(F32)).astype(BF)
+        if n:
+            base[...] += dot(ghid[here_t, (n - 1) * FT:n * FT], wup_ref[(n - 1) * FT:n * FT, :])
+
+    def decompose_three(w):
+        for i in range(nr):
             for c in range(nc):
                 cols = slice(c * CC, (c + 1) * CC)
-                rows = pl.ds(pl.multiple_of(w * L + i * CH, CH), CH)
+                rows = slice(w * L + i * CH, w * L + (i + 1) * CH)
                 v = v1[rows, cols]
                 g = base[rows, cols]
-                ats = [pl.ds(pl.multiple_of((w * 5 + k) * L + i * CH, CH), CH) for k in range(5)]
+                ats = [slice((w * 5 + k) * L + i * CH, (w * 5 + k) * L + (i + 1) * CH) for k in range(5)]
                 cs = [c1[at, cols] for at in ats]
                 avs = [avg1[at, cols] for at in ats]
                 mean = v - first[rows, cols]
-                for k in range(5):
-                    stk[pl.ds(pl.multiple_of(k * L + i * CH, CH), CH), cols] = (cs[k] * g).astype(BF)
-                g, extra = backward(v, g, cs, avs, mean, 0)
+                extra = backward(v, g, cs, avs, mean, 0, keep_at(w, i, cols))
                 base[rows, cols] = g + extra
                 accb[:, cols] += extra[0:8] + extra[8:16]
-            return 0
-        lax.fori_loop(0, nr, rows_b, 0)
-        rows = pl.ds(pl.multiple_of(w * L, L), L)
-        gs = base[rows, :] - dot(cntt_ref[...], stk[...])
+
+    def back_three(w):
+        rows = slice(w * L, (w + 1) * L)
+        gs = base[rows, :] - dot(cntt_ref[...], stk[w % 2])
         gsum_ref[w] = gs
         glow[rows, :] = gs.astype(BF)
-        return 0
-    lax.fori_loop(0, W, window_three, 0)
+
+    for w in range(W):
+        decompose_three(w)
+        if w:
+            back_three(w - 1)
+    back_three(W - 1)
 
     back = dot(glow[...], wq_ref[D:2 * D, :], NT).astype(BF)
     for w in range(W):
@@ -234,19 +252,28 @@
     @pl.when(step == steps - 1)
     def _():
         small_ref[0:8, :] = accb[...]
+        for at in (4, 9, 14, 19):
+            accs[at] = -(accs[at - 4] + accs[at - 3] + accs[at - 2] + accs[at - 1])
         for k in range(20):
             small_ref[8 + 8 * k:16 + 8 * k, 0:128] = accs[k]
             small_ref[8 + 8 * k:16 + 8 * k, 128:512] = jnp.zeros((8, 384), F32)
 
-        def wgrad(n, _):
-            cols = pl.ds(pl.multiple_of(n * FT, FT), FT)
-            gup_ref[cols, :] = dot(ghid[:, cols], flow[...], TN)
-            gdn_ref[cols, :] = dot(active[:, cols], gb[...], TN)
-            return 0
-        lax.fori_loop(0, FF // FT, wgrad, 0)
-
-
-def middle(mix, acts, sig, og, wqo, wup, wdn, bias, inv, W=4):
+        copies = {}
+        for n in range(tiles):
+            part = slice(n * FT, (n + 1) * FT)
+            for i, (left, right, ref) in enumerate(((ghid, flow, gup_ref), (active, gb, gdn_ref))):
+                k = (n % 2) * 2 + i
+                if n >= 2:
+                    copies[n - 2, i].wait()
+                wg[k] = dot(left[:, part], right[...], TN)
+                copies[n, i] = pltpu.make_async_copy(wg.at[k], ref.at[pl.ds(n * FT, FT)], wsem.at[k])
+                copies[n, i].start()
+        for n in range(max(tiles - 2, 0), tiles):
+            for i in range(2):
+                copies[n, i].wait()
+
+
+def middle(mix, acts, sig, og, wqo, wup, wdn, bias, invt, W=4):
     n, L, D = acts.shape
     FF = wup.shape[0]
     steps = n // W
@@ -257,9 +284,9 @@
     cnt[:, L:2 * L] = A.reshape(5 * L, L)
     cntt = np.zeros((L, 512), np.float32)
     cntt[:, :5 * L] = A.transpose(2, 0, 1).reshape(L, 5 * L)
-    cnt = jnp.asarray(cnt, BF)
-    cntt = jnp.asarray(cntt, BF)
+    cnt, cntt = (np.asarray(x, BF) for x in (cnt, cntt))
     whole = lambda *s: pl.BlockSpec(s, lambda i: (0,) * len(s), pipeline_mode=pl.Buffered(1))
+    anywhere = pl.BlockSpec(memory_space=pl.ANY)
     piece = lambda *s: pl.BlockSpec(s, lambda i: (i,) + (0,) * (len(s) - 1))
     return pl.pallas_call(
         functools.partial(middle_kernel, W, L, D, FF, steps),
@@ -276,13 +303,13 @@
         in_specs=[
             pl.BlockSpec(memory_space=pltpu.SMEM),
             piece(W, L, D), piece(W, L, D), piece(W, L, D),
-            whole(2 * D, D), whole(FF, D), whole(FF, D), whole(1, D), whole(L, L), whole(5 * L, 256), whole(L, 512),
+            whole(2 * D, D), whole(FF, D), whole(FF, D), whole(1, bias.shape[1]), whole(L, L), whole(5 * L, 256), whole(L, 512),
         ],
         out_specs=(
-            piece(W, L, D), piece(W, L, D), piece(W, L, D), whole(D, D), whole(FF, D), whole(FF, D), whole(168, D),
+            piece(W, L, D), piece(W, L, D), piece(W, L, D), whole(D, D), anywhere, anywhere, whole(168, D),
         ),
         scratch_shapes=[
-            pltpu.VMEM((256, D), BF),
+            pltpu.VMEM((2, 256, D), BF),
             pltpu.VMEM((T, D), F32),
             pltpu.VMEM((W * 5 * L, D), F32),
             pltpu.VMEM((W * 5 * L, D), F32),
@@ -294,14 +321,17 @@
             pltpu.VMEM((n * L, D), BF),
             pltpu.VMEM((n * L, FF), BF),
             pltpu.VMEM((T, D), BF),
-            pltpu.VMEM((5 * L, D), F32),
-            pltpu.VMEM((512, D), BF),
+            pltpu.VMEM((2, 5 * L, D), F32),
+            pltpu.VMEM((2, 512, D), BF),
             pltpu.VMEM((20, 8, 128), F32),
             pltpu.VMEM((8, D), F32),
+            pltpu.VMEM((2, T, 512), F32),
+            pltpu.VMEM((4, 512, D), F32),
+            pltpu.SemaphoreType.DMA((4,)),
         ],
         compiler_params=pltpu.CompilerParams(vmem_limit_bytes=60 * 1024 * 1024),
         name="middle",
-    )(mix, acts, sig, og, wqo, wup, wdn, bias, inv.T, cnt, cntt)
+    )(mix, acts, sig, og, wqo, wup, wdn, bias, invt, cnt, cntt)
 
 
 def sign_lanes(rows, left, right):
@@ -519,9 +549,9 @@
 
 
 def tail_kernel(n, L, D, slots, blocks, owner, gmix_h, z_h, acts_h, gsum_h, weights_h, gout_h, gup_h, gdn_h,
-                obs_ref, wq_ref, basist_ref, eye_ref, sums_ref,
+                obs_ref, wqo_h, basis_ref, eye_ref, sums_ref,
                 dense_out, mixer_out, small_out, gin_h,
-                gmix, z, acts, gsum, mix, src, tiles, glow, gbias, tmp, con,
+                gmix, z, acts, gsum, mix, src, tiles, glow, gbias, tmp, con, basist, wq_ref,
                 fc0, fc1, fv0, fv1, fu0, fu1, fa0, fa1, small_one, small_two,
                 loads, send, recv_c, recv_v, recv_u, recv_a, small_send, small_recv):
     sizes, here = roles()
@@ -538,7 +568,7 @@
     def load(i, a, b):
         return pltpu.make_async_copy(a, b, loads.at[i])
     firsts = [load(0, gmix_h, gmix), load(1, z_h, z), load(2, weights_h, mix)]
-    later = [load(3, acts_h, acts), load(4, gsum_h, gsum)]
+    later = [load(3, acts_h, acts), load(4, gsum_h, gsum), load(18, wqo_h.at[pl.ds(0, D)], wq_ref)]
     grads = []
     start = D
     for i, ref in enumerate((gout_h, gup_h, gdn_h)):
@@ -560,6 +590,7 @@
         sizes, here, con_at, fc0, fv0, fu0, fa0, dense_out,
         send.at[0], recv_c.at[0], recv_v.at[0], recv_u.at[0], recv_a.at[0])
 
+    basist[...] = basis_ref[...].astype(F32).T.astype(BF)
     firsts[0].wait()
 
     def spectra(w):
@@ -608,7 +639,7 @@
 
     def query(w):
         part = pl.ds(pl.multiple_of(w * L, 32), L)
-        g = dot(basist_ref[...], gather_rows(tiles, w, slots, n))
+        g = dot(basist[...], gather_rows(tiles, w, slots, n))
         glow[part, :] = g.astype(BF)
         gbias[...] += functools.reduce(lambda p, q: p + q, [g[i * 8:(i + 1) * 8] for i in range(L // 8)])
     each(0, n, query)
@@ -695,10 +726,10 @@
     result.wait()
 
 
-def tail(gmix, z, acts, gsum, observed, wqo, basist, weights, gout, gup, gdn, sums, owner_list, shard_rows):
+def tail(gmix, z, acts, gsum, observed, wqo, basis, weights, gout, gup, gdn, sums, owner_list, shard_rows):
     n, L = observed.shape
     D = acts.shape[1]
-    slots = basist.shape[1] // 2
+    slots = basis.shape[0] // 2
     ndp, nmode, mixer_rows = weights.shape[:3]
     nd = ndp * nmode
     total = nd * shard_rows
@@ -717,7 +748,7 @@
             jax.ShapeDtypeStruct((n * L, D), F32),
         ),
         in_specs=[pl.BlockSpec(memory_space=pltpu.SMEM)] + [anywhere] * 8 + [
-            vmem, pl.BlockSpec(memory_space=pltpu.VMEM), vmem, vmem, vmem],
+            vmem, anywhere, vmem, vmem, vmem],
         out_specs=(vmem, vmem, vmem, anywhere),
         scratch_shapes=[
             pltpu.VMEM((n * L, D), BF),
@@ -731,14 +762,16 @@
             pltpu.VMEM((8, D), F32),
             pltpu.VMEM((D // 128, 80, 128), F32),
             pltpu.VMEM((nd, shard_rows, D), BF),
+            pltpu.VMEM((L, 2 * slots), BF),
+            pltpu.VMEM((D, D), BF),
         ] + [pltpu.VMEM((count,) + s, BF) for count in counts for s in shapes] + [
             pltpu.VMEM((nmode, 32, 128), F32), pltpu.VMEM((ndp, 32, 128), F32),
-            sem(18), sem(2, 4), sem(2, counts[0]), sem(2, counts[1]), sem(2, counts[2]), sem(2, counts[3]),
+            sem(19), sem(2, 4), sem(2, counts[0]), sem(2, counts[1]), sem(2, counts[2]), sem(2, counts[3]),
             sem(ndp + nmode - 2), sem(ndp + nmode - 2),
         ],
         compiler_params=pltpu.CompilerParams(collective_id=1, has_side_effects=True, vmem_limit_bytes=62 * 1024 * 1024),
         name="tail",
-    )(owner_list, gmix, z, acts, gsum, weights, gout, gup, gdn, observed, wqo[:D], basist, jnp.eye(L, dtype=F32), sums)
+    )(owner_list, gmix, z, acts, gsum, weights, gout, gup, gdn, observed, wqo, basis, np.eye(L, dtype=np.float32), sums)
 
 
 def gatherer(sizes, here, slot_of, whole_of, send, send_a, recv):
@@ -914,7 +947,7 @@
 
     def project(i):
         part = pl.ds(pl.multiple_of(i * T, T), T)
-        query[part, :] = (dot(acts[part, :], table[0:D, :]) + bias_ref[...]).astype(BF)
+        query[part, :] = (dot(acts[part, :], table[0:D, :]) + bias_ref[:, 0:D]).astype(BF)
 
     def spectra(w):
         part = pl.ds(pl.multiple_of(w * L, 32), L)
@@ -1003,33 +1036,57 @@
         ],
         compiler_params=pltpu.CompilerParams(collective_id=0, has_side_effects=True, vmem_limit_bytes=62 * 1024 * 1024),
         name="head",
-    )(restore, inputs.reshape(tokens, D), dense, mixer, observed, bias, basis, inv, jnp.eye(L, dtype=F32))
-
-
-def fourier_tables(mode_index, length):
-    positions = jnp.arange(length, dtype=jnp.int32)
-    phases = mode_index[:, None] * positions[None, :] % length
-    angles = phases.astype(jnp.float32) * (2.0 * jnp.pi / length)
-    forward = jnp.stack([jnp.cos(angles), -jnp.sin(angles)])
-    slot_ids = jnp.arange(mode_index.shape[0], dtype=jnp.int32)
-    back_phase = slot_ids[:, None] * positions[None, :] % length
-    back_angle = back_phase.astype(jnp.float32) * (2.0 * jnp.pi / length)
-    coefs = jnp.where(slot_ids == 0, 1.0, 2.0).astype(jnp.float32) / length
-    inverse = jnp.stack(
-        [jnp.cos(back_angle) * coefs[:, None], -jnp.sin(back_angle) * coefs[:, None]]
-    )
-    return (forward, jnp.transpose(inverse, (2, 0, 1)))
-
-
-def adam_update(weight, gradient, moment, second, step_rate):
+    )(restore, inputs.reshape(tokens, D), dense, mixer, observed, bias, basis, inv, np.eye(L, dtype=np.float32))
+
+
+def adam_terms(weight, gradient, moment, second, step_rate):
     moment_new = BETA_ONE * moment + (1.0 - BETA_ONE) * gradient
     second_new = BETA_TWO * second + (1.0 - BETA_TWO) * gradient * gradient
-    scaled_m = moment_new / (1.0 - BETA_ONE**STEP)
-    scaled_v = second_new / (1.0 - BETA_TWO**STEP)
-    weight_new = weight - step_rate * (
-        scaled_m / (jnp.sqrt(scaled_v) + ADAM_EPS) + DECAY_RATE * weight
-    )
-    return (moment_new, second_new, weight_new)
+    scaled_m = moment_new * (1.0 / (1.0 - BETA_ONE**STEP))
+    scaled_v = second_new * (1.0 / (1.0 - BETA_TWO**STEP))
+    weight_new = weight - step_rate * (scaled_m / (jnp.sqrt(scaled_v) + ADAM_EPS) + DECAY_RATE * weight)
+    return moment_new, second_new, weight_new
+
+
+def update_kernel(*refs):
+    dense, mixer, passed = refs[:4], refs[4:8], refs[8]
+    dense_out, mixer_out, passed_out, sem = refs[9:12], refs[12:15], refs[15], refs[16]
+    copy = pltpu.make_async_copy(passed, passed_out, sem)
+    copy.start()
+    for ins, outs, rate in ((dense, dense_out, RATE_DENSE), (mixer, mixer_out, RATE_MIXER)):
+        for ref, value in zip(outs, adam_terms(*(x[...] for x in ins), rate)):
+            ref[...] = value
+    copy.wait()
+
+
+def update(dense, mixer, passed):
+    vmem = pl.BlockSpec(memory_space=pltpu.VMEM)
+    anywhere = pl.BlockSpec(memory_space=pl.ANY)
+    like = lambda x: jax.ShapeDtypeStruct(x.shape, x.dtype)
+    return pl.pallas_call(
+        update_kernel,
+        out_shape=(like(dense[0]),) * 3 + (like(mixer[0]),) * 3 + (like(passed),),
+        in_specs=[vmem] * 8 + [anywhere],
+        out_specs=(vmem,) * 6 + (anywhere,),
+        scratch_shapes=[pltpu.SemaphoreType.DMA],
+        compiler_params=pltpu.CompilerParams(vmem_limit_bytes=32 * 1024 * 1024),
+        name="update",
+    )(*dense, *mixer, passed)
+
+
+def forward_table(mode_index, length):
+    slots = mode_index.shape[0]
+    row = jnp.arange(2 * slots, dtype=jnp.int32)
+    mode = jnp.concatenate([mode_index, mode_index])
+    turn = (mode[:, None] * jnp.arange(length, dtype=jnp.int32)[None, :] + (row >= slots)[:, None] * (length // 4)) % length
+    return jnp.cos(turn.astype(F32) * (2.0 * math.pi / length)).astype(BF)
+
+
+def inverse_table(slots, length):
+    turn = np.arange(length)[:, None] * np.arange(slots)[None, :] % length
+    angle = turn * (2.0 * np.pi / length)
+    scale = np.where(np.arange(slots) == 0, 1.0, 2.0) / length
+    return np.concatenate([np.cos(angle) * scale, -np.sin(angle) * scale], 1).astype(np.float32).astype(BF)
 
 
 def shards(
@@ -1052,31 +1109,34 @@
     length, width = inputs.shape[1:]
     slots = mode_index.shape[0]
     hidden = (dense_master.shape[0] * ndp * nmode - 2 * width) // 2
-    forward, inverse = fourier_tables(mode_index, length)
-    basis = forward.astype(BF).reshape(2 * slots, length)
-    inv = inverse.astype(BF).reshape(length, 2 * slots)
+    basis = forward_table(mode_index, length)
+    inv = inverse_table(slots, length)
+    small_row = small_master[None]
     places = jnp.arange(owner_list.shape[0], dtype=jnp.int32)
     restore = jnp.sum(jnp.where(owner_list[None, :] == places[:, None], places[None, :], 0), axis=1)
     acts, spectra, sig, wqo, wup, wdn, weights = head(
-        inputs, observed, dense_master, mixer_master.reshape(-1, mixer_master.shape[2]), restore, small_master[None, :width],
+        inputs, observed, dense_master, mixer_master.reshape(-1, mixer_master.shape[2]), restore, small_row,
         basis, inv, hidden,
     )
     output, grad_summed, grad_mixed, g_out, g_up, g_down, sums = middle(
-        small_master[2 * width :], acts.reshape(inputs.shape), sig.reshape(inputs.shape), out_grad, wqo, wup, wdn,
-        small_master[None, width : 2 * width], inv,
+        small_master, acts.reshape(inputs.shape), sig.reshape(inputs.shape), out_grad, wqo, wup, wdn,
+        small_row, np.ascontiguousarray(inv.T),
     )
     dense_mine, mixer_mine, small_all, input_grad = tail(
-        grad_mixed.reshape(-1, width), spectra, acts, grad_summed.reshape(-1, width), observed, wqo, basis.T, weights,
+        grad_mixed.reshape(-1, width), spectra, acts, grad_summed.reshape(-1, width), observed, wqo, basis, weights,
         g_out, g_up, g_down, sums, owner_list, dense_master.shape[0],
     )
     small_total = jnp.concatenate([small_all[:8].reshape(-1), jnp.sum(small_all[8:28], axis=1)])
-    dense_first_new, dense_second_new, dense_new = adam_update(
-        dense_master, dense_mine, dense_first, dense_second, RATE_DENSE
+    flat = lambda x: x.reshape(-1, x.shape[-1])
+    dense_first_new, dense_second_new, dense_new, mixer_first_new, mixer_second_new, mixer_new, input_grad = update(
+        (dense_master, dense_mine, dense_first, dense_second),
+        (flat(mixer_master), mixer_mine, flat(mixer_first), flat(mixer_second)),
+        input_grad,
     )
-    mixer_first_new, mixer_second_new, mixer_new = adam_update(
-        mixer_master, mixer_mine.reshape(mixer_master.shape), mixer_first, mixer_second, RATE_MIXER
+    mixer_first_new, mixer_second_new, mixer_new = (
+        x.reshape(mixer_master.shape) for x in (mixer_first_new, mixer_second_new, mixer_new)
     )
-    small_first_new, small_second_new, small_new = adam_update(
+    small_first_new, small_second_new, small_new = adam_terms(
         small_master, small_total, small_first, small_second, RATE_SMALL
     )
     return (

time: 270 us -> 238 us (0.88)
  Pallas kernels: 251 us -> 223 us
  other arithmetic: 8.49 us -> 4.51 us
    pallas_call x1, Pallas kernels: 93.7 us -> 62.8 us  [middle(): pl.pallas_call(functools.partial(middle_kernel, W, L, D, FF, steps), grid...]
    sub x3 -> x1, other arithmetic: 4.09 us -> 0.63 us  [adam_terms(): weight - step_rate * (scaled_m / (jnp.sqrt(scaled_v) + ADAM_EPS) + DECAY_...]
    unnamed x29 -> x24, local copies, waits for them, and re-layouts: 1.73 us -> 4.87 us
    pallas_call x0 -> x1, Pallas kernels: none -> 3 us  [update(): pl.pallas_call(update_kernel, out_shape=(like(dense[0]),) * 3 + (like(mix...]
where the time goes in v4:
time: 238 us; the launch traced here: 237 us
  Pallas kernels  223 us (94%)
  local copies, waits for them, and re-layouts  8.1 us (3%)
  other arithmetic  4.51 us (2%)
    pallas_call x1, Pallas kernels, tail(): pl.pallas_call(functools.partial(tail_kernel, n, L, D, slots, owner_list....  82.8 us
    pallas_call x1, Pallas kernels, head(): pl.pallas_call(functools.partial(head_kernel, n, L, D, slots, restore.sha...  74.9 us
    pallas_call x1, Pallas kernels, middle(): pl.pallas_call(functools.partial(middle_kernel, W, L, D, FF, steps), grid...  62.8 us
    unnamed x24, local copies, waits for them, and re-layouts  4.87 us

profile of v4, /device:TPU:0, one launch (start us, length us, event | category | flops | bytes accessed | tf_op | source)
XLA Modules:
  0.0 237.0 jit_solution(16472583031233725417)
XLA Ops:
  0.6 1.4 select_reduce_fusion.restore
  2.0 0.8 compare_select_fusion
  2.8 1.3 broadcast_in_dim.23.bias_ref
  4.1 0.9 fusion.3.basis_ref
  5.0 74.9 %head.1 = (bf16[1536,512]{1,0:T(8,128)(2,1)}, bf16[8,1536,64]{2,1,0:T(8,128)(2,1)}, bf16[1536,512]{1,0:T(8,128)(2,1)}, bf16[1024,512]{1,0:T(8,128)(2,1)}, bf16[2...) custom-call(s32[256]{0:T(256)} %select_reduce_fusion.restore, ...), custom_call_target="tpu_custom_call" | custom-call | tf_op jit(solution)/shard_map/head/pallas_call | solution.py:1010
  79.9 62.8 %middle.1 = (bf16[16,96,512]{2,1,0:T(8,128)(2,1)}, f32[16,96,512]{2,1,0:T(8,128)}, bf16[16,96,512]{2,1,0:T(8,128)(2,1)}, f32[512,512]{1,0:T(8,128)}, f32[2048,51...) custom-call(f32[1044]{0:T(1024)} %mix_ref.1, bf16[16,96,512]{2,1,0:T(8,128)(2,1)} %bitcast.20, ...), custom_call_target="tpu_custom_call" | custom-call | tf_op jit(solution)/shard_map/middle/pallas_call | solution.py:291
  142.7 0.0 copy-start.9
  142.7 0.0 copy-start.10
  142.7 0.0 copy-start.11
  142.8 0.0 copy-start.1
  142.8 0.0 copy-start.2
  142.8 0.0 copy-start.3
  142.8 0.0 copy-start.4
  142.8 0.0 copy-start.6
  142.8 82.8 %tail.1 = (f32[160,512]{1,0:T(8,128)}, f32[768,128]{1,0:T(8,128)}, f32[32,128]{1,0:T(8,128)}, f32[1536,512]{1,0:T(8,128)}) custom-call(s32[256]{0:T(256)} %owner.1, bf16[1536,512]{1,0:T(8,128)(2,1)} %bitcast.22, bf16[8,1536,64]{2,1,0:T(8,128)(2,1)} %get-tuple-element.44.z_h, bf16[1536,512]{1,0:T(8,128)(2,1)} %get-tuple-element.37.acts_h, ...), custom_call_target="tpu_custom_call" | custom-call | tf_op jit(solution)/shard_map/tail/pallas_call | solution.py:744
  225.6 0.8 slice_reduce_fusion
  226.4 1.3 slice_bitcast_fusion.1
  227.7 0.7 slice_bitcast_fusion
  228.3 0.0 copy-done.9
  228.3 0.0 copy-done.10
  228.3 0.0 copy-done.11
  228.3 0.6 multiply_subtract_fusion
  229.0 0.0 copy-done.1
  229.0 0.0 copy-done.2
  229.0 0.0 copy-done.3
  229.0 0.0 copy-done.4
  229.0 0.0 copy-done.6
  229.0 0.0 copy-start
  229.0 1.9 copy-done
  230.9 0.0 copy-start.5
  230.9 1.0 copy-done.5
  231.9 0.0 copy-start.7
  231.9 1.0 copy-done.7
  232.9 0.0 copy-start.8
  232.9 1.0 copy-done.8
  233.8 3.0 %update.1 = (f32[160,512]{1,0:T(8,128)}, f32[160,512]{1,0:T(8,128)}, f32[160,512]{1,0:T(8,128)}, f32[768,128]{1,0:T(8,128)}, f32[768,128]{1,0:T(8,128)}, /*index=5*/f32[768,128]{1,0:T(8,128)}, f32[1536,512]{1,0:T(8,128)}) custom-call(f32[160,512]{1,0:T(8,128)S(1)} %copy-done.2, f32[160,512]{1,0:T(8,128)S(1)} %copy-done.8, f32[160,512]{1,0:T(8,128)S(1)} %copy-done.6, ...), custom_call_target="tpu_custom_call" | custom-call | tf_op jit(solution)/shard_map/update/pallas_call | solution.py:1066
Async XLA Ops:
  142.7 85.6 %copy-start.9 = (f32[1044]{0:T(1024)S(1)}, f32[1044]{0:T(1024)}, u32[]{:S(2)}) copy-start(f32[1044]{0:T(1024)} %mix_ref.1) | copy-start | bytes 12532
  142.7 85.6 %copy-start.10 = (f32[1044]{0:T(1024)S(1)}, f32[1044]{0:T(1024)}, u32[]{:S(2)}) copy-start(f32[1044]{0:T(1024)} %param.33) | copy-start | bytes 12532
  142.7 85.6 %copy-start.11 = (f32[1044]{0:T(1024)S(1)}, f32[1044]{0:T(1024)}, u32[]{:S(2)}) copy-start(f32[1044]{0:T(1024)} %param.32) | copy-start | bytes 12532
  142.8 86.2 %copy-start.1 = (f32[12,64,128]{2,1,0:T(8,128)S(1)}, f32[12,64,128]{2,1,0:T(8,128)}, u32[]{:S(2)}) copy-start(f32[12,64,128]{2,1,0:T(8,128)} %param.28) | copy-start | bytes 1179652
  142.8 86.2 %copy-start.2 = (f32[160,512]{1,0:T(8,128)S(1)}, f32[160,512]{1,0:T(8,128)}, u32[]{:S(2)}) copy-start(f32[160,512]{1,0:T(8,128)} %refs_0_.1) | copy-start | bytes 983044
  142.8 86.2 %copy-start.3 = (f32[12,64,128]{2,1,0:T(8,128)S(1)}, f32[12,64,128]{2,1,0:T(8,128)}, u32[]{:S(2)}) copy-start(f32[12,64,128]{2,1,0:T(8,128)} %param.29) | copy-start | bytes 1179652
  142.8 86.2 %copy-start.4 = (f32[12,64,128]{2,1,0:T(8,128)S(1)}, f32[12,64,128]{2,1,0:T(8,128)}, u32[]{:S(2)}) copy-start(f32[12,64,128]{2,1,0:T(8,128)} %param.30) | copy-start | bytes 1179652
  142.8 86.2 %copy-start.6 = (f32[160,512]{1,0:T(8,128)S(1)}, f32[160,512]{1,0:T(8,128)}, u32[]{:S(2)}) copy-start(f32[160,512]{1,0:T(8,128)} %refs_2_.1) | copy-start | bytes 983044
  229.0 1.9 copy-start
  230.9 1.0 copy-start.5
  231.9 1.0 copy-start.7
  232.9 1.0 copy-start.8

commit v5 on v4

--- a/solution.py
+++ b/solution.py
@@ -410,6 +410,9 @@
             stages[s](t - s)
 
 
+JOIN = 12
+
+
 def roles():
     ndp, nmode = lax.axis_size("dp"), lax.axis_size("mode")
     half = nmode // 2
@@ -600,40 +603,62 @@
     firsts[1].wait()
     firsts[2].wait()
 
-    def mix_mode(m):
-        def slot(jl, _):
-            at = pl.ds(pl.multiple_of((m * per + jl) * n, n), n)
-            at2 = pl.ds(pl.multiple_of((m * per + jl) * 2 * n, 2 * n), 2 * n)
+    def mix_slots(places):
+        taken = []
+        for m, jl, h in places:
+            y = tiles[h, pl.ds(pl.multiple_of((m * per + jl) * n, n), n), :]
+            both = jnp.concatenate([y, swap_halves(y) * sign_lanes(n, 1.0, -1.0)], 0).astype(BF)
             part = pl.ds(pl.multiple_of(jl * depth, depth), depth)
-            for h in range(heads):
-                y = tiles[h, at, :]
-                both = jnp.concatenate([y, swap_halves(y) * sign_lanes(n, 1.0, -1.0)], 0).astype(BF)
-                x = dot(both, head_weights(mix, h, pieces, m, part), NT)
-                tiles[h, at, :] = jnp.concatenate([x[:n], x[n:]], 1)
-                g = dot(z[h, at2, :], both, TN).astype(BF)
-                for q in range(pieces):
-                    mix[h * pieces + q, m, part, :] = g[q * depth:(q + 1) * depth]
-            return 0
-        lax.fori_loop(0, per, slot, 0, unroll=2)
-
-    mine_y = mode // 2
-
-    def mode_at(i, core):
-        return lax.rem(mine_y + 1 + i, nmode // 2) * 2 + core
-
-    def other_modes(i):
-        m = mode_at(i, 1 - here["c"])
-        mix_mode(m)
-
-        def hand(p):
-            half = sizes["u"]
-            b, y = lax.rem(p, half), m // 2
-            core = 1 - here["c"]
-            send_m({"a": p // half, "u": jnp.where(core == 0, b, y), "v": jnp.where(core == 0, y, b), "c": core}).start()
-        each(0, ndp, hand)
-    each(0, nmode // 2, other_modes)
-    each(0, nmode // 2, lambda i: mix_mode(mode_at(i, here["c"])))
-    each(0, na, first_m)
+            x = z[h, pl.ds(pl.multiple_of((m * per + jl) * 2 * n, 2 * n), 2 * n), :]
+            taken.append((both, head_weights(mix, h, pieces, m, part), x))
+        products = [(dot(both, w, NT), dot(x, both, TN).astype(BF)) for both, w, x in taken]
+        for (m, jl, h), (x, g) in zip(places, products):
+            part = pl.ds(pl.multiple_of(jl * depth, depth), depth)
+            tiles[h, pl.ds(pl.multiple_of((m * per + jl) * n, n), n), :] = jnp.concatenate([x[:n], x[n:]], 1)
+            for q in range(pieces):
+                mix[h * pieces + q, m, part, :] = g[q * depth:(q + 1) * depth]
+
+    if pieces == 1:
+        def mix_shard(at):
+            p, m = place_of(sizes, at)
+
+            for at in range(0, per, JOIN):
+                mix_slots([(m, jl, p) for jl in range(at, min(at + JOIN, per))])
+
+        def feed(t, d):
+            def pair(e):
+                other = move(sizes, move(sizes, move(sizes, partner_of(here), "a", t + 1), "u", e), "v", d)
+                mix_shard(other)
+                send_m(other).start()
+                mix_shard(move(sizes, move(sizes, move(sizes, here, "a", t + 1), "u", e), "v", d))
+            each(0, sizes["u"], pair)
+        for d in range(1, sizes["v"]):
+            each(0, na, lambda t: feed(t, d))
+        each(0, na, first_m)
+        each(0, na, lambda t: feed(t, 0))
+    else:
+        def mix_mode(m):
+            def slot(jl, _):
+                mix_slots([(m, jl, h) for h in range(heads)])
+                return 0
+            lax.fori_loop(0, per, slot, 0, unroll=2)
+
+        def mode_at(i, core):
+            return lax.rem(mode // 2 + 1 + i, nmode // 2) * 2 + core
+
+        def other_modes(i):
+            m = mode_at(i, 1 - here["c"])
+            mix_mode(m)
+
+            def hand(p):
+                half = sizes["u"]
+                b, y = lax.rem(p, half), m // 2
+                core = 1 - here["c"]
+                send_m({"a": p // half, "u": jnp.where(core == 0, b, y), "v": jnp.where(core == 0, y, b), "c": core}).start()
+            each(0, ndp, hand)
+        each(0, nmode // 2, other_modes)
+        each(0, nmode // 2, lambda i: mix_mode(mode_at(i, here["c"])))
+        each(0, na, first_m)
 
     gbias[...] = jnp.zeros_like(gbias)
 
@@ -1069,7 +1094,7 @@
         in_specs=[vmem] * 8 + [anywhere],
         out_specs=(vmem,) * 6 + (anywhere,),
         scratch_shapes=[pltpu.SemaphoreType.DMA],
-        compiler_params=pltpu.CompilerParams(vmem_limit_bytes=32 * 1024 * 1024),
+        compiler_params=pltpu.CompilerParams(vmem_limit_bytes=62 * 1024 * 1024),
         name="update",
     )(*dense, *mixer, passed)
 

time: 238 us -> 319 us (1.34)
  Pallas kernels: 223 us -> 310 us
  local copies, waits for them, and re-layouts: 8.1 us -> 3.26 us
    pallas_call x1, Pallas kernels: 3 us -> 99.5 us  [update(): pl.pallas_call(update_kernel, out_shape=(like(dense[0]),) * 3 + (like(mix...]
    pallas_call x1, Pallas kernels: 82.8 us -> 72.5 us  [tail(): pl.pallas_call(functools.partial(tail_kernel, n, L, D, slots, owner_list....]
    unnamed x24 -> x6, local copies, waits for them, and re-layouts: 4.87 us -> 0.02 us
where the time goes in v5:
time: 319 us; the launch traced here: 318 us
  Pallas kernels  310 us (97%)
  other arithmetic  4.51 us (1%)
  local copies, waits for them, and re-layouts  3.26 us (1%)
    pallas_call x1, Pallas kernels, update(): pl.pallas_call(update_kernel, out_shape=(like(dense[0]),) * 3 + (like(mix...  99.5 us
    pallas_call x1, Pallas kernels, head(): pl.pallas_call(functools.partial(head_kernel, n, L, D, slots, restore.sha...  75 us
    pallas_call x1, Pallas kernels, tail(): pl.pallas_call(functools.partial(tail_kernel, n, L, D, slots, owner_list....  72.5 us
    pallas_call x1, Pallas kernels, middle(): pl.pallas_call(functools.partial(middle_kernel, W, L, D, FF, steps), grid...  62.8 us

profile of v5, /device:TPU:0, one launch (start us, length us, event | category | flops | bytes accessed | tf_op | source)
XLA Modules:
  0.0 318.4 jit_solution(5247625295148804991)
XLA Ops:
  0.6 1.4 select_reduce_fusion.restore
  2.0 0.8 compare_select_fusion
  2.8 1.3 broadcast_in_dim.23.bias_ref
  4.1 0.9 fusion.3.basis_ref
  5.0 75.0 %head.1 = (bf16[1536,512]{1,0:T(8,128)(2,1)}, bf16[8,1536,64]{2,1,0:T(8,128)(2,1)}, bf16[1536,512]{1,0:T(8,128)(2,1)}, bf16[1024,512]{1,0:T(8,128)(2,1)}, bf16[2...) custom-call(s32[256]{0:T(256)} %select_reduce_fusion.restore, ...), custom_call_target="tpu_custom_call" | custom-call | tf_op jit(solution)/shard_map/head/pallas_call | solution.py:1035
  80.0 62.8 %middle.1 = (bf16[16,96,512]{2,1,0:T(8,128)(2,1)}, f32[16,96,512]{2,1,0:T(8,128)}, bf16[16,96,512]{2,1,0:T(8,128)(2,1)}, f32[512,512]{1,0:T(8,128)}, f32[2048,51...) custom-call(f32[1044]{0:T(1024)} %mix_ref.1, bf16[16,96,512]{2,1,0:T(8,128)(2,1)} %bitcast.16, ...), custom_call_target="tpu_custom_call" | custom-call | tf_op jit(solution)/shard_map/middle/pallas_call | solution.py:291
  142.8 0.0 copy-start
  142.8 0.0 copy-start.1
  142.8 0.0 copy-start.2
  142.8 72.5 %tail.1 = (f32[160,512]{1,0:T(8,128)}, f32[768,128]{1,0:T(8,128)}, f32[32,128]{1,0:T(8,128)}, f32[1536,512]{1,0:T(8,128)}) custom-call(s32[256]{0:T(256)} %owner.1, bf16[1536,512]{1,0:T(8,128)(2,1)} %bitcast.18, bf16[8,1536,64]{2,1,0:T(8,128)(2,1)} %get-tuple-element.44.z_h, bf16[1536,512]{1,0:T(8,128)(2,1)} %get-tuple-element.37.acts_h, ...), custom_call_target="tpu_custom_call" | custom-call | tf_op jit(solution)/shard_map/tail/pallas_call | solution.py:769
  215.3 0.8 slice_reduce_fusion
  216.2 1.3 slice_bitcast_fusion.1
  217.4 0.7 slice_bitcast_fusion
  218.1 0.0 copy-done
  218.1 0.0 copy-done.1
  218.1 0.0 copy-done.2
  218.1 0.6 multiply_subtract_fusion
  218.8 99.5 %update.1 = (f32[160,512]{1,0:T(8,128)}, f32[160,512]{1,0:T(8,128)}, f32[160,512]{1,0:T(8,128)}, f32[768,128]{1,0:T(8,128)}, f32[768,128]{1,0:T(8,128)}, /*index=5*/f32[768,128]{1,0:T(8,128)}, f32[1536,512]{1,0:T(8,128)}) custom-call(f32[160,512]{1,0:T(8,128)} %refs_0_.1, f32[160,512]{1,0:T(8,128)} %get-tuple-element.51.refs_1_, f32[160,512]{1,0:T(8,128)} %refs_2_.1, ...), custom_call_target="tpu_custom_call" | custom-call | tf_op jit(solution)/shard_map/update/pallas_call | solution.py:1091
Async XLA Ops:
  142.8 75.4 %copy-start = (f32[1044]{0:T(1024)S(1)}, f32[1044]{0:T(1024)}, u32[]{:S(2)}) copy-start(f32[1044]{0:T(1024)} %mix_ref.1) | copy-start | bytes 12532
  142.8 75.3 %copy-start.1 = (f32[1044]{0:T(1024)S(1)}, f32[1044]{0:T(1024)}, u32[]{:S(2)}) copy-start(f32[1044]{0:T(1024)} %param.33) | copy-start | bytes 12532
  142.8 75.3 %copy-start.2 = (f32[1044]{0:T(1024)S(1)}, f32[1044]{0:T(1024)}, u32[]{:S(2)}) copy-start(f32[1044]{0:T(1024)} %param.32) | copy-start | bytes 12532

commit v6 on v5

--- a/solution.py
+++ b/solution.py
@@ -100,6 +100,7 @@
                 accs[base_at + 5 + k] += fold(t)
         return total
 
+    bias = row_of(bias_ref, D, D)
     sig = sig_ref[...].reshape(T, D)
     base[...] = dot(sig, wq_ref[D:2 * D, :])
 
@@ -114,7 +115,7 @@
 
     def summed(w, i, cols):
         rows = slice(w * L + i * CH, w * L + (i + 1) * CH)
-        v = base[rows, cols] + acts_ref[w, i * CH:(i + 1) * CH, cols].astype(F32) + bias_ref[:, D + cols.start:D + cols.stop]
+        v = base[rows, cols] + acts_ref[w, i * CH:(i + 1) * CH, cols].astype(F32) + bias[:, cols]
         v1[rows, cols] = v
         return v
 
@@ -303,7 +304,7 @@
         in_specs=[
             pl.BlockSpec(memory_space=pltpu.SMEM),
             piece(W, L, D), piece(W, L, D), piece(W, L, D),
-            whole(2 * D, D), whole(FF, D), whole(FF, D), whole(1, bias.shape[1]), whole(L, L), whole(5 * L, 256), whole(L, 512),
+            whole(2 * D, D), whole(FF, D), whole(FF, D), whole(bias.shape[0]), whole(L, L), whole(5 * L, 256), whole(L, 512),
         ],
         out_specs=(
             piece(W, L, D), piece(W, L, D), piece(W, L, D), whole(D, D), anywhere, anywhere, whole(168, D),
@@ -413,6 +414,26 @@
 JOIN = 12
 
 
+def waves(length):
+    angle = (np.arange(length)[:, None] * np.arange(length)[None, :] % length) * (2.0 * np.pi / length)
+    table = np.zeros((2 * length, 128), np.float32)
+    table[:length, :length] = np.cos(angle)
+    table[length:, :length] = -np.sin(angle)
+    return table
+
+
+def pick_waves(mode_list, waves_ref, rows):
+    slots = mode_list.shape[0]
+    for j in range(slots):
+        for part in range(2):
+            at = mode_list[j] + part * (waves_ref.shape[0] // 2)
+            rows[part * slots + j:part * slots + j + 1, :] = waves_ref[pl.ds(at, 1), :]
+
+
+def row_of(ref, start, size):
+    return jnp.concatenate([ref[pl.ds(start + i * 128, 128)].reshape(1, 128) for i in range(size // 128)], 1)
+
+
 def roles():
     ndp, nmode = lax.axis_size("dp"), lax.axis_size("mode")
     half = nmode // 2
@@ -551,10 +572,10 @@
     lax.fori_loop(start, stop, body, 0)
 
 
-def tail_kernel(n, L, D, slots, blocks, owner, gmix_h, z_h, acts_h, gsum_h, weights_h, gout_h, gup_h, gdn_h,
-                obs_ref, wqo_h, basis_ref, eye_ref, sums_ref,
+def tail_kernel(n, L, D, slots, blocks, owner, mode_list, gmix_h, z_h, acts_h, gsum_h, weights_h, gout_h, gup_h, gdn_h,
+                obs_ref, wqo_h, waves_ref, eye_ref, sums_ref,
                 dense_out, mixer_out, small_out, gin_h,
-                gmix, z, acts, gsum, mix, src, tiles, glow, gbias, tmp, con, basist, wq_ref,
+                gmix, z, acts, gsum, mix, src, tiles, glow, gbias, tmp, con, basis_rows, basist, wq_ref,
                 fc0, fc1, fv0, fv1, fu0, fu1, fa0, fa1, small_one, small_two,
                 loads, send, recv_c, recv_v, recv_u, recv_a, small_send, small_recv):
     sizes, here = roles()
@@ -593,7 +614,8 @@
         sizes, here, con_at, fc0, fv0, fu0, fa0, dense_out,
         send.at[0], recv_c.at[0], recv_v.at[0], recv_u.at[0], recv_a.at[0])
 
-    basist[...] = basis_ref[...].astype(F32).T.astype(BF)
+    pick_waves(mode_list, waves_ref, basis_rows)
+    basist[...] = basis_rows[:, 0:L].T.astype(BF)
     firsts[0].wait()
 
     def spectra(w):
@@ -621,9 +643,18 @@
     if pieces == 1:
         def mix_shard(at):
             p, m = place_of(sizes, at)
-
-            for at in range(0, per, JOIN):
-                mix_slots([(m, jl, p) for jl in range(at, min(at + JOIN, per))])
+            y_at = tiles.at[p, pl.ds(pl.multiple_of(m * per * n, per * n), per * n)]
+            z_at = z.at[p, pl.ds(pl.multiple_of(m * per * 2 * n, per * 2 * n), per * 2 * n)]
+            w_at = mix.at[p, m]
+            for start in range(0, per, JOIN):
+                group = range(start, min(start + JOIN, per))
+                ys = [y_at[j * n:(j + 1) * n, :] for j in group]
+                boths = [jnp.concatenate([y, swap_halves(y) * sign_lanes(n, 1.0, -1.0)], 0).astype(BF) for y in ys]
+                xs = [dot(both, w_at[j * 64:(j + 1) * 64, :], NT) for both, j in zip(boths, group)]
+                gs = [dot(z_at[j * 2 * n:(j + 1) * 2 * n, :], both, TN).astype(BF) for both, j in zip(boths, group)]
+                for x, g, j in zip(xs, gs, group):
+                    y_at[j * n:(j + 1) * n, :] = jnp.concatenate([x[:n], x[n:]], 1)
+                    w_at[j * 64:(j + 1) * 64, :] = g
 
         def feed(t, d):
             def pair(e):
@@ -745,16 +776,20 @@
     last_d()
     for c in twos:
         c.wait()
-    small_out[...] = functools.reduce(lambda p, q: p + q, [small_two[i] for i in range(ndp)])
+    total = functools.reduce(lambda p, q: p + q, [small_two[i] for i in range(ndp)])
+    small_out[0:8, :] = total[0:8]
+    small_out[8:16, :] = jnp.zeros((8, 128), F32)
+    small_out[8:16, 0:24] = lax.dot_general(
+        jnp.ones((8, 128), F32), total[8:32], NT, precision=lax.Precision.HIGHEST, preferred_element_type=F32)
     drain_m()
     drain_d()
     result.wait()
 
 
-def tail(gmix, z, acts, gsum, observed, wqo, basis, weights, gout, gup, gdn, sums, owner_list, shard_rows):
+def tail(gmix, z, acts, gsum, observed, wqo, mode_index, weights, gout, gup, gdn, sums, owner_list, shard_rows):
     n, L = observed.shape
     D = acts.shape[1]
-    slots = basis.shape[0] // 2
+    slots = mode_index.shape[0]
     ndp, nmode, mixer_rows = weights.shape[:3]
     nd = ndp * nmode
     total = nd * shard_rows
@@ -769,10 +804,10 @@
     return pl.pallas_call(
         functools.partial(tail_kernel, n, L, D, slots, owner_list.shape[0]),
         out_shape=(
-            jax.ShapeDtypeStruct(shapes[0], F32), jax.ShapeDtypeStruct(shapes[1], F32), jax.ShapeDtypeStruct((32, 128), F32),
+            jax.ShapeDtypeStruct(shapes[0], F32), jax.ShapeDtypeStruct(shapes[1], F32), jax.ShapeDtypeStruct((16, 128), F32),
             jax.ShapeDtypeStruct((n * L, D), F32),
         ),
-        in_specs=[pl.BlockSpec(memory_space=pltpu.SMEM)] + [anywhere] * 8 + [
+        in_specs=[pl.BlockSpec(memory_space=pltpu.SMEM)] * 2 + [anywhere] * 8 + [
             vmem, anywhere, vmem, vmem, vmem],
         out_specs=(vmem, vmem, vmem, anywhere),
         scratch_shapes=[
@@ -787,6 +822,7 @@
             pltpu.VMEM((8, D), F32),
             pltpu.VMEM((D // 128, 80, 128), F32),
             pltpu.VMEM((nd, shard_rows, D), BF),
+            pltpu.VMEM((2 * slots, 128), F32),
             pltpu.VMEM((L, 2 * slots), BF),
             pltpu.VMEM((D, D), BF),
         ] + [pltpu.VMEM((count,) + s, BF) for count in counts for s in shapes] + [
@@ -796,7 +832,7 @@
         ],
         compiler_params=pltpu.CompilerParams(collective_id=1, has_side_effects=True, vmem_limit_bytes=62 * 1024 * 1024),
         name="tail",
-    )(owner_list, gmix, z, acts, gsum, weights, gout, gup, gdn, observed, wqo, basis, np.eye(L, dtype=np.float32), sums)
+    )(owner_list, mode_index, gmix, z, acts, gsum, weights, gout, gup, gdn, observed, wqo, waves(L), np.eye(L, dtype=np.float32), sums)
 
 
 def gatherer(sizes, here, slot_of, whole_of, send, send_a, recv):
@@ -886,9 +922,9 @@
     return start, line, second, third, partner, drain
 
 
-def head_kernel(n, L, D, slots, blocks, restore, in_h, dense_ref, mixer_ref, obs_ref, bias_ref, basis_ref, inv_ref, eye_ref,
+def head_kernel(n, L, D, slots, blocks, restore, mode_list, in_h, dense_ref, mixer_ref, obs_ref, bias_ref, waves_ref, inv_ref, eye_ref,
                 acts_h, z_h, sig_h, wqo_h, wup_h, wdn_h, weights_h,
-                inputs, acts, query, tiles, z, sig, buf, src, table, mix, tmp,
+                inputs, acts, query, tiles, z, sig, buf, src, table, mix, tmp, basis_rows, basis_ref,
                 loads, send, send_a, recv):
     sizes, here = roles()
     ndp, nmode = lax.axis_size("dp"), lax.axis_size("mode")
@@ -908,6 +944,9 @@
         return pltpu.make_async_copy(a, b, loads.at[i])
     load_in = load(0, in_h, inputs)
     load_in.start()
+    pick_waves(mode_list, waves_ref, basis_rows)
+    basis_ref[...] = basis_rows[:, 0:L].astype(BF)
+    bias = row_of(bias_ref, 0, D)
     buf[dp * nmode + mode] = dense_ref[...].astype(BF)
     mix[dp, mode] = mixer_ref[...].astype(BF)
     greet()
@@ -943,21 +982,31 @@
     each(0, n, mask)
     outs = [load(1, acts, acts_h)]
     outs[0].start()
-    for k in range(na + 2):
+    rest = []
+    for k in range(na + 1):
         if k < na - 1:
             line_d(k + 1, widen)
         if k < na:
             second_d(k, widen)
-        if 1 <= k <= na:
+        if k >= 1:
             third_d(k - 1, widen)
         if k == 0:
             start_m()
-        if 1 <= k < na:
-            line_m(k)
-        if 1 <= k <= na:
-            second_m(k - 1)
-        if 2 <= k <= na:
-            third_m(k - 2)
+        if 1 <= k + 1 - 2 < na:
+            line_m(k + 1 - 2)
+        if 0 <= k - 2 < na:
+            second_m(k - 2)
+        if 0 <= k - 2 - 1 < 0:
+            third_m(k - 2 - 1)
+    done_line, done_second, done_third = min(na - 1, na + 1 - 2), min(na - 1, na - 2), min(0 - 1, na - 2 - 1)
+    for k in range(na):
+        if k > done_line:
+            rest.append(lambda k=k: line_m(k))
+        if k > done_second:
+            rest.append(lambda k=k: second_m(k))
+    for k in range(na):
+        if k > done_third:
+            rest.append(lambda k=k: third_m(k))
     each(0, na, lambda t: partner_d(t, widen))
 
     def pick(p):
@@ -972,41 +1021,65 @@
 
     def project(i):
         part = pl.ds(pl.multiple_of(i * T, T), T)
-        query[part, :] = (dot(acts[part, :], table[0:D, :]) + bias_ref[:, 0:D]).astype(BF)
+        query[part, :] = (dot(acts[part, :], table[0:D, :]) + bias).astype(BF)
 
     def spectra(w):
         part = pl.ds(pl.multiple_of(w * L, 32), L)
         spread_rows(tiles, w, slots, n, dot(basis_ref[...], query[part, :]))
 
-    work = [lambda i=i: project(i) for i in range(n * L // T)]
-    work += [lambda i=i: each(i * n // 4, (i + 1) * n // 4, spectra) for i in range(4)]
-    cuts = [early + (units - early) * i // 4 for i in range(5)]
-    work += [lambda i=i: each(cuts[i], cuts[i + 1], pick) for i in range(4)]
-    for i, w in enumerate(work):
-        w()
-        if i == 1:
-            third_m(na - 1)
-    at = 0
-    for i, ref in enumerate((wqo_h, wup_h, wdn_h)):
-        outs.append(load(2 + i, table.at[pl.ds(at, ref.shape[0])], ref))
-        outs[-1].start()
-        at += ref.shape[0]
-    each(0, na, partner_m)
+    parts = n * L // T
+    for i in range(parts):
+        project(i)
+    for i in range(4):
+        if rest:
+            rest.pop(0)()
+        each(i * n // 4, (i + 1) * n // 4, spectra)
+    while rest:
+        rest.pop(0)()
+
+    def table_out():
+        at = 0
+        for i, ref in enumerate((wqo_h, wup_h, wdn_h)):
+            outs.append(load(2 + i, table.at[pl.ds(at, ref.shape[0])], ref))
+            outs[-1].start()
+            at += ref.shape[0]
+
+    def mix_slots(places):
+        taken = []
+        for j, jl, m, h in places:
+            x = tiles[h, pl.ds(pl.multiple_of(j * n, n), n), :]
+            both = jnp.concatenate([x, swap_halves(x)], 0)[:, :64].astype(BF)
+            taken.append((both, head_weights(mix, h, pieces, m, pl.ds(pl.multiple_of(jl * depth, depth), depth))))
+        products = [dot(both, w) for both, w in taken]
+        for (j, jl, m, h), (both, w), y in zip(places, taken, products):
+            z[h, pl.ds(pl.multiple_of(j * 2 * n, 2 * n), 2 * n), :] = both
+            tiles[h, pl.ds(pl.multiple_of(j * n, n), n), :] = y[:n] + swap_halves(y[n:]) * sign_lanes(n, -1.0, 1.0)
+
+    if pieces == 1:
+        def mix_core(core):
+            def some(i):
+                def slot(jl, _):
+                    m = i * 2 + core
+                    mix_slots([(m * per + jl, jl, m, p) for p in range(heads)])
+                    return 0
+                lax.fori_loop(0, per, slot, 0, unroll=4)
+            each(0, nmode // 2, some)
+        mix_core(here["c"])
+        each(early, units, pick)
+        table_out()
+        each(0, na, partner_m)
+        mix_core(1 - here["c"])
+    else:
+        each(early, units, pick)
+        table_out()
+        each(0, na, partner_m)
+
+        def slot(j, _):
+            mix_slots([(j, lax.rem(j, per), j // per, h) for h in range(heads)])
+            return 0
+        lax.fori_loop(0, slots, slot, 0, unroll=4)
     outs.append(load(5, mix, weights_h))
     outs[-1].start()
-
-    def slot(j, _):
-        m, jl = j // per, lax.rem(j, per)
-        at = pl.ds(pl.multiple_of(j * n, n), n)
-        part = pl.ds(pl.multiple_of(jl * depth, depth), depth)
-        for h in range(heads):
-            x = tiles[h, at, :]
-            both = jnp.concatenate([x, swap_halves(x)], 0)[:, :64].astype(BF)
-            z[h, pl.ds(pl.multiple_of(j * 2 * n, 2 * n), 2 * n), :] = both
-            y = dot(both, head_weights(mix, h, pieces, m, part))
-            tiles[h, at, :] = y[:n] + swap_halves(y[n:]) * sign_lanes(n, -1.0, 1.0)
-        return 0
-    lax.fori_loop(0, slots, slot, 0, unroll=4)
     outs.append(load(6, z, z_h))
     outs[-1].start()
 
@@ -1022,9 +1095,9 @@
         o.wait()
 
 
-def head(inputs, observed, dense, mixer, restore, bias, basis, inv, ff):
+def head(inputs, observed, dense, mixer, restore, bias, mode_index, inv, ff):
     n, L, D = inputs.shape
-    slots = basis.shape[0] // 2
+    slots = mode_index.shape[0]
     ndp, nmode = lax.axis_size("dp"), lax.axis_size("mode")
     nd = ndp * nmode
     rows, mixer_rows = dense.shape[0], mixer.shape[0]
@@ -1043,7 +1116,7 @@
             jax.ShapeDtypeStruct((ff, D), BF),
             jax.ShapeDtypeStruct((ndp, nmode, mixer_rows, 128), BF),
         ),
-        in_specs=[pl.BlockSpec(memory_space=pltpu.SMEM), anywhere] + [vmem] * 7,
+        in_specs=[pl.BlockSpec(memory_space=pltpu.SMEM)] * 2 + [anywhere] + [vmem] * 7,
         out_specs=(anywhere,) * 7,
         scratch_shapes=[
             pltpu.VMEM((tokens, D), BF),
@@ -1057,11 +1130,13 @@
             pltpu.VMEM((nd * rows, D), BF),
             pltpu.VMEM((ndp, nmode, mixer_rows, 128), BF),
             pltpu.VMEM((D // 128, 4 * (nd * rows // restore.shape[0]), 128), F32),
+            pltpu.VMEM((2 * slots, 128), F32),
+            pltpu.VMEM((2 * slots, L), BF),
             sem(8), sem(2, 3), sem(2, 2, ndp // (nmode // 2)), sem(2, nd),
         ],
         compiler_params=pltpu.CompilerParams(collective_id=0, has_side_effects=True, vmem_limit_bytes=62 * 1024 * 1024),
         name="head",
-    )(restore, inputs.reshape(tokens, D), dense, mixer, observed, bias, basis, inv, np.eye(L, dtype=np.float32))
+    )(restore, mode_index, inputs.reshape(tokens, D), dense, mixer, observed, bias, waves(L), inv, np.eye(L, dtype=np.float32))
 
 
 def adam_terms(weight, gradient, moment, second, step_rate):
@@ -1073,38 +1148,52 @@
     return moment_new, second_new, weight_new
 
 
-def update_kernel(*refs):
-    dense, mixer, passed = refs[:4], refs[4:8], refs[8]
-    dense_out, mixer_out, passed_out, sem = refs[9:12], refs[12:15], refs[15], refs[16]
-    copy = pltpu.make_async_copy(passed, passed_out, sem)
-    copy.start()
+def update_kernel(chunks, *refs):
+    dense, mixer, small, passed = refs[:4], refs[4:8], refs[8:12], refs[12]
+    dense_out, mixer_out, small_out, bias_out, passed_out = refs[13:16], refs[16:19], refs[19:22], refs[22], refs[23]
+    held, got, put = refs[24:]
+    step = held.shape[0] // chunks
+    parts = [pl.ds(i * step, step) for i in range(chunks)]
+    gets = [pltpu.make_async_copy(passed.at[p], held.at[p], got.at[i]) for i, p in enumerate(parts)]
+    puts = [pltpu.make_async_copy(held.at[p], passed_out.at[p], put.at[i]) for i, p in enumerate(parts)]
+    for c in gets:
+        c.start()
     for ins, outs, rate in ((dense, dense_out, RATE_DENSE), (mixer, mixer_out, RATE_MIXER)):
         for ref, value in zip(outs, adam_terms(*(x[...] for x in ins), rate)):
             ref[...] = value
-    copy.wait()
-
-
-def update(dense, mixer, passed):
+    for g, p in zip(gets, puts):
+        g.wait()
+        p.start()
+    size = small[0].shape[0]
+    for r in range(-(-size // 128)):
+        n = min(128, size - r * 128)
+        at = pl.ds(r * 128, n)
+        grad = small[1][r:r + 1, :][:, :n]
+        row = lambda x: x[at].reshape(1, n)
+        terms = adam_terms(row(small[0]), grad, row(small[2]), row(small[3]), RATE_SMALL)
+        for ref, value in zip(small_out, terms):
+            ref[at] = value.reshape(n)
+    for r in range(bias_out.shape[0] // 128):
+        bias_out[pl.ds(r * 128, 128)] = small[1][4 + r:5 + r, :].reshape(128)
+    for p in puts:
+        p.wait()
+
+
+def update(dense, mixer, small, passed):
     vmem = pl.BlockSpec(memory_space=pltpu.VMEM)
     anywhere = pl.BlockSpec(memory_space=pl.ANY)
     like = lambda x: jax.ShapeDtypeStruct(x.shape, x.dtype)
+    chunks = 4
     return pl.pallas_call(
-        update_kernel,
-        out_shape=(like(dense[0]),) * 3 + (like(mixer[0]),) * 3 + (like(passed),),
-        in_specs=[vmem] * 8 + [anywhere],
-        out_specs=(vmem,) * 6 + (anywhere,),
-        scratch_shapes=[pltpu.SemaphoreType.DMA],
+        functools.partial(update_kernel, chunks),
+        out_shape=(like(dense[0]),) * 3 + (like(mixer[0]),) * 3 + (like(small[0]),) * 3 + (
+            jax.ShapeDtypeStruct((dense[0].shape[1],), F32), like(passed)),
+        in_specs=[vmem] * 12 + [anywhere],
+        out_specs=(vmem,) * 10 + (anywhere,),
+        scratch_shapes=[pltpu.VMEM(passed.shape, F32), pltpu.SemaphoreType.DMA((chunks,)), pltpu.SemaphoreType.DMA((chunks,))],
         compiler_params=pltpu.CompilerParams(vmem_limit_bytes=62 * 1024 * 1024),
         name="update",
-    )(*dense, *mixer, passed)
-
-
-def forward_table(mode_index, length):
-    slots = mode_index.shape[0]
-    row = jnp.arange(2 * slots, dtype=jnp.int32)
-    mode = jnp.concatenate([mode_index, mode_index])
-    turn = (mode[:, None] * jnp.arange(length, dtype=jnp.int32)[None, :] + (row >= slots)[:, None] * (length // 4)) % length
-    return jnp.cos(turn.astype(F32) * (2.0 * math.pi / length)).astype(BF)
+    )(*dense, *mixer, *small, passed)
 
 
 def inverse_table(slots, length):
@@ -1134,35 +1223,30 @@
     length, width = inputs.shape[1:]
     slots = mode_index.shape[0]
     hidden = (dense_master.shape[0] * ndp * nmode - 2 * width) // 2
-    basis = forward_table(mode_index, length)
     inv = inverse_table(slots, length)
-    small_row = small_master[None]
     places = jnp.arange(owner_list.shape[0], dtype=jnp.int32)
     restore = jnp.sum(jnp.where(owner_list[None, :] == places[:, None], places[None, :], 0), axis=1)
     acts, spectra, sig, wqo, wup, wdn, weights = head(
-        inputs, observed, dense_master, mixer_master.reshape(-1, mixer_master.shape[2]), restore, small_row,
-        basis, inv, hidden,
+        inputs, observed, dense_master, mixer_master.reshape(-1, mixer_master.shape[2]), restore, small_master,
+        mode_index, inv, hidden,
     )
     output, grad_summed, grad_mixed, g_out, g_up, g_down, sums = middle(
         small_master, acts.reshape(inputs.shape), sig.reshape(inputs.shape), out_grad, wqo, wup, wdn,
-        small_row, np.ascontiguousarray(inv.T),
+        small_master, np.ascontiguousarray(inv.T),
     )
     dense_mine, mixer_mine, small_all, input_grad = tail(
-        grad_mixed.reshape(-1, width), spectra, acts, grad_summed.reshape(-1, width), observed, wqo, basis, weights,
+        grad_mixed.reshape(-1, width), spectra, acts, grad_summed.reshape(-1, width), observed, wqo, mode_index, weights,
         g_out, g_up, g_down, sums, owner_list, dense_master.shape[0],
     )
-    small_total = jnp.concatenate([small_all[:8].reshape(-1), jnp.sum(small_all[8:28], axis=1)])
     flat = lambda x: x.reshape(-1, x.shape[-1])
-    dense_first_new, dense_second_new, dense_new, mixer_first_new, mixer_second_new, mixer_new, input_grad = update(
+    dense_first_new, dense_second_new, dense_new, mixer_first_new, mixer_second_new, mixer_new, *small, input_grad = update(
         (dense_master, dense_mine, dense_first, dense_second),
         (flat(mixer_master), mixer_mine, flat(mixer_first), flat(mixer_second)),
+        (small_master, small_all, small_first, small_second),
         input_grad,
     )
     mixer_first_new, mixer_second_new, mixer_new = (
         x.reshape(mixer_master.shape) for x in (mixer_first_new, mixer_second_new, mixer_new)
-    )
-    small_first_new, small_second_new, small_new = adam_terms(
-        small_master, small_total, small_first, small_second, RATE_SMALL
     )
     return (
         output,
@@ -1173,10 +1257,7 @@
         mixer_first_new,
         mixer_second_new,
         mixer_new,
-        small_first_new,
-        small_second_new,
-        small_new,
-        small_total[width : 2 * width],
+        *small,
     )
 
 

time: 319 us -> 213 us (0.67)
  Pallas kernels: 310 us -> 210 us
  local copies, waits for them, and re-layouts: 3.26 us -> 0 us
    pallas_call x1, Pallas kernels: 99.5 us -> 5.99 us  [update(): pl.pallas_call(functools.partial(update_kernel, chunks), out_shape=(like(...]
    pallas_call x1, Pallas kernels: 75 us -> 70.6 us  [head(): pl.pallas_call(functools.partial(head_kernel, n, L, D, slots, restore.sha...]
where the time goes in v6:
time: 213 us; the launch traced here: 212 us
  Pallas kernels  210 us (99%)
    pallas_call x1, Pallas kernels, tail(): pl.pallas_call(functools.partial(tail_kernel, n, L, D, slots, owner_list....  70.8 us
    pallas_call x1, Pallas kernels, head(): pl.pallas_call(functools.partial(head_kernel, n, L, D, slots, restore.sha...  70.6 us
    pallas_call x1, Pallas kernels, middle(): pl.pallas_call(functools.partial(middle_kernel, W, L, D, FF, steps), grid...  62.8 us
    pallas_call x1, Pallas kernels, update(): pl.pallas_call(functools.partial(update_kernel, chunks), out_shape=(like(...  5.99 us

profile of v6, /device:TPU:0, one launch (start us, length us, event | category | flops | bytes accessed | tf_op | source)
XLA Modules:
  0.0 212.4 jit_solution(7368963417901518428)
XLA Ops:
  0.6 1.4 select_reduce_fusion.restore
  2.0 70.6 %head.1 = (bf16[1536,512]{1,0:T(8,128)(2,1)}, bf16[8,1536,64]{2,1,0:T(8,128)(2,1)}, bf16[1536,512]{1,0:T(8,128)(2,1)}, bf16[1024,512]{1,0:T(8,128)(2,1)}, bf16[2...) custom-call(s32[256]{0:T(256)} %select_reduce_fusion.restore, s32[48]{0:T(128)} %mode_list.3, ...), custom_call_target="tpu_custom_call" | custom-call | tf_op jit(solution)/shard_map/head/pallas_call | solution.py:1108
  72.6 62.8 %middle.1 = (bf16[16,96,512]{2,1,0:T(8,128)(2,1)}, f32[16,96,512]{2,1,0:T(8,128)}, bf16[16,96,512]{2,1,0:T(8,128)(2,1)}, f32[512,512]{1,0:T(8,128)}, f32[2048,51...) custom-call(f32[1044]{0:T(1024)} %refs_8_.1, bf16[16,96,512]{2,1,0:T(8,128)(2,1)} %bitcast.12, ...), custom_call_target="tpu_custom_call" | custom-call | tf_op jit(solution)/shard_map/middle/pallas_call | solution.py:292
  135.4 70.8 %tail.1 = (f32[160,512]{1,0:T(8,128)}, f32[768,128]{1,0:T(8,128)}, f32[16,128]{1,0:T(8,128)}, f32[1536,512]{1,0:T(8,128)}) custom-call(s32[256]{0:T(256)} %owner.1, s32[48]{0:T(128)} %mode_list.3, bf16[1536,512]{1,0:T(8,128)(2,1)} %bitcast.14, bf16[8,1536,64]{2,1,0:T(8,128)(2,1)} %get-tuple-element.48.z_h, bf16[1536,512]{1,0:T(8,128)(2,1)} %get-tuple-element.41.acts_h, ...), custom_call_target="tpu_custom_call" | custom-call | tf_op jit(solution)/shard_map/tail/pallas_call | solution.py:804
  206.2 6.0 %update.1 = (f32[160,512]{1,0:T(8,128)}, f32[160,512]{1,0:T(8,128)}, f32[160,512]{1,0:T(8,128)}, f32[768,128]{1,0:T(8,128)}, f32[768,128]{1,0:T(8,128)}, /*index...) custom-call(f32[160,512]{1,0:T(8,128)} %refs_0_.1, ...), custom_call_target="tpu_custom_call" | custom-call | tf_op jit(solution)/shard_map/update/pallas_call | solution.py:1187

commit v7 on v6

--- a/solution.py
+++ b/solution.py
@@ -52,19 +52,23 @@
 
 
 def middle_kernel(W, L, D, FF, steps,
-                  mix_ref, acts_ref, sig_ref, og_ref, wq_ref, wup_ref, wdn_ref, bias_ref, invt_ref, cnt_ref, cntt_ref,
+                  mix_ref, acts_ref, sig_ref, og_ref, wq_ref, wup_h, wdn_h, bias_ref, invt_ref, cnt_ref, cntt_ref,
                   out_ref, gsum_ref, gmix_ref, gw_ref, gup_ref, gdn_ref, small_ref,
-                  vs, base, avg1, c1, v1, active, dgelu, first, flow, gb, ghid, glow, avg2, stk, accs, accb, hs, wg, wsem):
+                  vs, base, avg1, c1, v1, active, dgelu, first, flow, gb, ghid, glow, avg2, stk, accs, accb, hs, wg, wsem, wup_ref, wdn_ref, lsem):
     step = pl.program_id(0)
     T = W * L
     CH = 16
-    CC = 256
+    CC = 512
     nc = D // CC
     nr = L // CH
     FT = 512
 
+    fetch = [pltpu.make_async_copy(a, b, lsem.at[i]) for i, (a, b) in enumerate(((wup_h, wup_ref), (wdn_h, wdn_ref)))]
+
     @pl.when(step == 0)
     def _():
+        for f in fetch:
+            f.start()
         vs[...] = jnp.zeros_like(vs)
         stk[...] = jnp.zeros_like(stk)
         accs[...] = jnp.zeros_like(accs)
@@ -153,6 +157,10 @@
         return dot(flow[here_t, :], wup_ref[n * FT:(n + 1) * FT, :], NT)
 
     tiles = FF // FT
+    @pl.when(step == 0)
+    def _():
+        for f in fetch:
+            f.wait()
     hs[0] = up(0)
     for n in range(tiles + 1):
         if n + 1 < tiles:
@@ -304,7 +312,7 @@
         in_specs=[
             pl.BlockSpec(memory_space=pltpu.SMEM),
             piece(W, L, D), piece(W, L, D), piece(W, L, D),
-            whole(2 * D, D), whole(FF, D), whole(FF, D), whole(bias.shape[0]), whole(L, L), whole(5 * L, 256), whole(L, 512),
+            whole(2 * D, D), anywhere, anywhere, whole(bias.shape[0]), whole(L, L), whole(5 * L, 256), whole(L, 512),
         ],
         out_specs=(
             piece(W, L, D), piece(W, L, D), piece(W, L, D), whole(D, D), anywhere, anywhere, whole(168, D),
@@ -329,6 +337,9 @@
             pltpu.VMEM((2, T, 512), F32),
             pltpu.VMEM((4, 512, D), F32),
             pltpu.SemaphoreType.DMA((4,)),
+            pltpu.VMEM((FF, D), BF),
+            pltpu.VMEM((FF, D), BF),
+            pltpu.SemaphoreType.DMA((2,)),
         ],
         compiler_params=pltpu.CompilerParams(vmem_limit_bytes=60 * 1024 * 1024),
         name="middle",
@@ -990,7 +1001,7 @@
             second_d(k, widen)
         if k >= 1:
             third_d(k - 1, widen)
-        if k == 0:
+        if k == 1:
             start_m()
         if 1 <= k + 1 - 2 < na:
             line_m(k + 1 - 2)
@@ -1158,12 +1169,13 @@
     puts = [pltpu.make_async_copy(held.at[p], passed_out.at[p], put.at[i]) for i, p in enumerate(parts)]
     for c in gets:
         c.start()
-    for ins, outs, rate in ((dense, dense_out, RATE_DENSE), (mixer, mixer_out, RATE_MIXER)):
+    for i, (ins, outs, rate) in enumerate(((dense, dense_out, RATE_DENSE), (mixer, mixer_out, RATE_MIXER))):
         for ref, value in zip(outs, adam_terms(*(x[...] for x in ins), rate)):
             ref[...] = value
-    for g, p in zip(gets, puts):
-        g.wait()
-        p.start()
+        if i == 0:
+            for g, p in zip(gets, puts):
+                g.wait()
+                p.start()
     size = small[0].shape[0]
     for r in range(-(-size // 128)):
         n = min(128, size - r * 128)

time: 213 us -> 212 us (level)
  no operation moved by 1% of the time
where the time goes in v7:
time: 212 us
  Pallas kernels  210 us (99%)
    pallas_call x1, Pallas kernels, tail(): pl.pallas_call(functools.partial(tail_kernel, n, L, D, slots, owner_list....  71.7 us
    pallas_call x1, Pallas kernels, head(): pl.pallas_call(functools.partial(head_kernel, n, L, D, slots, restore.sha...  69.9 us
    pallas_call x1, Pallas kernels, middle(): pl.pallas_call(functools.partial(middle_kernel, W, L, D, FF, steps), grid...  62.3 us
    pallas_call x1, Pallas kernels, update(): pl.pallas_call(functools.partial(update_kernel, chunks), out_shape=(like(...  5.99 us

profile of v7, /device:TPU:0, one launch (start us, length us, event | category | flops | bytes accessed | tf_op | source)
XLA Modules:
  0.0 212.1 jit_solution(8635645438429027591)
XLA Ops:
  0.6 1.4 select_reduce_fusion.restore
  2.0 69.9 %head.1 = (bf16[1536,512]{1,0:T(8,128)(2,1)}, bf16[8,1536,64]{2,1,0:T(8,128)(2,1)}, bf16[1536,512]{1,0:T(8,128)(2,1)}, bf16[1024,512]{1,0:T(8,128)(2,1)}, bf16[2...) custom-call(s32[256]{0:T(256)} %select_reduce_fusion.restore, s32[48]{0:T(128)} %mode_list.3, ...), custom_call_target="tpu_custom_call" | custom-call | tf_op jit(solution)/shard_map/head/pallas_call | solution.py:1119
  71.9 62.3 %middle.1 = (bf16[16,96,512]{2,1,0:T(8,128)(2,1)}, f32[16,96,512]{2,1,0:T(8,128)}, bf16[16,96,512]{2,1,0:T(8,128)(2,1)}, f32[512,512]{1,0:T(8,128)}, f32[2048,51...) custom-call(f32[1044]{0:T(1024)} %refs_8_.1, bf16[16,96,512]{2,1,0:T(8,128)(2,1)} %bitcast.12, ...), custom_call_target="tpu_custom_call" | custom-call | tf_op jit(solution)/shard_map/middle/pallas_call | solution.py:300
  134.2 71.7 %tail.1 = (f32[160,512]{1,0:T(8,128)}, f32[768,128]{1,0:T(8,128)}, f32[16,128]{1,0:T(8,128)}, f32[1536,512]{1,0:T(8,128)}) custom-call(s32[256]{0:T(256)} %owner.1, s32[48]{0:T(128)} %mode_list.3, bf16[1536,512]{1,0:T(8,128)(2,1)} %bitcast.14, bf16[8,1536,64]{2,1,0:T(8,128)(2,1)} %get-tuple-element.48.z_h, bf16[1536,512]{1,0:T(8,128)(2,1)} %get-tuple-element.41.acts_h, ...), custom_call_target="tpu_custom_call" | custom-call | tf_op jit(solution)/shard_map/tail/pallas_call | solution.py:815
  205.9 6.0 %update.1 = (f32[160,512]{1,0:T(8,128)}, f32[160,512]{1,0:T(8,128)}, f32[160,512]{1,0:T(8,128)}, f32[768,128]{1,0:T(8,128)}, f32[768,128]{1,0:T(8,128)}, /*index...) custom-call(f32[160,512]{1,0:T(8,128)} %refs_0_.1, ...), custom_call_target="tpu_custom_call" | custom-call | tf_op jit(solution)/shard_map/update/pallas_call | solution.py:1199

commit v8 on v7

--- a/solution.py
+++ b/solution.py
@@ -674,9 +674,10 @@
                 send_m(other).start()
                 mix_shard(move(sizes, move(sizes, move(sizes, here, "a", t + 1), "u", e), "v", d))
             each(0, sizes["u"], pair)
-        for d in range(1, sizes["v"]):
-            each(0, na, lambda t: feed(t, d))
-        each(0, na, first_m)
+        def far(t):
+            for d in range(1, sizes["v"]):
+                feed(t, d)
+        staggered(na, far, first_m)
         each(0, na, lambda t: feed(t, 0))
     else:
         def mix_mode(m):
@@ -709,7 +710,9 @@
         g = dot(basist[...], gather_rows(tiles, w, slots, n))
         glow[part, :] = g.astype(BF)
         gbias[...] += functools.reduce(lambda p, q: p + q, [g[i * 8:(i + 1) * 8] for i in range(L // 8)])
-    each(0, n, query)
+    each(0, n // 2, query)
+    each(0, 1, second_m)
+    each(n // 2, n, query)
 
     for k, sums in ((0, gbias[...]), (4, sums_ref[0:8, :])):
         total = jnp.sum(sums, axis=0, keepdims=True)
@@ -733,7 +736,7 @@
     g = dot(acts[...], glow[...], TN)
     for c in range(D // 128):
         src[c, 0:D, :] = g[:, c * 128:(c + 1) * 128]
-    each(0, na // 2, second_m)
+    each(1, na // 2, second_m)
     for c in grads:
         c.wait()
 

time: 212 us -> 210 us (level)
  no operation moved by 1% of the time
where the time goes in v8:
time: 210 us
  Pallas kernels  208 us (99%)
    pallas_call x1, Pallas kernels, head(): pl.pallas_call(functools.partial(head_kernel, n, L, D, slots, restore.sha...  69.9 us
    pallas_call x1, Pallas kernels, tail(): pl.pallas_call(functools.partial(tail_kernel, n, L, D, slots, owner_list....  69.7 us
    pallas_call x1, Pallas kernels, middle(): pl.pallas_call(functools.partial(middle_kernel, W, L, D, FF, steps), grid...  62.3 us
    pallas_call x1, Pallas kernels, update(): pl.pallas_call(functools.partial(update_kernel, chunks), out_shape=(like(...  5.99 us

profile of v8, /device:TPU:0, one launch (start us, length us, event | category | flops | bytes accessed | tf_op | source)
XLA Modules:
  0.0 210.1 jit_solution(17056064980787522298)
XLA Ops:
  0.6 1.4 select_reduce_fusion.restore
  2.0 69.9 %head.1 = (bf16[1536,512]{1,0:T(8,128)(2,1)}, bf16[8,1536,64]{2,1,0:T(8,128)(2,1)}, bf16[1536,512]{1,0:T(8,128)(2,1)}, bf16[1024,512]{1,0:T(8,128)(2,1)}, bf16[2...) custom-call(s32[256]{0:T(256)} %select_reduce_fusion.restore, s32[48]{0:T(128)} %mode_list.3, ...), custom_call_target="tpu_custom_call" | custom-call | tf_op jit(solution)/shard_map/head/pallas_call | solution.py:1122
  71.9 62.3 %middle.1 = (bf16[16,96,512]{2,1,0:T(8,128)(2,1)}, f32[16,96,512]{2,1,0:T(8,128)}, bf16[16,96,512]{2,1,0:T(8,128)(2,1)}, f32[512,512]{1,0:T(8,128)}, f32[2048,51...) custom-call(f32[1044]{0:T(1024)} %refs_8_.1, bf16[16,96,512]{2,1,0:T(8,128)(2,1)} %bitcast.12, ...), custom_call_target="tpu_custom_call" | custom-call | tf_op jit(solution)/shard_map/middle/pallas_call | solution.py:300
  134.2 69.7 %tail.1 = (f32[160,512]{1,0:T(8,128)}, f32[768,128]{1,0:T(8,128)}, f32[16,128]{1,0:T(8,128)}, f32[1536,512]{1,0:T(8,128)}) custom-call(s32[256]{0:T(256)} %owner.1, s32[48]{0:T(128)} %mode_list.3, bf16[1536,512]{1,0:T(8,128)(2,1)} %bitcast.14, bf16[8,1536,64]{2,1,0:T(8,128)(2,1)} %get-tuple-element.48.z_h, bf16[1536,512]{1,0:T(8,128)(2,1)} %get-tuple-element.41.acts_h, ...), custom_call_target="tpu_custom_call" | custom-call | tf_op jit(solution)/shard_map/tail/pallas_call | solution.py:818
  203.9 6.0 %update.1 = (f32[160,512]{1,0:T(8,128)}, f32[160,512]{1,0:T(8,128)}, f32[160,512]{1,0:T(8,128)}, f32[768,128]{1,0:T(8,128)}, f32[768,128]{1,0:T(8,128)}, /*index...) custom-call(f32[160,512]{1,0:T(8,128)} %refs_0_.1, ...), custom_call_target="tpu_custom_call" | custom-call | tf_op jit(solution)/shard_map/update/pallas_call | solution.py:1202
